TPU v7x, 32 devices: a whole 2x2x4 slice. The times are simulated.
32 devices in a mesh: shard: 16 (over z, y, x), replica: 2 (over core).
Axes of the slice: x: 2, y: 2, z: 4, core: 2. Of those that a mesh axis runs over, the one named last changes fastest.
Arguments:
- tokens: bfloat16 [8192, 2048], P(('shard', 'replica')), may hold values from -6 to 6
- seq_lengths: int32 [32, 8], P(('shard', 'replica')), may hold values from 0 to 256, as said below
- in_gain: float32 [2048], replicated, may hold values from 0.5 to 1.5
- q_gain: float32 [128], replicated, may hold values from 0.5 to 1.5
- key_norm_gain: float32 [128], replicated, may hold values from 0.5 to 1.5
- post_gain: float32 [2048], replicated, may hold values from 0.5 to 1.5
- w_qkv: bfloat16 [2048, 4096], P('shard'), may hold values from -0.125 to 0.125
- w_out: bfloat16 [2048, 2048], P('shard'), may hold values from -0.5 to 0.5
- w_gate_up: bfloat16 [2048, 12288], P('shard'), may hold values from -0.125 to 0.125
- w_down: bfloat16 [6144, 2048], P('shard'), may hold values from -0.078125 to 0.078125
- cotangent: bfloat16 [8192, 2048], P(('shard', 'replica')), may hold values from -6 to 6
Outputs:
- result: bfloat16 [8192, 2048], P(('shard', 'replica'))
- grad_tokens: bfloat16 [8192, 2048], P(('shard', 'replica'))
- grad_in_gain: float32 [2048], replicated
- grad_q_gain: float32 [128], replicated
- grad_k_gain: float32 [128], replicated
- grad_post_gain: float32 [2048], replicated
- grad_w_qkv: float32 [2048, 4096], P('shard')
- grad_w_out: float32 [2048, 2048], P('shard')
- grad_w_gate_up: float32 [2048, 12288], P('shard')
- grad_w_down: float32 [6144, 2048], P('shard')
Inputs may be any that keep to these rules, and one draw needn't show every extreme that they name: `seq_lengths`: each row lists the lengths of the sequences laid from the start of one pack; zero entries are empty. A row sums to 128 to 256, and some pack holds a single sequence of 256 tokens.
All inputs are finite; a program needn't handle non-finite values.
Results may differ from a plain program's by a relative error of at most 0.014.
Values may be sent and summed in bfloat16 or wider, within the bound.
No kernel may reach another device: no remote copies, remote signals or barrier semaphores. Data moves between devices by JAX's collectives and lax.ppermute only.
A program may use at most 512 MiB of HBM per device.

v0:
```python
import math

import jax
import jax.numpy as jnp
from jax import lax
from jax.sharding import PartitionSpec as P

QUERY_HEADS = 16
KEY_VALUE_HEADS = 8
HEAD_SIZE = 128
FF = 6144
PACK_CAPACITY = 256
NSEQ = 8


EPS = 1e-06
ROPE_BASE = 1000000.0
MASKED = -1e30


def pack_layout(lengths):
    ends = jnp.cumsum(lengths)
    starts = ends - lengths
    slots = jnp.arange(PACK_CAPACITY, dtype=jnp.int32)
    segment = jnp.sum((slots[:, None] >= ends[None, :]).astype(jnp.int32), axis=1)
    live = slots < ends[-1]
    labels = jnp.arange(NSEQ, dtype=jnp.int32)
    begin = jnp.sum(jnp.where(segment[:, None] == labels[None, :], starts[None, :], 0), axis=1)
    position = (slots - begin).astype(jnp.float32)
    segids = jnp.where(live, segment, NSEQ + slots)
    freqs = ROPE_BASE ** (-2.0 * jnp.arange(HEAD_SIZE // 2, dtype=jnp.float32) / HEAD_SIZE)
    angle = position[:, None] * freqs[None, :]
    cosine = jnp.concatenate([jnp.cos(angle), jnp.cos(angle)], axis=1)
    sine = jnp.concatenate([jnp.sin(angle), jnp.sin(angle)], axis=1)
    return (segids, cosine, sine, live)


def normalized_rows(value, gain):
    scale_inv = lax.rsqrt(jnp.mean(value * value, axis=-1, keepdims=True) + EPS)
    normed = value * scale_inv
    return (normed * gain, normed, scale_inv)


def norm_back(grad, normed, scale_inv, gain):
    scaled = grad * gain
    grad_in = scale_inv * (scaled - normed * jnp.mean(scaled * normed, axis=-1, keepdims=True))
    grad_gain = jnp.sum((grad * normed).reshape(-1, normed.shape[-1]), axis=0)
    return (grad_in, grad_gain)


def rotate_halves(value, cosine, sine):
    half = HEAD_SIZE // 2
    rotated = jnp.concatenate([-value[..., half:], value[..., :half]], axis=-1)
    return value * cosine + rotated * sine


def turn_back(grad, cosine, sine):
    half = HEAD_SIZE // 2
    moved = grad * sine
    back = jnp.concatenate([moved[..., half:], -moved[..., :half]], axis=-1)
    return grad * cosine + back


def against(grad, matrix):
    return lax.dot_general(
        grad, matrix, (((1,), (1,)), ((), ())), preferred_element_type=jnp.float32
    )


def through(left, grad):
    return lax.dot_general(left, grad, (((0,), (0,)), ((), ())), preferred_element_type=jnp.float32)


def owned_sum(left, grad):
    return lax.psum_scatter(
        through(left, grad), ("shard", "replica"), scatter_dimension=0, tiled=True
    )


def masked_scores(query_block, key_rows, segids, start, rows):
    slots = jnp.arange(PACK_CAPACITY, dtype=jnp.int32)
    query_slots = start + jnp.arange(rows, dtype=jnp.int32)
    scores = jnp.einsum(
        "qgrd,kgd->grqk", query_block, key_rows, preferred_element_type=jnp.float32
    ) * (1.0 / math.sqrt(HEAD_SIZE))
    allowed = (segids[:, None] == segids[None, :]) & (query_slots[:, None] >= slots[None, :])
    return jnp.where(allowed[None, None], scores, MASKED)


def attend_forward(query_rows, key_rows, value_rows, segids):
    rows = min(PACK_CAPACITY, 512)
    blocks = PACK_CAPACITY // rows

    def block(start):
        scores = masked_scores(query_rows, key_rows, segids, start, rows)
        top = jnp.max(scores, axis=-1, keepdims=True)
        expd = jnp.exp(scores - top)
        total = jnp.sum(expd, axis=-1, keepdims=True)
        probs = expd / total
        attn = jnp.einsum(
            "grqk,kgd->qgrd",
            probs.astype(jnp.bfloat16),
            value_rows,
            preferred_element_type=jnp.float32,
        )
        return (attn, top[..., 0] + jnp.log(total[..., 0]))

    starts = jnp.arange(blocks, dtype=jnp.int32) * rows
    attn, logsum = lax.map(block, starts)
    return (attn.reshape(PACK_CAPACITY, QUERY_HEADS * HEAD_SIZE), logsum)


def attend_backward(query_rows, key_rows, value_rows, segids, logsum, attention_gradient):
    rows = min(PACK_CAPACITY, 512)
    blocks = PACK_CAPACITY // rows
    scale = 1.0 / math.sqrt(HEAD_SIZE)

    def block(carry, item):
        start, logsum_block = item
        scores = masked_scores(query_rows, key_rows, segids, start, rows)
        probs = jnp.exp(scores - logsum_block[..., None])
        dprobs = jnp.einsum(
            "qgrd,kgd->grqk", attention_gradient, value_rows, preferred_element_type=jnp.float32
        )
        inner = jnp.sum(probs * dprobs, axis=-1, keepdims=True)
        grad_scores = (probs * (dprobs - inner)).astype(jnp.bfloat16)
        grad_query = (
            jnp.einsum("grqk,kgd->qgrd", grad_scores, key_rows, preferred_element_type=jnp.float32)
            * scale
        )
        grad_keys = (
            carry[0]
            + jnp.einsum(
                "grqk,qgrd->kgd", grad_scores, query_rows, preferred_element_type=jnp.float32
            )
            * scale
        )
        value_gradients = carry[1] + jnp.einsum(
            "grqk,qgrd->kgd",
            probs.astype(jnp.bfloat16),
            attention_gradient,
            preferred_element_type=jnp.float32,
        )
        return ((grad_keys, value_gradients), grad_query)

    starts = jnp.arange(blocks, dtype=jnp.int32) * rows
    zero_filled = jnp.zeros((PACK_CAPACITY, KEY_VALUE_HEADS, HEAD_SIZE), jnp.float32)
    (grad_keys, value_gradients), grad_query = lax.scan(
        block, (zero_filled, zero_filled), (starts, logsum)
    )
    return (grad_query.reshape(PACK_CAPACITY, QUERY_HEADS, HEAD_SIZE), grad_keys, value_gradients)


def on_device(
    tokens,
    seq_lengths,
    in_gain,
    q_gain,
    key_norm_gain,
    post_gain,
    w_qkv,
    w_out,
    w_gate_up,
    w_down,
    cotangent,
):
    replica_groupings = QUERY_HEADS // KEY_VALUE_HEADS
    segids, cosine, sine, live = pack_layout(seq_lengths[0])
    cosine_per_head = cosine[:, None, :]
    sine_per_head = sine[:, None, :]
    inputs = tokens.astype(jnp.float32)
    first, first_normed, first_scale = normalized_rows(inputs, in_gain)
    first_low = first.astype(jnp.bfloat16)
    qkv_full, out_full, gate_up_full, down_full = (
        lax.all_gather(w_qkv, "shard", axis=0, tiled=True),
        lax.all_gather(w_out, "shard", axis=0, tiled=True),
        lax.all_gather(w_gate_up, "shard", axis=0, tiled=True),
        lax.all_gather(w_down, "shard", axis=0, tiled=True),
    )
    attention_mixed = jnp.dot(first_low, qkv_full, preferred_element_type=jnp.float32)
    query_raw = attention_mixed[:, : QUERY_HEADS * HEAD_SIZE].reshape(
        PACK_CAPACITY, QUERY_HEADS, HEAD_SIZE
    )
    unnormed_key = attention_mixed[
        :, QUERY_HEADS * HEAD_SIZE : (QUERY_HEADS + KEY_VALUE_HEADS) * HEAD_SIZE
    ].reshape(PACK_CAPACITY, KEY_VALUE_HEADS, HEAD_SIZE)
    value_narrow = (
        attention_mixed[:, (QUERY_HEADS + KEY_VALUE_HEADS) * HEAD_SIZE :]
        .astype(jnp.bfloat16)
        .reshape(PACK_CAPACITY, KEY_VALUE_HEADS, HEAD_SIZE)
    )
    normalized_query, query_normed, query_scale = normalized_rows(query_raw, q_gain)
    query_low = (
        rotate_halves(normalized_query, cosine_per_head, sine_per_head)
        .astype(jnp.bfloat16)
        .reshape(PACK_CAPACITY, KEY_VALUE_HEADS, replica_groupings, HEAD_SIZE)
    )
    key_norm, key_normed, key_scale = normalized_rows(unnormed_key, key_norm_gain)
    key_low = rotate_halves(key_norm, cosine_per_head, sine_per_head).astype(jnp.bfloat16)
    attn, logsum = attend_forward(query_low, key_low, value_narrow, segids)
    attn_low = attn.astype(jnp.bfloat16)
    middle = inputs + jnp.dot(attn_low, out_full, preferred_element_type=jnp.float32)
    second, second_normed, second_scale = normalized_rows(middle, post_gain)
    second_low = second.astype(jnp.bfloat16)
    both = jnp.dot(second_low, gate_up_full, preferred_element_type=jnp.float32)
    gate = both[:, :FF]
    upward = both[:, FF:]
    sigma = jax.nn.sigmoid(gate)
    hidden_low = (gate * sigma * upward).astype(jnp.bfloat16)
    result = middle + jnp.dot(hidden_low, down_full, preferred_element_type=jnp.float32)
    qkv_full, out_full, gate_up_full, down_full = (
        lax.all_gather(w_qkv, "shard", axis=0, tiled=True),
        lax.all_gather(w_out, "shard", axis=0, tiled=True),
        lax.all_gather(w_gate_up, "shard", axis=0, tiled=True),
        lax.all_gather(w_down, "shard", axis=0, tiled=True),
    )
    grad_out = cotangent.astype(jnp.float32) * live[:, None].astype(jnp.float32)
    grad_low = grad_out.astype(jnp.bfloat16)
    grad_down = owned_sum(hidden_low, grad_low)
    grad_hidden = against(grad_low, down_full)
    grad_gate = grad_hidden * upward * sigma * (1.0 + gate * (1.0 - sigma))
    grad_up = grad_hidden * gate * sigma
    grad_both = jnp.concatenate([grad_gate, grad_up], axis=1).astype(jnp.bfloat16)
    grad_gate_up = owned_sum(second_low, grad_both)
    grad_second = against(grad_both, gate_up_full)
    grad_middle_norm, post_gain_grad = norm_back(
        grad_second, second_normed, second_scale, post_gain
    )
    grad_middle = grad_out + grad_middle_norm
    grad_middle_low = grad_middle.astype(jnp.bfloat16)
    grad_out_weight = owned_sum(attn_low, grad_middle_low)
    attention_gradient = against(grad_middle_low, out_full)
    attention_gradient_narrow = attention_gradient.astype(jnp.bfloat16).reshape(
        PACK_CAPACITY, KEY_VALUE_HEADS, replica_groupings, HEAD_SIZE
    )
    grad_query, grad_keys, value_gradients = attend_backward(
        query_low, key_low, value_narrow, segids, logsum, attention_gradient_narrow
    )
    grad_query = turn_back(grad_query, cosine_per_head, sine_per_head)
    grad_query_raw, q_gain_grad = norm_back(grad_query, query_normed, query_scale, q_gain)
    grad_keys = turn_back(grad_keys, cosine_per_head, sine_per_head)
    unnormed_key_gradient, k_gain_grad = norm_back(grad_keys, key_normed, key_scale, key_norm_gain)
    grad_mixed = jnp.concatenate(
        [
            grad_query_raw.reshape(PACK_CAPACITY, QUERY_HEADS * HEAD_SIZE),
            unnormed_key_gradient.reshape(PACK_CAPACITY, KEY_VALUE_HEADS * HEAD_SIZE),
            value_gradients.reshape(PACK_CAPACITY, KEY_VALUE_HEADS * HEAD_SIZE),
        ],
        axis=1,
    ).astype(jnp.bfloat16)
    grad_qkv = owned_sum(first_low, grad_mixed)
    grad_first = against(grad_mixed, qkv_full)
    grad_input_norm, in_gain_grad = norm_back(grad_first, first_normed, first_scale, in_gain)
    grad_tokens = (grad_middle + grad_input_norm).astype(jnp.bfloat16)
    gains = lax.psum((in_gain_grad, q_gain_grad, k_gain_grad, post_gain_grad), ("shard", "replica"))
    weights = (
        lax.all_gather(grad_qkv.astype(jnp.bfloat16), "replica", axis=0, tiled=True).astype(
            grad_qkv.dtype
        ),
        lax.all_gather(grad_out_weight.astype(jnp.bfloat16), "replica", axis=0, tiled=True).astype(
            grad_out_weight.dtype
        ),
        lax.all_gather(grad_gate_up.astype(jnp.bfloat16), "replica", axis=0, tiled=True).astype(
            grad_gate_up.dtype
        ),
        lax.all_gather(grad_down.astype(jnp.bfloat16), "replica", axis=0, tiled=True).astype(
            grad_down.dtype
        ),
    )
    return (
        result.astype(jnp.bfloat16),
        grad_tokens,
        gains[0],
        gains[1],
        gains[2],
        gains[3],
        weights[0],
        weights[1],
        weights[2],
        weights[3],
    )


def solution(mesh):
    in_specs = (
        P(("shard", "replica"), None),
        P(("shard", "replica"), None),
        P(),
        P(),
        P(),
        P(),
        P("shard", None),
        P("shard", None),
        P("shard", None),
        P("shard", None),
        P(("shard", "replica"), None),
    )
    out_specs = (
        P(("shard", "replica"), None),
        P(("shard", "replica"), None),
        P(),
        P(),
        P(),
        P(),
        P("shard", None),
        P("shard", None),
        P("shard", None),
        P("shard", None),
    )
    return jax.shard_map(
        on_device, mesh=mesh, in_specs=in_specs, out_specs=out_specs, check_vma=False
    )
```

profile of v0, /device:TPU:0, one launch (start us, length us, event | category | flops | bytes accessed | tf_op | source)
XLA Modules:
  0.0 3090.8 jit_solution(4346784095041720535)
XLA Ops:
  17.0 188.1 %all-gather.8.cloned.1.call-done = bf16[2048,4096]{1,0:T(8,128)(2,1)} async-done(((bf16[128,4096]{1,0:T(8,128)(2,1)}), bf16[2048,4096]{1,0:T(8,128)(2,1)}) %all-gather.8.cloned.1.call-update) | async-done | bytes 16777232 | tf_op jit(solution)/shard_map/all_gather | solution.py:175
  205.1 8.2 fusion.55
  224.1 2.9 copy.165
  236.1 82.8 %all-gather.10.cloned.1.call-done = bf16[2048,2048]{1,0:T(8,128)(2,1)} async-done(((bf16[128,2048]{1,0:T(8,128)(2,1)}), bf16[2048,2048]{1,0:T(8,128)(2,1)}) %all-gather.10.cloned.1.call-update) | async-done | bytes 8388624 | tf_op jit(solution)/shard_map/all_gather | solution.py:176
  319.0 7.6 multiply_reduce_fusion.4
  326.6 502.7 %all-gather.12.cloned.1.call-done = bf16[2048,12288]{1,0:T(8,128)(2,1)} async-done(((bf16[128,12288]{1,0:T(8,128)(2,1)}), bf16[2048,12288]{1,0:T(8,128)(2,1)}) %all-gather.12.cloned.1.call-update) | async-done | bytes 50331664 | tf_op jit(solution)/shard_map/all_gather | solution.py:177
  829.3 26.2 fusion.64
  855.5 245.9 %all-gather.14.cloned.1.call-done = bf16[6144,2048]{1,0:T(8,128)(2,1)} async-done(((bf16[384,2048]{1,0:T(8,128)(2,1)}), bf16[6144,2048]{1,0:T(8,128)(2,1)}) %all-gather.14.cloned.1.call-update) | async-done | bytes 25165840 | tf_op jit(solution)/shard_map/all_gather | solution.py:178
  1101.4 20.3 multiply_convert_fusion.1
  1121.7 24.9 multiply_reduce_fusion
  1146.6 3.2 multiply_add_fusion
  1151.1 6.7 convolution_convert_fusion
  1157.8 2.3 copy.192
  1160.1 4.3 fusion.35
  1166.5 2.8 bitcast_multiply_fusion.4
  1169.3 3.2 copy.160
  1174.4 2.6 fusion.65
  1177.0 3.5 copy.163
  1180.5 3.5 copy.162
  1184.0 4.2 pad_maximum_fusion.3
  1188.1 2.0 copy.191
  1190.2 2.7 broadcast_multiply_fusion.1
  1195.2 2.1 copy.190
  1197.3 3.1 multiply_reduce_fusion.1
  1200.5 1.9 copy.189
  1204.7 4.3 fusion.24
  1210.0 13.6 fusion.40
  1224.8 22.0 fusion.50
  1248.4 36.5 %fusion.3 = f32[2048,12288]{1,0:T(8,128)} fusion(bf16[256,6144]{1,0:T(8,128)(2,1)} %get-tuple-element.75, bf16[256,6144]{1,0:T(8,128)(2,1)} %get-tuple-element.74, f32[256,2048]{1,0:T(8,128)S(1)} %copy-done.4, f32[2048]{0:T(1024)S(1)} %copy-done.21, f32[256]{0:T(256)S(1)} %add_rsqrt_fusion.2), kind=kOutput, calls=%fused_computation.14 | convolution fusion | flops 12899057664 | bytes 109061120 | tf_op jit(solution)/shard_map/dot_general | solution.py:71
  1285.0 10.1 fusion.44
  1295.1 281.1 %reduce-scatter.5.cloned.1.call-done = f32[64,4096]{1,0:T(8,128)} async-done(((f32[2048,4096]{1,0:T(8,128)}), f32[64,4096]{1,0:T(8,128)}) %reduce-scatter.5.cloned.1.call-update) | async-done | bytes 1048592 | tf_op jit(solution)/shard_map/reduce_scatter | solution.py:75
  1576.2 2.1 convert_element_type.124
  1578.4 443.3 %reduce-scatter.11.cloned.1.call-done = f32[192,2048]{1,0:T(8,128)} async-done(((f32[6144,2048]{1,0:T(8,128)}), f32[192,2048]{1,0:T(8,128)}) %reduce-scatter.11.cloned.1.call-update) | async-done | bytes 1572880 | tf_op jit(solution)/shard_map/reduce_scatter | solution.py:75
  2021.7 2.4 convert_element_type.130
  2024.4 12.6 fusion.18
  2037.0 39.5 %all-reduce = (f32[2048]{0:T(1024)}, f32[128]{0:T(128)}, f32[128]{0:T(128)}, f32[2048]{0:T(1024)}) all-reduce(f32[2048]{0:T(1024)S(1)} %get-tuple-element.55, f32[128]{0:T(128)S(1)} %get-tuple-element.51, f32[128]{0:T(128)S(1)} %get-tuple-element.57, f32[2048]{0:T(1024)S(1)} %copy-done.37), channel_id=1, replica_groups=mesh['shard'=16,'replica'=2] {'shard','replica'}, use_global_device_ids=true, to_apply=%region_15.16 | all-reduce | flops 4352 | bytes 34816 | tf_op jit(solution)/shard_map/psum | solution.py:255
  2076.5 777.2 %reduce-scatter.9.cloned.1.call-done = f32[64,12288]{1,0:T(8,128)} async-done(((f32[2048,12288]{1,0:T(8,128)}), f32[64,12288]{1,0:T(8,128)}) %reduce-scatter.9.cloned.1.call-update) | async-done | bytes 3145744 | tf_op jit(solution)/shard_map/reduce_scatter | solution.py:75
  2853.7 3.2 convert_element_type.128
  2857.0 4.0 fusion.17
  2860.9 12.9 fusion.11
  2873.8 164.1 %reduce-scatter.7.cloned.1.call-done = f32[64,2048]{1,0:T(8,128)} async-done(((f32[2048,2048]{1,0:T(8,128)}), f32[64,2048]{1,0:T(8,128)}) %reduce-scatter.7.cloned.1.call-update) | async-done | bytes 524304 | tf_op jit(solution)/shard_map/reduce_scatter | solution.py:75
  3039.0 2.2 all_gather.33
  3042.3 7.9 all-gather.16.cloned.1.call-done
  3050.2 2.8 convert_element_type.125
  3052.9 10.2 all-gather.20.cloned.1.call-done
  3063.2 3.4 convert_element_type.131
  3066.6 12.0 all-gather.18.cloned.1.call-done
  3078.6 5.2 convert_element_type.129
  (165 shorter events, 45.6 us)
Async XLA Ops:
  7.2 198.0 %all-gather.8.cloned.1.call-start = ((), (), s32[]{:S(2)}) async-start(), calls=%async_computation.4 | async-start | bytes 17825792 | tf_op jit(solution)/shard_map/all_gather | solution.py:175
  7.9 311.0 %all-gather.10.cloned.1.call-start = ((), (), s32[]{:S(2)}) async-start(), calls=%async_computation.5 | async-start | bytes 8912896 | tf_op jit(solution)/shard_map/all_gather | solution.py:176
  8.7 1.4 copy-start.41
  8.7 820.6 %all-gather.12.cloned.1.call-start = ((), (), s32[]{:S(2)}) async-start(), calls=%async_computation.6 | async-start | bytes 53477376 | tf_op jit(solution)/shard_map/all_gather | solution.py:177
  9.4 5.3 copy-start.2
  9.4 6.3 copy-start.34
  9.4 195.7 %copy-start.26 = (f32[2048]{0:T(1024)S(1)}, f32[2048]{0:T(1024)}, u32[]{:S(2)}) copy-start(f32[2048]{0:T(1024)} %param.13) | copy-start | bytes 24580
  9.4 1091.9 %all-gather.14.cloned.1.call-start = ((), (), s32[]{:S(2)}) async-start(), calls=%async_computation.7 | async-start | bytes 26738688 | tf_op jit(solution)/shard_map/all_gather | solution.py:178
  10.0 1566.2 %reduce-scatter.5.cloned.1.call-start = ((), (), s32[]{:S(2)}) async-start(), calls=%async_computation.8 | async-start | bytes 34603008 | tf_op jit(solution)/shard_map/reduce_scatter | solution.py:75
  15.7 197.6 %copy-start.31 = (f32[256]{0:T(256)}, f32[256]{0:T(256)S(1)}, u32[]{:S(2)}) copy-start(f32[256]{0:T(256)S(1)} %add_rsqrt_fusion.3) | copy-start | bytes 3076
  213.3 2.6 copy-start.11
  227.8 1.0 copy-start.28
  227.8 1.0 copy-start.38
  229.3 1.7 copy-start.12
  231.3 1.0 copy-start.8
  232.3 2.0 copy-start
  232.3 2.0 copy-start.19
  318.9 510.4 %copy-start.21 = (f32[2048]{0:T(1024)S(1)}, f32[2048]{0:T(1024)}, u32[]{:S(2)}) copy-start(f32[2048]{0:T(1024)} %param.16) | copy-start | bytes 24580
  829.3 272.1 %copy-start.40 = (f32[256]{0:T(256)S(1)}, f32[256]{0:T(256)}, u32[]{:S(2)}) copy-start(f32[256]{0:T(256)} %fusion.58) | copy-start | bytes 3076
  1149.8 1.3 copy-start.5
  1160.1 4.3 copy-start.1
  1160.1 4.3 copy-start.7
  1160.1 4.3 copy-start.20
  1165.4 1.1 copy-start.13
  1166.4 2.8 copy-start.6
  1169.3 3.3 copy-start.23
  1183.9 6.2 copy-start.24
  1194.1 3.2 copy-start.36
  1197.3 5.8 copy-start.22
  1202.4 1.6 copy-start.9
  1202.4 2.2 copy-start.10
  1202.4 2.2 copy-start.33
  1204.6 5.3 copy-start.3
  1204.6 5.3 copy-start.17
  1204.6 5.3 copy-start.18
  1204.6 5.3 copy-start.27
  1204.7 5.3 copy-start.32
  1209.0 1.0 copy-start.16
  1223.6 1.2 copy-start.15
  1223.6 798.1 %reduce-scatter.11.cloned.1.call-start = ((), (), s32[]{:S(2)}) async-start(), calls=%async_computation.13 | async-start | bytes 51904512 | tf_op jit(solution)/shard_map/reduce_scatter | solution.py:75
  1246.8 1.6 copy-start.4
  1246.8 1606.9 %reduce-scatter.9.cloned.1.call-start = ((), (), s32[]{:S(2)}) async-start(), calls=%async_computation.11 | async-start | bytes 103809024 | tf_op jit(solution)/shard_map/reduce_scatter | solution.py:75
  1284.9 1753.0 %reduce-scatter.7.cloned.1.call-start = ((), (), s32[]{:S(2)}) async-start(), calls=%async_computation.10 | async-start | bytes 17301504 | tf_op jit(solution)/shard_map/reduce_scatter | solution.py:75
  1295.1 1755.1 %all-gather.16.cloned.1.call-start = ((), (), s32[]{:S(2)}) async-start(), calls=%async_computation.9 | async-start | bytes 1572864 | tf_op jit(solution)/shard_map/all_gather | solution.py:257
  1578.3 1484.9 %all-gather.20.cloned.1.call-start = ((), (), s32[]{:S(2)}) async-start(), calls=%async_computation.14 | async-start | bytes 2359296 | tf_op jit(solution)/shard_map/all_gather | solution.py:266
  2024.1 12.9 copy-start.37
  2024.1 1054.5 %all-gather.18.cloned.1.call-start = ((), (), s32[]{:S(2)}) async-start(), calls=%async_computation.12 | async-start | bytes 4718592 | tf_op jit(solution)/shard_map/all_gather | solution.py:263
  2857.0 4.0 copy-start.14
  (5 other events, 3.6 us)
Sparse Core Ops, SparseCore 0:
  10.8 194.3 all-gather.7
  207.9 111.0 all-gather.9
  321.7 507.5 all-gather.11
  831.9 269.4 all-gather.13
  1223.7 352.4 reduce-scatter.4
  1582.5 439.1 reduce-scatter.10
  2028.1 825.6 reduce-scatter.8
  2856.0 181.8 reduce-scatter.6
  3039.5 10.6 all-gather.15
  3052.1 10.9 all-gather.19
  3065.3 13.2 all-gather.17
where the time goes:
time: 3100 us; the launch traced here: 3090 us
  waiting for transfers between devices  2720 us (88%)
  matrix products  215 us (7%)
  other arithmetic  55.7 us (2%)
  local copies, waits for them, and re-layouts  44.6 us (1%)
  blocking collectives  41.7 us (1%)
    reduce_scatter x4, waiting for transfers between devices, owned_sum(): lax.psum_scatter(through(left, grad), ('shard', 'replica'), scatter_dimen...  1670 us
    all_gather x1, waiting for transfers between devices, on_device(): lax.all_gather(w_gate_up, 'shard', axis=0, tiled=True)  503 us
    all_gather x1, waiting for transfers between devices, on_device(): lax.all_gather(w_down, 'shard', axis=0, tiled=True)  246 us
    all_gather x1, waiting for transfers between devices, on_device(): lax.all_gather(w_qkv, 'shard', axis=0, tiled=True)  188 us
    all_gather x1, waiting for transfers between devices, on_device(): lax.all_gather(w_out, 'shard', axis=0, tiled=True)  82.8 us
    dot_general x4, matrix products, through(): lax.dot_general(left, grad, (((0,), (0,)), ((), ())), preferred_element_t...  82.2 us
    dot_general x4, matrix products, against(): lax.dot_general(grad, matrix, (((1,), (1,)), ((), ())), preferred_element...  64.6 us
  transfers between devices with their start and end apart: 11, of which 11 were waited for; matrix products, arithmetic and copies ran while one was open for 6% of the time, Pallas kernels for 0%

commit v1 on v0

v1 whole, which is shorter than its diff:
```python
import math

import jax
import jax.numpy as jnp
from jax import lax
from jax.experimental import pallas as pl
from jax.experimental.pallas import tpu as pltpu
from jax.sharding import PartitionSpec as P

QUERY_HEADS = 16
KEY_VALUE_HEADS = 8
HEAD_SIZE = 128
FF = 6144
PACK_CAPACITY = 256
NSEQ = 8
GROUPS = QUERY_HEADS // KEY_VALUE_HEADS


EPS = 1e-06
ROPE_BASE = 1000000.0
MASKED = -1e30
AXES = ("shard", "replica")
F32, BF16 = jnp.float32, jnp.bfloat16
SCALE = 1.0 / math.sqrt(HEAD_SIZE)
VMEM = 60 << 20


def pack_layout(lengths):
    ends = jnp.cumsum(lengths)
    starts = ends - lengths
    slots = jnp.arange(PACK_CAPACITY, dtype=jnp.int32)
    segment = jnp.sum((slots[:, None] >= ends[None, :]).astype(jnp.int32), axis=1)
    live = slots < ends[-1]
    labels = jnp.arange(NSEQ, dtype=jnp.int32)
    begin = jnp.sum(jnp.where(segment[:, None] == labels[None, :], starts[None, :], 0), axis=1)
    position = (slots - begin).astype(jnp.float32)
    segids = jnp.where(live, segment, NSEQ + slots)
    freqs = ROPE_BASE ** (-2.0 * jnp.arange(HEAD_SIZE // 2, dtype=jnp.float32) / HEAD_SIZE)
    angle = position[:, None] * freqs[None, :]
    cosine = jnp.concatenate([jnp.cos(angle), jnp.cos(angle)], axis=1)
    sine = jnp.concatenate([jnp.sin(angle), jnp.sin(angle)], axis=1)
    return (segids, cosine, sine, live)


def normalized_rows(value, gain):
    scale_inv = lax.rsqrt(jnp.mean(value * value, axis=-1, keepdims=True) + EPS)
    normed = value * scale_inv
    return (normed * gain, normed, scale_inv)


def norm_back(grad, normed, scale_inv, gain):
    scaled = grad * gain
    grad_in = scale_inv * (scaled - normed * jnp.mean(scaled * normed, axis=-1, keepdims=True))
    grad_gain = jnp.sum((grad * normed).reshape(-1, normed.shape[-1]), axis=0)
    return (grad_in, grad_gain)


def against(grad, matrix):
    return lax.dot_general(
        grad, matrix, (((1,), (1,)), ((), ())), preferred_element_type=jnp.float32
    )


def through(left, grad):
    return lax.dot_general(left, grad, (((0,), (0,)), ((), ())), preferred_element_type=jnp.float32)


class Wires:
    def __init__(self, shards, copies):
        self.shards, self.copies = shards, copies
        bits = shards.bit_length() - 1
        self.masks = [1 << b for b in range(bits)]
        self.top = shards >> 1
        self.team = [1, 4]
        self.far = [m for m in self.masks if m > 4]
        self.spread = self.far + [2]
        self.me = lax.axis_index("shard")
        self.core = lax.axis_index("replica")

    def send(self, value, to):
        pairs = []
        for i in range(self.shards * self.copies):
            goal = to(i // self.copies, i % self.copies)
            if goal is not None:
                pairs.append((i, goal[0] * self.copies + goal[1]))
        return lax.ppermute(value, AXES, pairs)

    def swap(self, value, mask):
        return self.send(value, lambda s, c: (s ^ mask, c))

    def swap_core(self, value):
        return self.send(value, lambda s, c: (s, 1 - c))

    def has(self, mask):
        return (self.me & mask) != 0

    def place(self, shard):
        at = 0
        for i, mask in enumerate(self.spread):
            at = at + ((shard // mask) % 2) * (1 << i)
        return at

    def others(self):
        team = self.team[0] | self.team[1]
        return sorted((s for s in range(self.shards) if s & team == 0), key=self.place)


def masks_of(order):
    out = [0]
    for mask in reversed(order):
        out = out + [mask ^ m for m in out]
    return out


def pick_columns(value, block, groups):
    rows, width = value.shape
    places = jnp.stack([jnp.asarray(g, jnp.int32) for group in groups for g in group])
    if block % 128:
        blocks = value.reshape(rows, width // block, block)
        out, at = [], 0
        for group in groups:
            taken = jnp.take(blocks, places[at : at + len(group)], axis=1)
            out.append(taken.reshape(rows, len(group) * block))
            at += len(group)
        return out
    tile = math.gcd(rows, 256)

    def kernel(places_ref, in_ref, *out_refs):
        at = 0
        for group, out_ref in zip(groups, out_refs):
            for i in range(len(group)):
                start = pl.multiple_of(places_ref[at] * block, 128)
                out_ref[:, i * block : (i + 1) * block] = in_ref[:, pl.ds(start, block)]
                at += 1

    widths = [len(group) * block for group in groups]
    return list(
        pl.pallas_call(
            kernel,
            grid_spec=pltpu.PrefetchScalarGridSpec(
                num_scalar_prefetch=1,
                grid=(rows // tile,),
                in_specs=[pl.BlockSpec((tile, width), lambda i, s: (i, 0))],
                out_specs=[pl.BlockSpec((tile, w), lambda i, s: (i, 0)) for w in widths],
            ),
            out_shape=[jax.ShapeDtypeStruct((rows, w), value.dtype) for w in widths],
            compiler_params=pltpu.CompilerParams(vmem_limit_bytes=VMEM),
            cost_estimate=pl.CostEstimate(
                flops=0, bytes_accessed=2 * rows * (width + sum(widths)), transcendentals=0
            ),
            name="pick_columns",
        )(places, value)
    )


def put_columns(values, block, groups):
    rows = values[0].shape[0]
    places = jnp.stack([jnp.asarray(g, jnp.int32) for group in groups for g in group])
    width = block * places.shape[0]
    if block % 128:
        flat = jnp.concatenate([v.astype(F32) for v in values], axis=1)
        blocks = flat.reshape(rows, width // block, block)
        return jnp.zeros_like(blocks).at[:, places].set(blocks).reshape(rows, width)
    tile = math.gcd(rows, 32)

    def kernel(places_ref, *refs):
        out_ref, at = refs[-1], 0
        for group, ref in zip(groups, refs[:-1]):
            for i in range(len(group)):
                start = pl.multiple_of(places_ref[at] * block, 128)
                part = ref[:, i * block : (i + 1) * block]
                out_ref[:, pl.ds(start, block)] = part.astype(F32)
                at += 1

    return pl.pallas_call(
        kernel,
        grid_spec=pltpu.PrefetchScalarGridSpec(
            num_scalar_prefetch=1,
            grid=(rows // tile,),
            in_specs=[pl.BlockSpec((tile, v.shape[1]), lambda i, s: (i, 0)) for v in values],
            out_specs=pl.BlockSpec((tile, width), lambda i, s: (i, 0)),
        ),
        out_shape=jax.ShapeDtypeStruct((rows, width), F32),
        compiler_params=pltpu.CompilerParams(vmem_limit_bytes=VMEM),
        cost_estimate=pl.CostEstimate(flops=0, bytes_accessed=7 * rows * width, transcendentals=0),
        name="put_columns",
    )(places, *values)


def collect(wires, own, order):
    pieces = [own]
    for at, mask in enumerate(order):
        if at == 2:
            pieces = [jnp.concatenate(pieces, axis=0)]
        pieces = pieces + [wires.swap(p, mask) for p in pieces]
    return pieces


def collect_in_order(wires, own, order):
    for mask in order:
        got, bit = wires.swap(own, mask), wires.has(mask)
        own = jnp.concatenate([jnp.where(bit, got, own), jnp.where(bit, own, got)], axis=0)
    return own


def scatter_sum(wires, keep, order):
    for mask in order:
        half = keep.shape[0] // 2
        got = wires.swap(keep[half:].astype(BF16), mask)
        keep = keep[:half].astype(F32) + got.astype(F32)
    return keep


def gather_team(wires, value):
    one, two = wires.team
    by_two = wires.swap(value, two)
    by_one = wires.swap(value, one)
    return [value, by_one, by_two, wires.swap(by_two, one)]


def sum_team(wires, parts):
    one, two = wires.team
    got_two = wires.swap(parts[3].astype(BF16), one)
    got_own = wires.swap(parts[1].astype(BF16), one)
    for_two = parts[2].astype(F32) + got_two.astype(F32)
    got = wires.swap(for_two.astype(BF16), two)
    return parts[0].astype(F32) + got_own.astype(F32) + got.astype(F32)


def team_blocks(wires, half):
    one, two = wires.team
    mine = wires.me & (one | two)
    return [
        [half * wires.shards + ((mine ^ t) | s) for s in wires.others()]
        for t in (0, one, two, one | two)
    ]


def turned(value):
    return pltpu.roll(value, HEAD_SIZE // 2, 1)


def head_forward(raw, gain, cosine, sine):
    scale = lax.rsqrt(jnp.mean(raw * raw, axis=1, keepdims=True) + EPS)
    normed = raw * scale
    v = normed * gain
    return (v * cosine + turned(v) * sine).astype(BF16), normed, scale


def head_back(grad, normed, scale, gain, cosine, sine):
    g = grad * cosine + turned(grad * sine)
    scaled = g * gain
    raw = scale * (scaled - normed * jnp.mean(scaled * normed, axis=1, keepdims=True))
    return raw, jnp.sum(g * normed, axis=0, keepdims=True)


def attend_group(first, pieces, cosine, sine, bias, q_gain, k_gain):
    tokens = first.shape[0]
    packs = tokens // PACK_CAPACITY
    width = (GROUPS + 2) * HEAD_SIZE
    n = len(pieces)
    depth = first.shape[1] // n

    def kernel(first_ref, *refs):
        w_refs = refs[:n]
        cos_ref, sin_ref, bias_ref, qg_ref, kg_ref, attn_ref, mixed_ref = refs[n:]
        mixed = jnp.zeros((tokens, width), F32)
        for i in range(n):
            mixed += jnp.dot(
                first_ref[:, i * depth : (i + 1) * depth], w_refs[i][...],
                preferred_element_type=F32,
            )
        mixed_ref[...] = mixed
        for p in range(packs):
            at = slice(p * PACK_CAPACITY, (p + 1) * PACK_CAPACITY)
            cosine, sine, bias = cos_ref[at], sin_ref[at], bias_ref[at]
            head = lambda j: mixed_ref[at, j * HEAD_SIZE : (j + 1) * HEAD_SIZE]
            key, _, _ = head_forward(head(GROUPS), kg_ref[...], cosine, sine)
            value = head(GROUPS + 1).astype(BF16)
            for j in range(GROUPS):
                query, _, _ = head_forward(head(j), qg_ref[...], cosine, sine)
                scores = against(query, key) * SCALE + bias
                expd = jnp.exp(scores - jnp.max(scores, axis=1, keepdims=True))
                probs = expd / jnp.sum(expd, axis=1, keepdims=True)
                attn = jnp.dot(probs.astype(BF16), value, preferred_element_type=F32)
                attn_ref[at, j * HEAD_SIZE : (j + 1) * HEAD_SIZE] = attn.astype(BF16)

    return pl.pallas_call(
        kernel,
        out_shape=[
            jax.ShapeDtypeStruct((tokens, GROUPS * HEAD_SIZE), BF16),
            jax.ShapeDtypeStruct((tokens, width), F32),
        ],
        compiler_params=pltpu.CompilerParams(vmem_limit_bytes=VMEM),
        cost_estimate=pl.CostEstimate(
            flops=2 * tokens * first.shape[1] * width + 8 * tokens * PACK_CAPACITY * HEAD_SIZE,
            bytes_accessed=2 * first.size + 2 * first.shape[1] * width + 6 * tokens * width,
            transcendentals=GROUPS * tokens * PACK_CAPACITY,
        ),
        name="attend_group",
    )(first, *pieces, cosine, sine, bias, q_gain, k_gain)


def attend_group_back(mixed, grad, cosine, sine, bias, q_gain, k_gain):
    tokens, width = mixed.shape
    packs = tokens // PACK_CAPACITY

    def kernel(mixed_ref, grad_ref, cos_ref, sin_ref, bias_ref, qg_ref, kg_ref, out_ref, gain_ref):
        q_gain, k_gain = qg_ref[...], kg_ref[...]
        q_sum = jnp.zeros((1, HEAD_SIZE), F32)
        k_sum = jnp.zeros((1, HEAD_SIZE), F32)
        for p in range(packs):
            at = slice(p * PACK_CAPACITY, (p + 1) * PACK_CAPACITY)
            cosine, sine, bias = cos_ref[at], sin_ref[at], bias_ref[at]
            head = lambda j: mixed_ref[at, j * HEAD_SIZE : (j + 1) * HEAD_SIZE]
            key, key_normed, key_scale = head_forward(head(GROUPS), k_gain, cosine, sine)
            value = head(GROUPS + 1).astype(BF16)
            grad_key = jnp.zeros((PACK_CAPACITY, HEAD_SIZE), F32)
            grad_value = jnp.zeros((PACK_CAPACITY, HEAD_SIZE), F32)
            for j in range(GROUPS):
                cols = slice(j * HEAD_SIZE, (j + 1) * HEAD_SIZE)
                query, normed, scale = head_forward(head(j), q_gain, cosine, sine)
                g = grad_ref[at, cols]
                scores = against(query, key) * SCALE + bias
                expd = jnp.exp(scores - jnp.max(scores, axis=1, keepdims=True))
                probs = expd / jnp.sum(expd, axis=1, keepdims=True)
                dprobs = against(g, value)
                inner = jnp.sum(probs * dprobs, axis=1, keepdims=True)
                grad_scores = (probs * (dprobs - inner)).astype(BF16)
                grad_query = jnp.dot(grad_scores, key, preferred_element_type=F32) * SCALE
                grad_key += through(grad_scores, query)
                grad_value += through(probs.astype(BF16), g)
                raw, gain = head_back(grad_query, normed, scale, q_gain, cosine, sine)
                out_ref[at, cols] = raw.astype(BF16)
                q_sum += gain
            raw, gain = head_back(grad_key * SCALE, key_normed, key_scale, k_gain, cosine, sine)
            k_sum += gain
            out_ref[at, GROUPS * HEAD_SIZE : (GROUPS + 1) * HEAD_SIZE] = raw.astype(BF16)
            out_ref[at, (GROUPS + 1) * HEAD_SIZE :] = grad_value.astype(BF16)
        gain_ref[...] = jnp.concatenate([q_sum, k_sum] + [jnp.zeros_like(q_sum)] * 6, axis=0)

    return pl.pallas_call(
        kernel,
        out_shape=[
            jax.ShapeDtypeStruct((tokens, width), BF16),
            jax.ShapeDtypeStruct((8, HEAD_SIZE), F32),
        ],
        compiler_params=pltpu.CompilerParams(vmem_limit_bytes=VMEM),
        cost_estimate=pl.CostEstimate(
            flops=20 * tokens * PACK_CAPACITY * HEAD_SIZE,
            bytes_accessed=8 * tokens * width,
            transcendentals=GROUPS * tokens * PACK_CAPACITY,
        ),
        name="attend_group_back",
    )(mixed, grad, cosine, sine, bias, q_gain, k_gain)


def spread_back(grads, weights, groups, block):
    tokens = grads[0].shape[0]
    width = sum(w.shape[0] for w in weights[0])
    places = jnp.stack([jnp.asarray(g, jnp.int32) for group in groups for g in group])
    if block % 128:
        total = 0.0
        for grad, pieces, group in zip(grads, weights, groups):
            part = jnp.concatenate([against(grad, w) for w in pieces], axis=1)
            total = total + put_columns([part], block, [group])
        return total
    flat = [w for pieces in weights for w in pieces]

    def kernel(places_ref, *refs):
        grad_refs, refs = refs[: len(grads)], refs[len(grads) :]
        out_ref, at, k = refs[-1], 0, 0
        for gi, grad_ref in enumerate(grad_refs):
            for _ in weights[gi]:
                part = against(grad_ref[...], refs[k][...])
                for b in range(part.shape[1] // block):
                    start = pl.multiple_of(places_ref[at] * block, 128)
                    cols = pl.ds(start, block)
                    new = part[:, b * block : (b + 1) * block]
                    out_ref[:, cols] = new if gi == 0 else out_ref[:, cols] + new
                    at += 1
                k += 1

    whole = lambda v: pl.BlockSpec(v.shape, lambda i, s: (0, 0))
    return pl.pallas_call(
        kernel,
        grid_spec=pltpu.PrefetchScalarGridSpec(
            num_scalar_prefetch=1,
            grid=(1,),
            in_specs=[whole(v) for v in grads] + [whole(w) for w in flat],
            out_specs=pl.BlockSpec((tokens, width), lambda i, s: (0, 0)),
        ),
        out_shape=jax.ShapeDtypeStruct((tokens, width), F32),
        compiler_params=pltpu.CompilerParams(vmem_limit_bytes=VMEM),
        cost_estimate=pl.CostEstimate(
            flops=2 * tokens * sum(w.size for w in flat),
            bytes_accessed=2 * sum(w.size for w in flat) + 8 * tokens * width,
            transcendentals=0,
        ),
        name="spread_back",
    )(places, *grads, *flat)


def feed_forward(second, own, other, grad_low, down_own, down_other, core):
    tokens, d = second.shape
    units = down_own.shape[0]
    n = len(own)
    depth = d // n
    tile, rows = 384, 256

    def kernel(core_ref, x_ref, go_ref, gx_ref, *refs):
        own_refs, other_refs = refs[:n], refs[n : 2 * n]
        do_ref, dx_ref, hidden_ref, out_own_ref, out_other_ref = refs[2 * n :]
        first = core_ref[0] == 0

        @pl.loop(0, tokens // rows)
        def _(r):
            at = pl.ds(pl.multiple_of(r * rows, rows), rows)
            a = jnp.zeros((rows, tile), F32)
            b = jnp.zeros((rows, tile), F32)
            for i in range(n):
                x = x_ref[at, i * depth : (i + 1) * depth]
                a += jnp.dot(x, own_refs[i][...], preferred_element_type=F32)
                b += jnp.dot(x, other_refs[i][...], preferred_element_type=F32)
            gate, upward = jnp.where(first, a, b), jnp.where(first, b, a)
            sigma = jax.nn.sigmoid(gate)
            silu = gate * sigma
            hidden_ref[at, :] = (silu * upward).astype(BF16)
            grad = against(go_ref[at, :], do_ref[...]) + against(gx_ref[at, :], dx_ref[...])
            grad_gate = grad * upward * sigma * (1.0 + gate * (1.0 - sigma))
            grad_up = grad * silu
            out_own_ref[at, :] = jnp.where(first, grad_gate, grad_up).astype(BF16)
            out_other_ref[at, :] = jnp.where(first, grad_up, grad_gate).astype(BF16)

    once = pl.Buffered(1)
    half = d // 2
    in_specs = [
        pl.BlockSpec((tokens, d), lambda j, s: (0, 0), pipeline_mode=once),
        pl.BlockSpec((tokens, half), lambda j, s: (0, s[0]), pipeline_mode=once),
        pl.BlockSpec((tokens, half), lambda j, s: (0, 1 - s[0]), pipeline_mode=once),
    ]
    in_specs += [pl.BlockSpec((depth, tile), lambda j, s: (0, j))] * (2 * n)
    in_specs += [pl.BlockSpec((tile, half), lambda j, s: (j, 0))] * 2
    return pl.pallas_call(
        kernel,
        grid_spec=pltpu.PrefetchScalarGridSpec(
            num_scalar_prefetch=1,
            grid=(units // tile,),
            in_specs=in_specs,
            out_specs=[pl.BlockSpec((tokens, tile), lambda j, s: (0, j))] * 3,
        ),
        out_shape=[jax.ShapeDtypeStruct((tokens, units), BF16)] * 3,
        compiler_params=pltpu.CompilerParams(vmem_limit_bytes=VMEM),
        cost_estimate=pl.CostEstimate(
            flops=6 * tokens * d * units,
            bytes_accessed=4 * tokens * d + 6 * d * units + 6 * tokens * units,
            transcendentals=tokens * units,
        ),
        name="feed_forward",
    )(core.reshape(1), second, grad_low, grad_low, *own, *other, down_own, down_other)


def feed_forward_back(grad_own, grad_other, own, other, places, block):
    tokens, units = grad_own.shape
    d = sum(w.shape[0] for w in own)
    if block % 128:
        parts = [against(grad_own, a) + against(grad_other, b) for a, b in zip(own, other)]
        return put_columns([jnp.concatenate(parts, axis=1)], block, [places]).astype(BF16)
    n, rows = len(own), 256

    def kernel(places_ref, go_ref, gx_ref, *refs):
        own_refs, other_refs, out_ref = refs[:n], refs[n : 2 * n], refs[2 * n]
        at = 0
        for i in range(n):
            part = against(go_ref[...], own_refs[i][...])
            part += against(gx_ref[...], other_refs[i][...])
            for b in range(part.shape[1] // block):
                start = pl.multiple_of(places_ref[at] * block, 128)
                out_ref[:, pl.ds(start, block)] = part[:, b * block : (b + 1) * block].astype(BF16)
                at += 1

    return pl.pallas_call(
        kernel,
        grid_spec=pltpu.PrefetchScalarGridSpec(
            num_scalar_prefetch=1,
            grid=(tokens // rows,),
            in_specs=[pl.BlockSpec((rows, units), lambda i, s: (i, 0))] * 2
            + [
                pl.BlockSpec(w.shape, lambda i, s: (0, 0), pipeline_mode=pl.Buffered(1))
                for w in own + other
            ],
            out_specs=pl.BlockSpec((rows, d), lambda i, s: (i, 0)),
        ),
        out_shape=jax.ShapeDtypeStruct((tokens, d), BF16),
        compiler_params=pltpu.CompilerParams(vmem_limit_bytes=VMEM),
        cost_estimate=pl.CostEstimate(
            flops=4 * tokens * d * units,
            bytes_accessed=4 * d * units + 4 * tokens * units + 2 * tokens * d,
            transcendentals=0,
        ),
        name="feed_forward_back",
    )(jnp.stack([jnp.asarray(p, jnp.int32) for p in places]), grad_own, grad_other, *own, *other)


def tables(lengths):
    segids, cosine, sine, live = pack_layout(lengths)
    slots = jnp.arange(PACK_CAPACITY, dtype=jnp.int32)
    allowed = (segids[:, None] == segids[None, :]) & (slots[:, None] >= slots[None, :])
    half = HEAD_SIZE // 2
    sine = jnp.concatenate([-sine[:, :half], sine[:, half:]], axis=1)
    return cosine, sine, jnp.where(allowed, 0.0, MASKED).astype(F32), live


def on_device(
    shards,
    copies,
    tokens,
    seq_lengths,
    in_gain,
    q_gain,
    key_norm_gain,
    post_gain,
    w_qkv,
    w_out,
    w_gate_up,
    w_down,
    cotangent,
):
    wires = Wires(shards, copies)
    me, core, top = wires.me, wires.core, wires.top
    first_core = core == 0
    rows = w_qkv.shape[0]
    d = in_gain.shape[0]
    half = d // 2
    by_core = lambda own, other: (jnp.where(first_core, own, other), jnp.where(first_core, other, own))
    ordered = lambda own, other: jnp.concatenate(by_core(own, other), axis=-1)
    dot = lambda a, b: jnp.dot(a, b, preferred_element_type=F32)
    through_low = lambda a, b: through(a, b).astype(BF16)
    both_packs = lambda v: jnp.concatenate([v, wires.swap_core(v)], axis=0)

    per_core = KEY_VALUE_HEADS // 2
    column_groups = [
        [GROUPS * (per_core * core + g) + j for j in range(GROUPS)]
        + [QUERY_HEADS + per_core * core + g, QUERY_HEADS + KEY_VALUE_HEADS + per_core * core + g]
        for g in range(per_core)
    ]
    orders = [wires.far + o for o in ([1, 2, 4], [2, 4, 1], [4, 1, 2], [1, 4, 2])]
    qkv = [
        collect(wires, half_group, order)
        for half_group, order in zip(pick_columns(w_qkv, HEAD_SIZE, column_groups), orders)
    ]
    at_home = wires.has(top) == (core == 1)
    away = wires.send(w_out, lambda s, c: (s ^ top, c) if (s & top != 0) == (c == 1) else None)
    out_order = [m for m in wires.far if m != top] + [1, 2, 4]
    out_pieces = collect(wires, jnp.where(at_home, w_out, away), out_order)
    out_back = out_order[::-1]
    out_rel = masks_of(out_back)

    inputs = tokens.astype(F32)
    first, first_normed, first_scale = normalized_rows(inputs, in_gain)
    first_low = both_packs(first.astype(BF16))
    block_places = [[me ^ m for m in masks_of(order[::-1])] for order in orders]
    first_moved = pick_columns(first_low, rows, block_places)
    lengths = seq_lengths.astype(F32)
    lengths_other = wires.swap_core(lengths)[0].astype(jnp.int32)
    cosine, sine, bias, live = tables(seq_lengths[0])
    packs = [
        jnp.concatenate(pair, axis=0)
        for pair in zip((cosine, sine, bias), tables(lengths_other)[:3])
    ]
    gains = [q_gain.reshape(1, -1), key_norm_gain.reshape(1, -1)]
    attn, mixed = zip(
        *[attend_group(x, w, *packs, *gains) for x, w in zip(first_moved, qkv)]
    )
    below = top - 1
    (attn_moved,) = pick_columns(
        jnp.concatenate(attn, axis=1), rows, [[(me & below) ^ m for m in out_rel]]
    )
    depth = attn_moved.shape[1] // len(out_pieces)
    out_part = sum(
        dot(attn_moved[:, i * depth : (i + 1) * depth], w) for i, w in enumerate(out_pieces)
    )
    out_got = wires.swap_core(out_part[PACK_CAPACITY:].astype(BF16))
    middle = inputs + (out_part[:PACK_CAPACITY] + out_got.astype(F32))
    second, second_normed, second_scale = normalized_rows(middle, post_gain)

    one, two = wires.team
    team = [0, one, two, one | two]
    gu_parts = pick_columns(w_gate_up, FF // shards, team_blocks(wires, core))
    gu_got = [gu_parts[0]] + [wires.swap(p, t) for p, t in zip(gu_parts[1:], team[1:])]
    gu_own = collect(wires, jnp.concatenate(gu_got, axis=0), wires.spread)
    gu_other = [wires.swap_core(p) for p in gu_own]
    (down_half,) = pick_columns(w_down, half, [[core]])
    down_own = collect_in_order(wires, down_half, wires.spread)
    down_other = wires.swap_core(down_own)

    grad_out = cotangent.astype(F32) * live[:, None].astype(F32)
    grad_low_team = jnp.concatenate(gather_team(wires, grad_out.astype(BF16)), axis=0)

    second_team = jnp.concatenate(gather_team(wires, second.astype(BF16)), axis=0)
    back = wires.spread[::-1]
    row_places = [me ^ m for m in masks_of(back + [two, one])]
    (second_moved,) = pick_columns(second_team, rows, [row_places])
    hidden_low, grad_own, grad_other = feed_forward(
        second_moved, gu_own, gu_other, grad_low_team, down_own, down_other, core
    )
    split = lambda v: [v[i * PACK_CAPACITY : (i + 1) * PACK_CAPACITY] for i in range(4)]
    grad_second = sum_team(
        wires, split(feed_forward_back(grad_own, grad_other, gu_own, gu_other, row_places, rows))
    )
    partial = jnp.concatenate([dot(hidden_low, down_own), dot(hidden_low, down_other)], axis=1)
    down_sum = sum_team(wires, split(partial.astype(BF16)))
    result = middle + ordered(down_sum[:, :half], down_sum[:, half:])

    (hidden_moved,) = pick_columns(
        hidden_low, FF // shards, [[wires.place(me ^ m) for m in masks_of(back)]]
    )
    grad_low_own, grad_low_other = pick_columns(grad_low_team, half, [[core], [1 - core]])
    down_sent = wires.swap_core(through_low(hidden_moved, grad_low_other))
    down_keep = through_low(hidden_moved, grad_low_own).astype(F32) + down_sent.astype(F32)
    down_done = scatter_sum(wires, down_keep, back)

    gu_sent = wires.swap_core(through_low(second_moved, grad_other))
    gu_keep = through_low(second_moved, grad_own).astype(F32) + gu_sent.astype(F32)
    gu_done = scatter_sum(wires, gu_keep, back)
    gu_blocks = [gu_done[i * rows : (i + 1) * rows].astype(BF16) for i in range(4)]
    gu_back = [gu_blocks[0]] + [wires.swap(b, t) for b, t in zip(gu_blocks[1:], team[1:])]
    gu_sibling = wires.swap_core(jnp.concatenate(gu_back, axis=1))

    grad_middle_norm, post_gain_grad = norm_back(
        grad_second, second_normed, second_scale, post_gain
    )
    grad_middle = grad_out + grad_middle_norm
    grad_middle_low = both_packs(grad_middle.astype(BF16))
    grad_attn_moved = jnp.concatenate([against(grad_middle_low, w) for w in out_pieces], axis=1)
    position = {m: i for i, m in enumerate(out_rel)}
    table = jnp.asarray([position[m] for m in range(len(out_rel))], jnp.int32)
    group_blocks = GROUPS * HEAD_SIZE // rows
    grad_attn = pick_columns(
        grad_attn_moved.astype(BF16),
        rows,
        [
            [table[(me & below) ^ (g * group_blocks + j)] for j in range(group_blocks)]
            for g in range(per_core)
        ],
    )
    out_keep = scatter_sum(wires, through_low(attn_moved, grad_middle_low), out_back)
    out_got = wires.send(
        out_keep.astype(BF16), lambda s, c: (s ^ top, c) if (s & top != 0) != (c == 1) else None
    )
    out_low = out_keep + out_got.astype(F32)
    out_sibling = wires.send(
        out_low.astype(BF16), lambda s, c: (s, 1 - c) if (s & top != 0) == (c == 1) else None
    )
    out_done = jnp.where(at_home, out_low, out_sibling.astype(F32))

    grad_mixed, gain_grads = zip(
        *[attend_group_back(m, g, *packs, *gains) for m, g in zip(mixed, grad_attn)]
    )
    qkv_done = [
        scatter_sum(wires, through_low(x, g), order[::-1])
        for x, g, order in zip(first_moved, grad_mixed, orders)
    ]
    grad_first_part = spread_back(grad_mixed, qkv, block_places, rows)
    first_got = wires.swap_core(grad_first_part[PACK_CAPACITY:].astype(BF16))
    grad_first = grad_first_part[:PACK_CAPACITY] + first_got.astype(F32)
    grad_input_norm, in_gain_grad = norm_back(grad_first, first_normed, first_scale, in_gain)
    grad_tokens = (grad_middle + grad_input_norm).astype(BF16)

    gain_sum = sum(gain_grads)
    sums = jnp.concatenate(
        [in_gain_grad.reshape(-1, HEAD_SIZE), post_gain_grad.reshape(-1, HEAD_SIZE), gain_sum]
    )
    sums = sums + wires.swap_core(sums)
    for mask in wires.masks:
        sums = sums + wires.swap(sums, mask)
    lanes = d // HEAD_SIZE

    qkv_low = jnp.concatenate([v.astype(BF16) for v in qkv_done], axis=1)
    qkv_sibling = wires.swap_core(qkv_low)
    other_groups = [
        [GROUPS * (per_core * (1 - core) + g) + j for j in range(GROUPS)]
        + [
            QUERY_HEADS + per_core * (1 - core) + g,
            QUERY_HEADS + KEY_VALUE_HEADS + per_core * (1 - core) + g,
        ]
        for g in range(per_core)
    ]
    return (
        result.astype(BF16),
        grad_tokens,
        sums[:lanes].reshape(-1),
        sums[2 * lanes],
        sums[2 * lanes + 1],
        sums[lanes : 2 * lanes].reshape(-1),
        put_columns([qkv_low, qkv_sibling], HEAD_SIZE, [sum(column_groups, []), sum(other_groups, [])]),
        out_done,
        put_columns(
            gu_back + [gu_sibling],
            FF // shards,
            team_blocks(wires, core) + [sum(team_blocks(wires, 1 - core), [])],
        ),
        put_columns([down_done, wires.swap_core(down_done.astype(BF16))], half, [[core], [1 - core]]),
    )


def solution(mesh):
    shards, copies = mesh.shape["shard"], mesh.shape["replica"]
    body = lambda *args: on_device(shards, copies, *args)
    in_specs = (
        P(("shard", "replica"), None),
        P(("shard", "replica"), None),
        P(),
        P(),
        P(),
        P(),
        P("shard", None),
        P("shard", None),
        P("shard", None),
        P("shard", None),
        P(("shard", "replica"), None),
    )
    out_specs = (
        P(("shard", "replica"), None),
        P(("shard", "replica"), None),
        P(),
        P(),
        P(),
        P(),
        P("shard", None),
        P("shard", None),
        P("shard", None),
        P("shard", None),
    )
    return jax.shard_map(
        body, mesh=mesh, in_specs=in_specs, out_specs=out_specs, check_vma=False
    )
```

time: 3100 us -> 1030 us (0.33)
  waiting for transfers between devices: 2720 us -> 543 us
  Pallas kernels: 0 us -> 182 us
  matrix products: 215 us -> 56.4 us
  starting transfers between devices: 0.69 us -> 99.3 us
  blocking collectives: 41.7 us -> 0 us
  other arithmetic: 55.7 us -> 91.6 us
    reduce_scatter x4 -> x0, waiting for transfers between devices: 1670 us -> none  [owned_sum(): lax.psum_scatter(through(left, grad), ('shard', 'replica'), scatter_dimen...]
    all_gather x7 -> x0, waiting for transfers between devices: 1050 us -> none  [the longest x1 503 us: on_device(): lax.all_gather(w_gate_up, 'shard', axis=0, tiled=True)]
    ppermute x0 -> x97, waiting for transfers between devices: none -> 543 us  [send(): return lax.ppermute(value, AXES, pairs)]
    pallas_call x0 -> x23, Pallas kernels: none -> 182 us  [the longest x9 39.1 us: pick_columns(): pl.pallas_call(kernel, grid_spec=pltpu.PrefetchScalarGridSpec(num_scalar_...]
    ppermute x0 -> x97, starting transfers between devices: none -> 99.3 us  [send(): return lax.ppermute(value, AXES, pairs)]
    dot_general x4 -> x2, matrix products: 64.6 us -> 4.3 us  [against(): lax.dot_general(grad, matrix, (((1,), (1,)), ((), ())), preferred_element...]
    dot_general x10 -> x4, matrix products: 68.4 us -> 16.7 us  [on_device(): dot = lambda a, b: jnp.dot(a, b, preferred_element_type=F32)]
    dot_general x4 -> x9, matrix products: 82.2 us -> 35.4 us  [through(): lax.dot_general(left, grad, (((0,), (0,)), ((), ())), preferred_element_t...]
  transfers between devices with their start and end apart: 11 -> 97, of which waited for: 11 -> 44; matrix products, arithmetic and copies ran while one was open for 6% -> 18% of each run, Pallas kernels for 0% -> 11%
where the time goes in v1:
time: 1030 us
  waiting for transfers between devices  543 us (53%)
  Pallas kernels  182 us (18%)
  starting transfers between devices  99.3 us (10%)
  other arithmetic  91.6 us (9%)
  matrix products  56.4 us (5%)
  local copies, waits for them, and re-layouts  52.2 us (5%)
    ppermute x97, waiting for transfers between devices, send(): return lax.ppermute(value, AXES, pairs)  543 us
    ppermute x97, starting transfers between devices, send(): return lax.ppermute(value, AXES, pairs)  99.3 us
    pallas_call x9, Pallas kernels, pick_columns(): pl.pallas_call(kernel, grid_spec=pltpu.PrefetchScalarGridSpec(num_scalar_...  39.1 us
    pallas_call x1, Pallas kernels, feed_forward(): pl.pallas_call(kernel, grid_spec=pltpu.PrefetchScalarGridSpec(num_scalar_...  37 us
    dot_general x9, matrix products, through(): lax.dot_general(left, grad, (((0,), (0,)), ((), ())), preferred_element_t...  35.4 us
    unnamed x221, local copies, waits for them, and re-layouts  27.1 us
    pallas_call x4, Pallas kernels, attend_group(): pl.pallas_call(kernel, out_shape=[jax.ShapeDtypeStruct((tokens, GROUPS *...  26 us
    pallas_call x4, Pallas kernels, attend_group_back(): pl.pallas_call(kernel, out_shape=[jax.ShapeDtypeStruct((tokens, width), B...  25.6 us
  transfers between devices with their start and end apart: 97, of which 44 were waited for; matrix products, arithmetic and copies ran while one was open for 18% of the time, Pallas kernels for 11%

profile of v1, /device:TPU:0, one launch (start us, length us, event | category | flops | bytes accessed | tf_op | source)
XLA Modules:
  0.0 1026.7 jit_solution(6843577398375296744)
XLA Ops:
  52.5 11.1 %collective-permute-start.16 = (bf16[128,512]{1,0:T(8,128)(2,1)}, bf16[128,512]{1,0:T(8,128)(2,1)S(1)}, u32[]{:S(2)}, u32[]{:S(2)}) collective-permute-start(bf16[128,512]{1,0:T(8,128)(2,1)} %collective-permute-done.14), channel_id=1, source_target_pairs={{0,8},{1,9},{2,10},{3,11},{4,12},{5,13},{6,14},{7,15},{8,0},{9,1},... | collective-permute-start | bytes 393224 | tf_op jit(solution)/shard_map/ppermute | solution.py:86
  71.4 9.9 collective-permute-done.10
  97.1 5.9 collective-permute-done.40
  109.1 8.8 collective-permute-done.18.refs_2_.refs_14_
  121.8 7.4 collective-permute-done.4.refs_1_.refs_5_
  132.1 7.5 collective-permute-done.25.refs_3_.refs_19_
  148.4 6.9 pick_columns.9
  155.4 6.5 attend_group.7
  161.8 6.5 attend_group.6
  171.4 6.5 attend_group.5
  177.8 11.2 %collective-permute-done.5.refs_2_.refs_6_ = bf16[512,512]{1,0:T(8,128)(2,1)} collective-permute-done((bf16[512,512]{1,0:T(8,128)(2,1)S(1)}, bf16[512,512]{1,0:T(8,128)(2,1)}, u32[]{:S(2)}, u32[]{:S(2)}) %collective-permute-start.5) | collective-permute-done | bytes 524320 | tf_op jit(solution)/shard_map/ppermute | solution.py:86
  194.7 6.5 attend_group.4
  211.7 28.9 %collective-permute-done.48 = bf16[384,1024]{1,0:T(8,128)(2,1)} collective-permute-done((bf16[384,1024]{1,0:T(8,128)(2,1)S(1)}, bf16[384,1024]{1,0:T(8,128)(2,1)}, u32[]{:S(2)}, u32[]{:S(2)}) %collective-permute-start.48) | collective-permute-done | bytes 786464 | tf_op jit(solution)/shard_map/ppermute | solution.py:86
  246.6 20.3 %collective-permute-done.41.refs_1_ = bf16[512,1536]{1,0:T(8,128)(2,1)} collective-permute-done((bf16[512,1536]{1,0:T(8,128)(2,1)}, bf16[512,1536]{1,0:T(8,128)(2,1)}, u32[]{:S(2)}, u32[]{:S(2)}) %collective-permute-start.41) | collective-permute-done | bytes 1572896 | tf_op jit(solution)/shard_map/ppermute | solution.py:86
  279.0 9.6 collective-permute-done.36
  290.0 14.5 %collective-permute-done.42.refs_2_ = bf16[512,1536]{1,0:T(8,128)(2,1)} collective-permute-done((bf16[512,1536]{1,0:T(8,128)(2,1)}, bf16[512,1536]{1,0:T(8,128)(2,1)}, u32[]{:S(2)}, u32[]{:S(2)}) %collective-permute-start.42) | collective-permute-done | bytes 1572896 | tf_op jit(solution)/shard_map/ppermute | solution.py:86
  307.4 7.4 collective-permute-done.37
  314.8 16.4 %collective-permute-done.43.refs_3_ = bf16[512,1536]{1,0:T(8,128)(2,1)} collective-permute-done((bf16[512,1536]{1,0:T(8,128)(2,1)}, bf16[512,1536]{1,0:T(8,128)(2,1)}, u32[]{:S(2)}, u32[]{:S(2)}) %collective-permute-start.43) | collective-permute-done | bytes 1572896 | tf_op jit(solution)/shard_map/ppermute | solution.py:86
  331.2 6.0 collective-permute-done.32
  337.3 22.1 %collective-permute-done.34 = bf16[256,2048]{1,0:T(8,128)(2,1)S(1)} collective-permute-done((bf16[256,2048]{1,0:T(8,128)(2,1)S(1)}, bf16[256,2048]{1,0:T(8,128)(2,1)S(1)}, u32[]{:S(2)}, u32[]{:S(2)}) %collective-permute-start.34) | collective-permute-done | bytes 1048608 | tf_op jit(solution)/shard_map/ppermute | solution.py:86
  382.8 37.0 %feed_forward.1 = (bf16[1024,1536]{1,0:T(8,128)(2,1)}, bf16[1024,1536]{1,0:T(8,128)(2,1)}, bf16[1024,1536]{1,0:T(8,128)(2,1)}) custom-call(s32[1]{0:T(128)} %bitcast.52.places_ref.core_ref, bf16[1024,2048]{1,0:T(8,128)(2,1)} %pick_columns.12.x_ref, bf16[1024,2048]{1,0:T(8,128)(2,1)} %pad_maximum_fusion.1.go_ref.gx_ref.in_ref, ...), custom_call_target="tpu_custom_call" | custom-call | flops 19327352832 | bytes 36700160 | tf_op jit(solution)/shard_map/feed_forward/pallas_call | solution.py:444
  419.8 21.7 %feed_forward_back.1 = bf16[1024,2048]{1,0:T(8,128)(2,1)} custom-call(s32[16]{0:T(128)} %stack.249.places_ref, bf16[1024,1536]{1,0:T(8,128)(2,1)} %get-tuple-element.64.go_ref, bf16[1024,1536]{1,0:T(8,128)(2,1)} %get-tuple-element.65.gx_ref, bf16[512,1536]{1,0:T(8,128)(2,1)} %constant_dynamic-update-slice_fusion.16.refs_0_, ...), custom_call_target="tpu_custom_call" | custom-call | flops 12884901888 | bytes 23068672 | tf_op jit(solution)/shard_map/feed_forward_back/pallas_call | solution.py:482
  445.7 5.9 convolution_convert_fusion.10
  451.6 6.4 convolution_convert_fusion.9
  461.4 8.8 convolution_convert_fusion
  474.8 18.0 %collective-permute-done.52 = bf16[256,2048]{1,0:T(8,128)(2,1)S(1)} collective-permute-done((bf16[256,2048]{1,0:T(8,128)(2,1)S(1)}, bf16[256,2048]{1,0:T(8,128)(2,1)S(1)}, u32[]{:S(2)}, u32[]{:S(2)}) %collective-permute-start.52) | collective-permute-done | bytes 1048608 | tf_op jit(solution)/shard_map/ppermute | solution.py:86
  494.2 8.8 convolution_convert_fusion.1
  508.3 7.1 collective-permute-done.54
  518.2 19.3 %collective-permute-done.51 = bf16[256,2048]{1,0:T(8,128)(2,1)} collective-permute-done((bf16[256,2048]{1,0:T(8,128)(2,1)}, bf16[256,2048]{1,0:T(8,128)(2,1)}, u32[]{:S(2)}, u32[]{:S(2)}) %collective-permute-start.51) | collective-permute-done | bytes 1048608 | tf_op jit(solution)/shard_map/ppermute | solution.py:86
  564.4 6.4 attend_group_back.4
  570.8 6.4 attend_group_back.5
  577.2 6.4 attend_group_back.6
  583.6 6.4 attend_group_back.7
  590.0 14.1 %spread_back.1 = f32[512,2048]{1,0:T(8,128)} custom-call(s32[64]{0:T(128)} %stack.231.places_ref, bf16[512,512]{1,0:T(8,128)(2,1)} %get-tuple-element.68.refs_0_, bf16[512,512]{1,0:T(8,128)(2,1)} %get-tuple-element.71.refs_1_, bf16[512,512]{1,0:T(8,128)(2,1)} %get-tuple-element.74.refs_2_, bf16[512,512]{1,0:T(8,128)(2,1)} %get-tuple-element.77.refs_3_, ...), custom_call_target="tpu_custom_call" | custom-call | flops 4294967296 | bytes 16777216 | tf_op jit(solution)/shard_map/spread_back/pallas_call | solution.py:385
  634.1 21.5 %collective-permute-done.72 = bf16[1024,512]{1,0:T(8,128)(2,1)S(1)} collective-permute-done((bf16[1024,512]{1,0:T(8,128)(2,1)S(1)}, bf16[1024,512]{1,0:T(8,128)(2,1)S(1)}, u32[]{:S(2)}, u32[]{:S(2)}) %collective-permute-start.72) | collective-permute-done | bytes 1048608 | tf_op jit(solution)/shard_map/ppermute | solution.py:86
  668.7 43.3 %collective-permute-done.62 = f32[40,128]{1,0:T(8,128)S(1)} collective-permute-done((f32[40,128]{1,0:T(8,128)S(1)}, f32[40,128]{1,0:T(8,128)S(1)}, u32[]{:S(2)}, u32[]{:S(2)}) %collective-permute-start.62) | collective-permute-done | bytes 20512 | tf_op jit(solution)/shard_map/ppermute | solution.py:86
  715.5 10.0 collective-permute-done.69
  727.2 11.0 %convert_add_fusion = f32[2048,1536]{1,0:T(8,128)} fusion(bf16[2048,1536]{1,0:T(8,128)(2,1)} %collective-permute-done.86, bf16[2048,1536]{1,0:T(8,128)(2,1)} %convolution_convert_fusion.1), kind=kLoop, calls=%fused_computation | loop fusion | flops 9437184 | bytes 25165824 | tf_op jit(solution)/shard_map/add | solution.py:624
  741.3 17.6 %collective-permute-done.65 = bf16[512,512]{1,0:T(8,128)(2,1)} collective-permute-done((bf16[512,512]{1,0:T(8,128)(2,1)}, bf16[512,512]{1,0:T(8,128)(2,1)}, u32[]{:S(2)}, u32[]{:S(2)}) %collective-permute-start.65) | collective-permute-done | bytes 524320 | tf_op jit(solution)/shard_map/ppermute | solution.py:86
  769.2 63.6 %collective-permute-done.70 = bf16[256,512]{1,0:T(8,128)(2,1)S(1)} collective-permute-done((bf16[256,512]{1,0:T(8,128)(2,1)S(1)}, bf16[256,512]{1,0:T(8,128)(2,1)S(1)}, u32[]{:S(2)}, u32[]{:S(2)}) %collective-permute-start.70) | collective-permute-done | bytes 262176 | tf_op jit(solution)/shard_map/ppermute | solution.py:86
  836.0 37.2 %collective-permute-done.79 = bf16[128,512]{1,0:T(8,128)(2,1)S(1)} collective-permute-done((bf16[128,512]{1,0:T(8,128)(2,1)S(1)}, bf16[128,512]{1,0:T(8,128)(2,1)S(1)}, u32[]{:S(2)}, u32[]{:S(2)}) %collective-permute-start.79) | collective-permute-done | bytes 131104 | tf_op jit(solution)/shard_map/ppermute | solution.py:86
  873.2 6.9 collective-permute-done.75
  880.2 8.9 collective-permute-done.71
  900.8 16.0 %collective-permute-done.82 = bf16[256,2048]{1,0:T(8,128)(2,1)S(1)} collective-permute-done((bf16[256,2048]{1,0:T(8,128)(2,1)S(1)}, bf16[256,2048]{1,0:T(8,128)(2,1)S(1)}, u32[]{:S(2)}, u32[]{:S(2)}) %collective-permute-start.82) | collective-permute-done | bytes 1048608 | tf_op jit(solution)/shard_map/ppermute | solution.py:86
  924.4 8.1 collective-permute-done.83
  934.0 43.1 %collective-permute-done.88 = bf16[512,1536]{1,0:T(8,128)(2,1)S(1)} collective-permute-done((bf16[512,1536]{1,0:T(8,128)(2,1)S(1)}, bf16[512,1536]{1,0:T(8,128)(2,1)S(1)}, u32[]{:S(2)}, u32[]{:S(2)}) %collective-permute-start.88) | collective-permute-done | bytes 1572896 | tf_op jit(solution)/shard_map/ppermute | solution.py:86
  994.3 7.0 collective-permute-done.91.refs_3_
  1009.8 8.5 put_columns.5
  (537 shorter events, 328.7 us)
Async XLA Ops:
  4.1 38.0 %collective-permute-start.20 = (bf16[128,512]{1,0:T(8,128)(2,1)}, bf16[128,512]{1,0:T(8,128)(2,1)}, u32[]{:S(2)}, u32[]{:S(2)}) collective-permute-start(bf16[128,512]{1,0:T(8,128)(2,1)} %get-tuple-element.57), channel_id=1, source_target_pairs={{0,16},{1,17},{2,18},{3,19},{4,20},{5,21},{6,22},{7,23},{8,24},{9,... | collective-permute-start | bytes 393224 | tf_op jit(solution)/shard_map/ppermute | solution.py:86
  8.1 37.6 %collective-permute-start.21 = (bf16[128,512]{1,0:T(8,128)(2,1)}, bf16[128,512]{1,0:T(8,128)(2,1)}, u32[]{:S(2)}, u32[]{:S(2)}) collective-permute-start(bf16[128,512]{1,0:T(8,128)(2,1)} %get-tuple-element.57), channel_id=1, source_target_pairs={{0,2},{1,3},{2,0},{3,1},{4,6},{5,7},{6,4},{7,5},{8,10},{9,11},{10,... | collective-permute-start | bytes 393224 | tf_op jit(solution)/shard_map/ppermute | solution.py:86
  9.6 37.6 %collective-permute-start.14 = (bf16[128,512]{1,0:T(8,128)(2,1)}, bf16[128,512]{1,0:T(8,128)(2,1)}, u32[]{:S(2)}, u32[]{:S(2)}) collective-permute-start(bf16[128,512]{1,0:T(8,128)(2,1)} %get-tuple-element.54), channel_id=1, source_target_pairs={{0,16},{1,17},{2,18},{3,19},{4,20},{5,21},{6,22},{7,23},{8,24},{9,... | collective-permute-start | bytes 393224 | tf_op jit(solution)/shard_map/ppermute | solution.py:86
  9.9 39.0 %collective-permute-start.15 = (bf16[128,512]{1,0:T(8,128)(2,1)}, bf16[128,512]{1,0:T(8,128)(2,1)S(1)}, u32[]{:S(2)}, u32[]{:S(2)}) collective-permute-start(bf16[128,512]{1,0:T(8,128)(2,1)} %get-tuple-element.54), channel_id=1, source_target_pairs={{0,8},{1,9},{2,10},{3,11},{4,12},{5,13},{6,14},{7,15},{8,0},{9,1},... | collective-permute-start | bytes 393224 | tf_op jit(solution)/shard_map/ppermute | solution.py:86
  105.0 101.4 %collective-permute-start.30 = (bf16[512,2048]{1,0:T(8,128)(2,1)}, bf16[512,2048]{1,0:T(8,128)(2,1)}, u32[]{:S(2)}, u32[]{:S(2)}) collective-permute-start(bf16[512,2048]{1,0:T(8,128)(2,1)} %pad_maximum_fusion.4), channel_id=1, source_target_pairs={{0,8},{1,9},{2,10},{3,11},{4,12},{5,13},{6,14},{7,15},{8,0},{9,1},... | collective-permute-start | bytes 6291464 | tf_op jit(solution)/shard_map/ppermute | solution.py:86
  129.3 39.1 %collective-permute-start.12 = (bf16[512,512]{1,0:T(8,128)(2,1)}, bf16[512,512]{1,0:T(8,128)(2,1)}, u32[]{:S(2)}, u32[]{:S(2)}) collective-permute-start(bf16[512,512]{1,0:T(8,128)(2,1)} %constant_dynamic-update-slice_fusion.4.refs_0_.refs_8_), channel_id=1, source_target_pairs={{0,2},{1,3},{2,0},{3,1},{4,6},{5,7},{6,4},{7,5},{8,10},{9,11},{10,... | collective-permute-start | bytes 1572872 | tf_op jit(solution)/shard_map/ppermute | solution.py:86
  129.3 39.2 %collective-permute-start.13 = (bf16[512,512]{1,0:T(8,128)(2,1)}, bf16[512,512]{1,0:T(8,128)(2,1)}, u32[]{:S(2)}, u32[]{:S(2)}) collective-permute-start(bf16[512,512]{1,0:T(8,128)(2,1)} %collective-permute-done.11.refs_1_.refs_9_), channel_id=1, source_target_pairs={{0,2},{1,3},{2,0},{3,1},{4,6},{5,7},{6,4},{7,5},{8,10},{9,11},{10,... | collective-permute-start | bytes 1572872 | tf_op jit(solution)/shard_map/ppermute | solution.py:86
  139.6 49.5 %collective-permute-start.5 = (bf16[512,512]{1,0:T(8,128)(2,1)S(1)}, bf16[512,512]{1,0:T(8,128)(2,1)}, u32[]{:S(2)}, u32[]{:S(2)}) collective-permute-start(bf16[512,512]{1,0:T(8,128)(2,1)S(1)} %constant_dynamic-update-slice_fusion.refs_0_.refs_4_), channel_id=1, source_target_pairs={{0,8},{1,9},{2,10},{3,11},{4,12},{5,13},{6,14},{7,15},{8,0},{9,1},... | collective-permute-start | bytes 1572872 | tf_op jit(solution)/shard_map/ppermute | solution.py:86
  145.2 49.5 %collective-permute-start.6 = (bf16[512,512]{1,0:T(8,128)(2,1)}, bf16[512,512]{1,0:T(8,128)(2,1)}, u32[]{:S(2)}, u32[]{:S(2)}) collective-permute-start(bf16[512,512]{1,0:T(8,128)(2,1)} %collective-permute-done.4.refs_1_.refs_5_), channel_id=1, source_target_pairs={{0,8},{1,9},{2,10},{3,11},{4,12},{5,13},{6,14},{7,15},{8,0},{9,1},... | collective-permute-start | bytes 1572872 | tf_op jit(solution)/shard_map/ppermute | solution.py:86
  168.4 72.2 %collective-permute-start.48 = (bf16[384,1024]{1,0:T(8,128)(2,1)S(1)}, bf16[384,1024]{1,0:T(8,128)(2,1)}, u32[]{:S(2)}, u32[]{:S(2)}) collective-permute-start(bf16[384,1024]{1,0:T(8,128)(2,1)S(1)} %copy-done.32), channel_id=1, source_target_pairs={{0,16},{1,17},{2,18},{3,19},{4,20},{5,21},{6,22},{7,23},{8,24},{9,... | collective-permute-start | bytes 2359304 | tf_op jit(solution)/shard_map/ppermute | solution.py:86
  168.5 98.4 %collective-permute-start.41 = (bf16[512,1536]{1,0:T(8,128)(2,1)}, bf16[512,1536]{1,0:T(8,128)(2,1)}, u32[]{:S(2)}, u32[]{:S(2)}) collective-permute-start(bf16[512,1536]{1,0:T(8,128)(2,1)} %constant_dynamic-update-slice_fusion.16.refs_0_), channel_id=1, source_target_pairs={{0,16},{1,17},{2,18},{3,19},{4,20},{5,21},{6,22},{7,23},{8,24},{9,... | collective-permute-start | bytes 4718600 | tf_op jit(solution)/shard_map/ppermute | solution.py:86
  211.0 56.8 %collective-permute-start.31 = (bf16[256,2048]{1,0:T(8,128)(2,1)S(1)}, bf16[256,2048]{1,0:T(8,128)(2,1)S(1)}, u32[]{:S(2)}, u32[]{:S(2)}) collective-permute-start(bf16[256,2048]{1,0:T(8,128)(2,1)S(1)} %slice.502), channel_id=1, source_target_pairs={{0,1},{1,0},{2,3},{3,2},{4,5},{5,4},{6,7},{7,6},{8,9},{9,8},{10,11... | collective-permute-start | bytes 3145736 | tf_op jit(solution)/shard_map/ppermute | solution.py:86
  245.1 43.6 %collective-permute-start.36 = (bf16[256,2048]{1,0:T(8,128)(2,1)}, bf16[256,2048]{1,0:T(8,128)(2,1)}, u32[]{:S(2)}, u32[]{:S(2)}) collective-permute-start(bf16[256,2048]{1,0:T(8,128)(2,1)} %fusion.14), channel_id=1, source_target_pairs={{0,8},{1,9},{2,10},{3,11},{4,12},{5,13},{6,14},{7,15},{8,0},{9,1},... | collective-permute-start | bytes 3145736 | tf_op jit(solution)/shard_map/ppermute | solution.py:86
  245.1 43.6 %collective-permute-start.35 = (bf16[256,2048]{1,0:T(8,128)(2,1)}, bf16[256,2048]{1,0:T(8,128)(2,1)}, u32[]{:S(2)}, u32[]{:S(2)}) collective-permute-start(bf16[256,2048]{1,0:T(8,128)(2,1)} %fusion.14), channel_id=1, source_target_pairs={{0,2},{1,3},{2,0},{3,1},{4,6},{5,7},{6,4},{7,5},{8,10},{9,11},{10,... | collective-permute-start | bytes 3145736 | tf_op jit(solution)/shard_map/ppermute | solution.py:86
  266.9 37.6 %collective-permute-start.42 = (bf16[512,1536]{1,0:T(8,128)(2,1)}, bf16[512,1536]{1,0:T(8,128)(2,1)}, u32[]{:S(2)}, u32[]{:S(2)}) collective-permute-start(bf16[512,1536]{1,0:T(8,128)(2,1)} %constant_dynamic-update-slice_fusion.16.refs_0_), channel_id=1, source_target_pairs={{0,4},{1,5},{2,6},{3,7},{4,0},{5,1},{6,2},{7,3},{8,12},{9,13},{10,... | collective-permute-start | bytes 4718600 | tf_op jit(solution)/shard_map/ppermute | solution.py:86
  268.8 62.5 %collective-permute-start.43 = (bf16[512,1536]{1,0:T(8,128)(2,1)}, bf16[512,1536]{1,0:T(8,128)(2,1)}, u32[]{:S(2)}, u32[]{:S(2)}) collective-permute-start(bf16[512,1536]{1,0:T(8,128)(2,1)} %collective-permute-done.41.refs_1_), channel_id=1, source_target_pairs={{0,4},{1,5},{2,6},{3,7},{4,0},{5,1},{6,2},{7,3},{8,12},{9,13},{10,... | collective-permute-start | bytes 4718600 | tf_op jit(solution)/shard_map/ppermute | solution.py:86
  272.6 34.8 %collective-permute-start.33 = (bf16[256,2048]{1,0:T(8,128)(2,1)S(1)}, bf16[256,2048]{1,0:T(8,128)(2,1)S(1)}, u32[]{:S(2)}, u32[]{:S(2)}) collective-permute-start(bf16[256,2048]{1,0:T(8,128)(2,1)S(1)} %multiply_convert_fusion), channel_id=1, source_target_pairs={{0,8},{1,9},{2,10},{3,11},{4,12},{5,13},{6,14},{7,15},{8,0},{9,1},... | collective-permute-start | bytes 3145736 | tf_op jit(solution)/shard_map/ppermute | solution.py:86
  288.7 94.2 %collective-permute-start.50 = (bf16[1536,1024]{1,0:T(8,128)(2,1)}, bf16[1536,1024]{1,0:T(8,128)(2,1)}, u32[]{:S(2)}, u32[]{:S(2)}) collective-permute-start(bf16[1536,1024]{1,0:T(8,128)(2,1)} %pad_maximum_fusion.2.refs_8_), channel_id=1, source_target_pairs={{0,1},{1,0},{2,3},{3,2},{4,5},{5,4},{6,7},{7,6},{8,9},{9,8},{10,11... | collective-permute-start | bytes 9437192 | tf_op jit(solution)/shard_map/ppermute | solution.py:86
  304.5 32.8 %collective-permute-start.32 = (bf16[256,2048]{1,0:T(8,128)(2,1)S(1)}, bf16[256,2048]{1,0:T(8,128)(2,1)S(1)}, u32[]{:S(2)}, u32[]{:S(2)}) collective-permute-start(bf16[256,2048]{1,0:T(8,128)(2,1)S(1)} %multiply_convert_fusion), channel_id=1, source_target_pairs={{0,2},{1,3},{2,0},{3,1},{4,6},{5,7},{6,4},{7,5},{8,10},{9,11},{10,... | collective-permute-start | bytes 3145736 | tf_op jit(solution)/shard_map/ppermute | solution.py:86
  307.4 52.0 %collective-permute-start.34 = (bf16[256,2048]{1,0:T(8,128)(2,1)S(1)}, bf16[256,2048]{1,0:T(8,128)(2,1)S(1)}, u32[]{:S(2)}, u32[]{:S(2)}) collective-permute-start(bf16[256,2048]{1,0:T(8,128)(2,1)S(1)} %collective-permute-done.33), channel_id=1, source_target_pairs={{0,2},{1,3},{2,0},{3,1},{4,6},{5,7},{6,4},{7,5},{8,10},{9,11},{10,... | collective-permute-start | bytes 3145736 | tf_op jit(solution)/shard_map/ppermute | solution.py:86
  314.8 68.0 %collective-permute-start.44 = (bf16[512,1536]{1,0:T(8,128)(2,1)}, bf16[512,1536]{1,0:T(8,128)(2,1)}, u32[]{:S(2)}, u32[]{:S(2)}) collective-permute-start(bf16[512,1536]{1,0:T(8,128)(2,1)} %constant_dynamic-update-slice_fusion.16.refs_0_), channel_id=1, source_target_pairs={{0,1},{1,0},{2,3},{3,2},{4,5},{5,4},{6,7},{7,6},{8,9},{9,8},{10,11... | collective-permute-start | bytes 4718600 | tf_op jit(solution)/shard_map/ppermute | solution.py:86
  331.2 51.6 %collective-permute-start.45 = (bf16[512,1536]{1,0:T(8,128)(2,1)}, bf16[512,1536]{1,0:T(8,128)(2,1)}, u32[]{:S(2)}, u32[]{:S(2)}) collective-permute-start(bf16[512,1536]{1,0:T(8,128)(2,1)} %collective-permute-done.41.refs_1_), channel_id=1, source_target_pairs={{0,1},{1,0},{2,3},{3,2},{4,5},{5,4},{6,7},{7,6},{8,9},{9,8},{10,11... | collective-permute-start | bytes 4718600 | tf_op jit(solution)/shard_map/ppermute | solution.py:86
  337.3 45.5 %collective-permute-start.46 = (bf16[512,1536]{1,0:T(8,128)(2,1)}, bf16[512,1536]{1,0:T(8,128)(2,1)}, u32[]{:S(2)}, u32[]{:S(2)}) collective-permute-start(bf16[512,1536]{1,0:T(8,128)(2,1)} %collective-permute-done.42.refs_2_), channel_id=1, source_target_pairs={{0,1},{1,0},{2,3},{3,2},{4,5},{5,4},{6,7},{7,6},{8,9},{9,8},{10,11... | collective-permute-start | bytes 4718600 | tf_op jit(solution)/shard_map/ppermute | solution.py:86
  459.2 33.6 %collective-permute-start.52 = (bf16[256,2048]{1,0:T(8,128)(2,1)S(1)}, bf16[256,2048]{1,0:T(8,128)(2,1)S(1)}, u32[]{:S(2)}, u32[]{:S(2)}) collective-permute-start(bf16[256,2048]{1,0:T(8,128)(2,1)S(1)} %get-tuple-element.97), channel_id=1, source_target_pairs={{0,2},{1,3},{2,0},{3,1},{4,6},{5,7},{6,4},{7,5},{8,10},{9,11},{10,... | collective-permute-start | bytes 3145736 | tf_op jit(solution)/shard_map/ppermute | solution.py:86
  470.2 45.2 %collective-permute-start.54 = (bf16[256,2048]{1,0:T(8,128)(2,1)}, bf16[256,2048]{1,0:T(8,128)(2,1)}, u32[]{:S(2)}, u32[]{:S(2)}) collective-permute-start(bf16[256,2048]{1,0:T(8,128)(2,1)} %get-tuple-element.94), channel_id=1, source_target_pairs={{0,2},{1,3},{2,0},{3,1},{4,6},{5,7},{6,4},{7,5},{8,10},{9,11},{10,... | collective-permute-start | bytes 3145736 | tf_op jit(solution)/shard_map/ppermute | solution.py:86
  470.9 66.6 %collective-permute-start.51 = (bf16[256,2048]{1,0:T(8,128)(2,1)}, bf16[256,2048]{1,0:T(8,128)(2,1)}, u32[]{:S(2)}, u32[]{:S(2)}) collective-permute-start(bf16[256,2048]{1,0:T(8,128)(2,1)} %get-tuple-element.96), channel_id=1, source_target_pairs={{0,2},{1,3},{2,0},{3,1},{4,6},{5,7},{6,4},{7,5},{8,10},{9,11},{10,... | collective-permute-start | bytes 3145736 | tf_op jit(solution)/shard_map/ppermute | solution.py:86
  474.8 40.6 %collective-permute-start.56 = (bf16[256,2048]{1,0:T(8,128)(2,1)}, bf16[256,2048]{1,0:T(8,128)(2,1)}, u32[]{:S(2)}, u32[]{:S(2)}) collective-permute-start(bf16[256,2048]{1,0:T(8,128)(2,1)} %add_convert_fusion), channel_id=1, source_target_pairs={{0,8},{1,9},{2,10},{3,11},{4,12},{5,13},{6,14},{7,15},{8,0},{9,1},... | collective-permute-start | bytes 3145736 | tf_op jit(solution)/shard_map/ppermute | solution.py:86
  494.2 43.3 %collective-permute-start.53 = (bf16[256,2048]{1,0:T(8,128)(2,1)}, bf16[256,2048]{1,0:T(8,128)(2,1)}, u32[]{:S(2)}, u32[]{:S(2)}) collective-permute-start(bf16[256,2048]{1,0:T(8,128)(2,1)} %add_convert_fusion.1), channel_id=1, source_target_pairs={{0,8},{1,9},{2,10},{3,11},{4,12},{5,13},{6,14},{7,15},{8,0},{9,1},... | collective-permute-start | bytes 3145736 | tf_op jit(solution)/shard_map/ppermute | solution.py:86
  503.0 222.6 %collective-permute-start.86 = (bf16[2048,1536]{1,0:T(8,128)(2,1)}, bf16[2048,1536]{1,0:T(8,128)(2,1)}, u32[]{:S(2)}, u32[]{:S(2)}) collective-permute-start(bf16[2048,1536]{1,0:T(8,128)(2,1)} %convolution_convert_fusion), channel_id=1, source_target_pairs={{0,1},{1,0},{2,3},{3,2},{4,5},{5,4},{6,7},{7,6},{8,9},{9,8},{10,11... | collective-permute-start | bytes 18874376 | tf_op jit(solution)/shard_map/ppermute | solution.py:86
  550.5 73.4 %collective-permute-start.93 = (bf16[1536,1024]{1,0:T(8,128)(2,1)}, bf16[1536,1024]{1,0:T(8,128)(2,1)}, u32[]{:S(2)}, u32[]{:S(2)}) collective-permute-start(bf16[1536,1024]{1,0:T(8,128)(2,1)} %convolution_convert_fusion.3), channel_id=1, source_target_pairs={{0,1},{1,0},{2,3},{3,2},{4,5},{5,4},{6,7},{7,6},{8,9},{9,8},{10,11... | collective-permute-start | bytes 9437192 | tf_op jit(solution)/shard_map/ppermute | solution.py:86
  610.6 44.9 %collective-permute-start.72 = (bf16[1024,512]{1,0:T(8,128)(2,1)S(1)}, bf16[1024,512]{1,0:T(8,128)(2,1)S(1)}, u32[]{:S(2)}, u32[]{:S(2)}) collective-permute-start(bf16[1024,512]{1,0:T(8,128)(2,1)S(1)} %slice.353), channel_id=1, source_target_pairs={{0,4},{1,5},{2,6},{3,7},{4,0},{5,1},{6,2},{7,3},{8,12},{9,13},{10,... | collective-permute-start | bytes 3145736 | tf_op jit(solution)/shard_map/ppermute | solution.py:86
  623.9 32.8 %collective-permute-start.68 = (bf16[1024,512]{1,0:T(8,128)(2,1)S(1)}, bf16[1024,512]{1,0:T(8,128)(2,1)}, u32[]{:S(2)}, u32[]{:S(2)}) collective-permute-start(bf16[1024,512]{1,0:T(8,128)(2,1)S(1)} %slice.345), channel_id=1, source_target_pairs={{0,2},{1,3},{2,0},{3,1},{4,6},{5,7},{6,4},{7,5},{8,10},{9,11},{10,... | collective-permute-start | bytes 3145736 | tf_op jit(solution)/shard_map/ppermute | solution.py:86
  633.7 255.4 %collective-permute-start.81 = (bf16[512,2048]{1,0:T(8,128)(2,1)}, bf16[512,2048]{1,0:T(8,128)(2,1)}, u32[]{:S(2)}, u32[]{:S(2)}) collective-permute-start(bf16[512,2048]{1,0:T(8,128)(2,1)} %slice.369), channel_id=1, source_target_pairs={{0,8},{1,9},{2,10},{3,11},{4,12},{5,13},{6,14},{7,15},{8,0},{9,1},... | collective-permute-start | bytes 6291464 | tf_op jit(solution)/shard_map/ppermute | solution.py:86
  656.7 56.0 %collective-permute-start.77 = (bf16[512,512]{1,0:T(8,128)(2,1)S(1)}, bf16[512,512]{1,0:T(8,128)(2,1)S(1)}, u32[]{:S(2)}, u32[]{:S(2)}) collective-permute-start(bf16[512,512]{1,0:T(8,128)(2,1)S(1)} %slice.505), channel_id=1, source_target_pairs={{0,8},{1,9},{2,10},{3,11},{4,12},{5,13},{6,14},{7,15},{8,0},{9,1},... | collective-permute-start | bytes 1572872 | tf_op jit(solution)/shard_map/ppermute | solution.py:86
  660.6 53.4 %collective-permute-start.73 = (bf16[512,512]{1,0:T(8,128)(2,1)S(1)}, bf16[512,512]{1,0:T(8,128)(2,1)S(1)}, u32[]{:S(2)}, u32[]{:S(2)}) collective-permute-start(bf16[512,512]{1,0:T(8,128)(2,1)S(1)} %slice.506), channel_id=1, source_target_pairs={{0,2},{1,3},{2,0},{3,1},{4,6},{5,7},{6,4},{7,5},{8,10},{9,11},{10,... | collective-permute-start | bytes 1572872 | tf_op jit(solution)/shard_map/ppermute | solution.py:86
  665.7 46.3 %collective-permute-start.62 = (f32[40,128]{1,0:T(8,128)S(1)}, f32[40,128]{1,0:T(8,128)S(1)}, u32[]{:S(2)}, u32[]{:S(2)}) collective-permute-start(f32[40,128]{1,0:T(8,128)S(1)} %add.550), channel_id=1, source_target_pairs={{0,8},{1,9},{2,10},{3,11},{4,12},{5,13},{6,14},{7,15},{8,0},{9,1},... | collective-permute-start | bytes 61448 | tf_op jit(solution)/shard_map/ppermute | solution.py:86
  712.0 49.0 %collective-permute-start.94 = (bf16[768,1024]{1,0:T(8,128)(2,1)}, bf16[768,1024]{1,0:T(8,128)(2,1)}, u32[]{:S(2)}, u32[]{:S(2)}) collective-permute-start(bf16[768,1024]{1,0:T(8,128)(2,1)} %slice.498), channel_id=1, source_target_pairs={{0,4},{1,5},{2,6},{3,7},{4,0},{5,1},{6,2},{7,3},{8,12},{9,13},{10,... | collective-permute-start | bytes 4718600 | tf_op jit(solution)/shard_map/ppermute | solution.py:86
  714.0 45.0 %collective-permute-start.65 = (bf16[512,512]{1,0:T(8,128)(2,1)}, bf16[512,512]{1,0:T(8,128)(2,1)}, u32[]{:S(2)}, u32[]{:S(2)}) collective-permute-start(bf16[512,512]{1,0:T(8,128)(2,1)} %slice.508), channel_id=1, source_target_pairs={{0,4},{1,5},{2,6},{3,7},{4,0},{5,1},{6,2},{7,3},{8,12},{9,13},{10,... | collective-permute-start | bytes 1572872 | tf_op jit(solution)/shard_map/ppermute | solution.py:86
  725.4 278.9 %collective-permute-start.63 = (f32[40,128]{1,0:T(8,128)S(1)}, f32[40,128]{1,0:T(8,128)S(1)}, u32[]{:S(2)}, u32[]{:S(2)}) collective-permute-start(f32[40,128]{1,0:T(8,128)S(1)} %add.551), channel_id=1, source_target_pairs={{0,16},{1,17},{2,18},{3,19},{4,20},{5,21},{6,22},{7,23},{8,24},{9,... | collective-permute-start | bytes 61448 | tf_op jit(solution)/shard_map/ppermute | solution.py:86
  725.6 40.1 %collective-permute-start.78 = (bf16[256,512]{1,0:T(8,128)(2,1)}, bf16[256,512]{1,0:T(8,128)(2,1)S(1)}, u32[]{:S(2)}, u32[]{:S(2)}) collective-permute-start(bf16[256,512]{1,0:T(8,128)(2,1)} %slice.509), channel_id=1, source_target_pairs={{0,2},{1,3},{2,0},{3,1},{4,6},{5,7},{6,4},{7,5},{8,10},{9,11},{10,... | collective-permute-start | bytes 786440 | tf_op jit(solution)/shard_map/ppermute | solution.py:86
  759.0 138.5 %collective-permute-start.87 = (bf16[1024,1536]{1,0:T(8,128)(2,1)S(1)}, bf16[1024,1536]{1,0:T(8,128)(2,1)}, u32[]{:S(2)}, u32[]{:S(2)}) collective-permute-start(bf16[1024,1536]{1,0:T(8,128)(2,1)S(1)} %slice.497), channel_id=1, source_target_pairs={{0,4},{1,5},{2,6},{3,7},{4,0},{5,1},{6,2},{7,3},{8,12},{9,13},{10,... | collective-permute-start | bytes 9437192 | tf_op jit(solution)/shard_map/ppermute | solution.py:86
  765.8 67.0 %collective-permute-start.70 = (bf16[256,512]{1,0:T(8,128)(2,1)S(1)}, bf16[256,512]{1,0:T(8,128)(2,1)S(1)}, u32[]{:S(2)}, u32[]{:S(2)}) collective-permute-start(bf16[256,512]{1,0:T(8,128)(2,1)S(1)} %slice.511), channel_id=1, source_target_pairs={{0,4},{1,5},{2,6},{3,7},{4,0},{5,1},{6,2},{7,3},{8,12},{9,13},{10,... | collective-permute-start | bytes 786440 | tf_op jit(solution)/shard_map/ppermute | solution.py:86
  767.5 65.5 %collective-permute-start.66 = (bf16[256,512]{1,0:T(8,128)(2,1)S(1)}, bf16[256,512]{1,0:T(8,128)(2,1)S(1)}, u32[]{:S(2)}, u32[]{:S(2)}) collective-permute-start(bf16[256,512]{1,0:T(8,128)(2,1)S(1)} %slice.512), channel_id=1, source_target_pairs={{0,2},{1,3},{2,0},{3,1},{4,6},{5,7},{6,4},{7,5},{8,10},{9,11},{10,... | collective-permute-start | bytes 786440 | tf_op jit(solution)/shard_map/ppermute | solution.py:86
  832.8 88.7 %collective-permute-start.95 = (bf16[384,1024]{1,0:T(8,128)(2,1)}, bf16[384,1024]{1,0:T(8,128)(2,1)}, u32[]{:S(2)}, u32[]{:S(2)}) collective-permute-start(bf16[384,1024]{1,0:T(8,128)(2,1)} %slice.503), channel_id=1, source_target_pairs={{0,16},{1,17},{2,18},{3,19},{4,20},{5,21},{6,22},{7,23},{8,24},{9,... | collective-permute-start | bytes 2359304 | tf_op jit(solution)/shard_map/ppermute | solution.py:86
  832.9 40.2 %collective-permute-start.79 = (bf16[128,512]{1,0:T(8,128)(2,1)S(1)}, bf16[128,512]{1,0:T(8,128)(2,1)S(1)}, u32[]{:S(2)}, u32[]{:S(2)}) collective-permute-start(bf16[128,512]{1,0:T(8,128)(2,1)S(1)} %slice.513), channel_id=1, source_target_pairs={{0,16},{1,17},{2,18},{3,19},{4,20},{5,21},{6,22},{7,23},{8,24},{9,... | collective-permute-start | bytes 393224 | tf_op jit(solution)/shard_map/ppermute | solution.py:86
  900.7 76.4 %collective-permute-start.88 = (bf16[512,1536]{1,0:T(8,128)(2,1)S(1)}, bf16[512,1536]{1,0:T(8,128)(2,1)S(1)}, u32[]{:S(2)}, u32[]{:S(2)}) collective-permute-start(bf16[512,1536]{1,0:T(8,128)(2,1)S(1)} %slice.499), channel_id=1, source_target_pairs={{0,16},{1,17},{2,18},{3,19},{4,20},{5,21},{6,22},{7,23},{8,24},{9,... | collective-permute-start | bytes 4718600 | tf_op jit(solution)/shard_map/ppermute | solution.py:86
  921.4 84.2 %collective-permute-start.80 = (bf16[128,2048]{1,0:T(8,128)(2,1)S(1)}, bf16[128,2048]{1,0:T(8,128)(2,1)}, u32[]{:S(2)}, u32[]{:S(2)}) collective-permute-start(bf16[128,2048]{1,0:T(8,128)(2,1)S(1)} %pad_maximum_fusion.15.refs_0_), channel_id=1, source_target_pairs={{0,1},{1,0},{2,3},{3,2},{4,5},{5,4},{6,7},{7,6},{8,9},{9,8},{10,11... | collective-permute-start | bytes 1572872 | tf_op jit(solution)/shard_map/ppermute | solution.py:86
  932.7 50.1 %collective-permute-start.84 = (bf16[128,2048]{1,0:T(8,128)(2,1)S(1)}, bf16[128,2048]{1,0:T(8,128)(2,1)S(1)}, u32[]{:S(2)}, u32[]{:S(2)}) collective-permute-start(bf16[128,2048]{1,0:T(8,128)(2,1)S(1)} %fusion.22), channel_id=1, source_target_pairs={{1,17},{3,19},{5,21},{7,23},{9,25},{11,27},{13,29},{15,31},{16,0},... | collective-permute-start | bytes 1572872 | tf_op jit(solution)/shard_map/ppermute | solution.py:86
  (153 other events, 2516.8 us)

commit v2 on v1

v2 whole, which is shorter than its diff:
```python
import math

import jax
import jax.numpy as jnp
from jax import lax
from jax.experimental import pallas as pl
from jax.experimental.pallas import tpu as pltpu
from jax.sharding import PartitionSpec as P

QUERY_HEADS = 16
KEY_VALUE_HEADS = 8
HEAD_SIZE = 128
FF = 6144
PACK_CAPACITY = 256
NSEQ = 8
GROUPS = QUERY_HEADS // KEY_VALUE_HEADS


EPS = 1e-06
ROPE_BASE = 1000000.0
MASKED = -1e30
AXES = ("shard", "replica")
F32, BF16 = jnp.float32, jnp.bfloat16
SCALE = 1.0 / math.sqrt(HEAD_SIZE)
VMEM = 60 << 20
LIGHT = pl.CostEstimate(flops=1, bytes_accessed=1, transcendentals=0)


def pack_layout(lengths):
    ends = jnp.cumsum(lengths)
    starts = ends - lengths
    slots = jnp.arange(PACK_CAPACITY, dtype=jnp.int32)
    segment = jnp.sum((slots[:, None] >= ends[None, :]).astype(jnp.int32), axis=1)
    live = slots < ends[-1]
    labels = jnp.arange(NSEQ, dtype=jnp.int32)
    begin = jnp.sum(jnp.where(segment[:, None] == labels[None, :], starts[None, :], 0), axis=1)
    position = (slots - begin).astype(jnp.float32)
    segids = jnp.where(live, segment, NSEQ + slots)
    freqs = ROPE_BASE ** (-2.0 * jnp.arange(HEAD_SIZE // 2, dtype=jnp.float32) / HEAD_SIZE)
    angle = position[:, None] * freqs[None, :]
    cosine = jnp.concatenate([jnp.cos(angle), jnp.cos(angle)], axis=1)
    sine = jnp.concatenate([jnp.sin(angle), jnp.sin(angle)], axis=1)
    return (segids, cosine, sine, live)


def normalized_rows(value, gain):
    scale_inv = lax.rsqrt(jnp.mean(value * value, axis=-1, keepdims=True) + EPS)
    normed = value * scale_inv
    return (normed * gain, normed, scale_inv)


def norm_back(grad, normed, scale_inv, gain):
    scaled = grad * gain
    grad_in = scale_inv * (scaled - normed * jnp.mean(scaled * normed, axis=-1, keepdims=True))
    grad_gain = jnp.sum((grad * normed).reshape(-1, normed.shape[-1]), axis=0)
    return (grad_in, grad_gain)


def against(grad, matrix):
    return lax.dot_general(
        grad, matrix, (((1,), (1,)), ((), ())), preferred_element_type=jnp.float32
    )


def through(left, grad):
    return lax.dot_general(left, grad, (((0,), (0,)), ((), ())), preferred_element_type=jnp.float32)


class Wires:
    def __init__(self, shards, copies):
        self.shards, self.copies = shards, copies
        bits = shards.bit_length() - 1
        self.masks = [1 << b for b in range(bits)]
        self.top = shards >> 1
        self.team = [1, 4]
        self.far = [m for m in self.masks if m > 4]
        self.spread = [2] + self.far
        self.me = lax.axis_index("shard")
        self.core = lax.axis_index("replica")

    def send(self, value, to):
        pairs = []
        for i in range(self.shards * self.copies):
            goal = to(i // self.copies, i % self.copies)
            if goal is not None:
                pairs.append((i, goal[0] * self.copies + goal[1]))
        return lax.ppermute(value, AXES, pairs)

    def swap(self, value, mask):
        return self.send(value, lambda s, c: (s ^ mask, c))

    def swap_core(self, value):
        return self.send(value, lambda s, c: (s, 1 - c))

    def has(self, mask):
        return (self.me & mask) != 0

    def sharers(self):
        return self.groups(self.team)

    def teams(self):
        return self.groups(self.spread)

    def groups(self, fixed):
        fixed = sum(fixed)
        return [
            [s for s in range(self.shards) if s & fixed == f]
            for f in sorted({s & fixed for s in range(self.shards)})
        ]

    def others(self):
        return self.sharers()[0]


def masks_of(order):
    out = [0]
    for mask in reversed(order):
        out = out + [mask ^ m for m in out]
    return out


def pick_columns(value, block, groups):
    rows, width = value.shape
    places = jnp.stack([jnp.asarray(g, jnp.int32) for group in groups for g in group])
    if block % 128:
        blocks = value.reshape(rows, width // block, block)
        out, at = [], 0
        for group in groups:
            taken = jnp.take(blocks, places[at : at + len(group)], axis=1)
            out.append(taken.reshape(rows, len(group) * block))
            at += len(group)
        return out
    tile = math.gcd(rows, 256)

    def kernel(places_ref, in_ref, *out_refs):
        at = 0
        for group, out_ref in zip(groups, out_refs):
            for i in range(len(group)):
                start = pl.multiple_of(places_ref[at] * block, 128)
                out_ref[:, i * block : (i + 1) * block] = in_ref[:, pl.ds(start, block)]
                at += 1

    widths = [len(group) * block for group in groups]
    return list(
        pl.pallas_call(
            kernel,
            grid_spec=pltpu.PrefetchScalarGridSpec(
                num_scalar_prefetch=1,
                grid=(rows // tile,),
                in_specs=[pl.BlockSpec((tile, width), lambda i, s: (i, 0))],
                out_specs=[pl.BlockSpec((tile, w), lambda i, s: (i, 0)) for w in widths],
            ),
            out_shape=[jax.ShapeDtypeStruct((rows, w), value.dtype) for w in widths],
            compiler_params=pltpu.CompilerParams(vmem_limit_bytes=VMEM),
            cost_estimate=pl.CostEstimate(
                flops=0, bytes_accessed=2 * rows * (width + sum(widths)), transcendentals=0
            ),
            name="pick_columns",
        )(places, value)
    )


def put_columns(values, block, groups):
    rows = values[0].shape[0]
    places = jnp.stack([jnp.asarray(g, jnp.int32) for group in groups for g in group])
    width = block * places.shape[0]
    if block % 128:
        flat = jnp.concatenate([v.astype(F32) for v in values], axis=1)
        blocks = flat.reshape(rows, width // block, block)
        return jnp.zeros_like(blocks).at[:, places].set(blocks).reshape(rows, width)
    tile = math.gcd(rows, 64)

    def kernel(places_ref, *refs):
        out_ref, at = refs[-1], 0
        for group, ref in zip(groups, refs[:-1]):
            for i in range(len(group)):
                start = pl.multiple_of(places_ref[at] * block, 128)
                part = ref[:, i * block : (i + 1) * block]
                out_ref[:, pl.ds(start, block)] = part.astype(F32)
                at += 1

    return pl.pallas_call(
        kernel,
        grid_spec=pltpu.PrefetchScalarGridSpec(
            num_scalar_prefetch=1,
            grid=(rows // tile,),
            in_specs=[pl.BlockSpec((tile, v.shape[1]), lambda i, s: (i, 0)) for v in values],
            out_specs=pl.BlockSpec((tile, width), lambda i, s: (i, 0)),
        ),
        out_shape=jax.ShapeDtypeStruct((rows, width), F32),
        compiler_params=pltpu.CompilerParams(vmem_limit_bytes=VMEM),
        cost_estimate=LIGHT,
        name="put_columns",
    )(places, *values)


def after(value, *others):
    return lax.optimization_barrier((value, others))[0]


class Line:
    def __init__(self):
        self.last = ()

    def take(self, value):
        value = lax.optimization_barrier((value, self.last))[0]
        self.last = value
        return value

    def run(self, fn, *inputs):
        inputs = lax.optimization_barrier((inputs, self.last))[0]
        out = fn(*inputs)
        self.last = out
        return out

    def light(self, fn, *inputs, flags=()):
        return self.run(lambda *v: light(fn, *v, flags=flags), *inputs)


def ordered_pair(bit, own, other):
    return jnp.concatenate([jnp.where(bit, other, own), jnp.where(bit, own, other)], axis=0)


def scatter_sum(wires, keep, order):
    for mask in order:
        half = keep.shape[0] // 2
        got = wires.swap(keep[half:].astype(BF16), mask)
        keep = keep[:half].astype(F32) + got.astype(F32)
    return keep


def team_blocks(wires, half):
    one, two = wires.team
    mine = wires.me & (one | two)
    return [
        [half * wires.shards + ((mine ^ t) | s) for s in wires.others()]
        for t in (0, one, two, one | two)
    ]


def turned(value):
    return pltpu.roll(value, HEAD_SIZE // 2, 1)


def head_forward(raw, gain, cosine, sine):
    scale = lax.rsqrt(jnp.mean(raw * raw, axis=1, keepdims=True) + EPS)
    normed = raw * scale
    v = normed * gain
    return (v * cosine + turned(v) * sine).astype(BF16), normed, scale


def head_back(grad, normed, scale, gain, cosine, sine):
    g = grad * cosine + turned(grad * sine)
    scaled = g * gain
    raw = scale * (scaled - normed * jnp.mean(scaled * normed, axis=1, keepdims=True))
    return raw, jnp.sum(g * normed, axis=0, keepdims=True)


def attend_group(sources, cosine, sine, bias, q_gain, k_gain):
    tokens = sources[0][0].shape[0]
    packs = tokens // PACK_CAPACITY
    width = (GROUPS + 2) * HEAD_SIZE
    counts = [len(pieces) for _, pieces, _ in sources]
    columns = [c for _, _, c in sources]
    n_in = len(sources) + sum(counts)

    def kernel(*refs):
        cos_ref, sin_ref, bias_ref, qg_ref, kg_ref, attn_ref, mixed_ref = refs[n_in:]
        at, to = 0, 0
        for count, (start, stop) in zip(counts, columns):
            x_ref, w_refs = refs[at], refs[at + 1 : at + 1 + count]
            at += 1 + count
            depth = w_refs[0].shape[0]
            part = jnp.zeros((tokens, stop - start), F32)
            for i, w_ref in enumerate(w_refs):
                part += jnp.dot(
                    x_ref[:, i * depth : (i + 1) * depth], w_ref[:, start:stop],
                    preferred_element_type=F32,
                )
            mixed_ref[:, to : to + stop - start] = part
            to += stop - start
        for p in range(packs):
            at = slice(p * PACK_CAPACITY, (p + 1) * PACK_CAPACITY)
            cosine, sine, bias = cos_ref[at], sin_ref[at], bias_ref[at]
            head = lambda j: mixed_ref[at, j * HEAD_SIZE : (j + 1) * HEAD_SIZE]
            key, _, _ = head_forward(head(GROUPS), kg_ref[...], cosine, sine)
            value = head(GROUPS + 1).astype(BF16)
            for j in range(GROUPS):
                query, _, _ = head_forward(head(j), qg_ref[...], cosine, sine)
                scores = against(query, key) * SCALE + bias
                expd = jnp.exp(scores - jnp.max(scores, axis=1, keepdims=True))
                probs = expd / jnp.sum(expd, axis=1, keepdims=True)
                attn = jnp.dot(probs.astype(BF16), value, preferred_element_type=F32)
                attn_ref[at, j * HEAD_SIZE : (j + 1) * HEAD_SIZE] = attn.astype(BF16)

    d = sources[0][0].shape[1]
    return pl.pallas_call(
        kernel,
        out_shape=[
            jax.ShapeDtypeStruct((tokens, GROUPS * HEAD_SIZE), BF16),
            jax.ShapeDtypeStruct((tokens, width), F32),
        ],
        compiler_params=pltpu.CompilerParams(vmem_limit_bytes=VMEM),
        cost_estimate=LIGHT,
        name="attend_group",
    )(
        *[v for x, pieces, _ in sources for v in (x, *pieces)],
        cosine, sine, bias, q_gain, k_gain,
    )


def attend_group_back(mixed, grad, cosine, sine, bias, q_gain, k_gain):
    tokens, width = mixed.shape
    packs = tokens // PACK_CAPACITY

    def kernel(mixed_ref, grad_ref, cos_ref, sin_ref, bias_ref, qg_ref, kg_ref, out_ref, gain_ref):
        q_gain, k_gain = qg_ref[...], kg_ref[...]
        q_sum = jnp.zeros((1, HEAD_SIZE), F32)
        k_sum = jnp.zeros((1, HEAD_SIZE), F32)
        for p in range(packs):
            at = slice(p * PACK_CAPACITY, (p + 1) * PACK_CAPACITY)
            cosine, sine, bias = cos_ref[at], sin_ref[at], bias_ref[at]
            head = lambda j: mixed_ref[at, j * HEAD_SIZE : (j + 1) * HEAD_SIZE]
            key, key_normed, key_scale = head_forward(head(GROUPS), k_gain, cosine, sine)
            value = head(GROUPS + 1).astype(BF16)
            grad_key = jnp.zeros((PACK_CAPACITY, HEAD_SIZE), F32)
            grad_value = jnp.zeros((PACK_CAPACITY, HEAD_SIZE), F32)
            for j in range(GROUPS):
                cols = slice(j * HEAD_SIZE, (j + 1) * HEAD_SIZE)
                query, normed, scale = head_forward(head(j), q_gain, cosine, sine)
                g = grad_ref[at, cols]
                scores = against(query, key) * SCALE + bias
                expd = jnp.exp(scores - jnp.max(scores, axis=1, keepdims=True))
                probs = expd / jnp.sum(expd, axis=1, keepdims=True)
                dprobs = against(g, value)
                inner = jnp.sum(probs * dprobs, axis=1, keepdims=True)
                grad_scores = (probs * (dprobs - inner)).astype(BF16)
                grad_query = jnp.dot(grad_scores, key, preferred_element_type=F32) * SCALE
                grad_key += through(grad_scores, query)
                grad_value += through(probs.astype(BF16), g)
                raw, gain = head_back(grad_query, normed, scale, q_gain, cosine, sine)
                out_ref[at, cols] = raw.astype(BF16)
                q_sum += gain
            raw, gain = head_back(grad_key * SCALE, key_normed, key_scale, k_gain, cosine, sine)
            k_sum += gain
            out_ref[at, GROUPS * HEAD_SIZE : (GROUPS + 1) * HEAD_SIZE] = raw.astype(BF16)
            out_ref[at, (GROUPS + 1) * HEAD_SIZE :] = grad_value.astype(BF16)
        gain_ref[...] = jnp.concatenate([q_sum, k_sum] + [jnp.zeros_like(q_sum)] * 6, axis=0)

    return pl.pallas_call(
        kernel,
        out_shape=[
            jax.ShapeDtypeStruct((tokens, width), BF16),
            jax.ShapeDtypeStruct((8, HEAD_SIZE), F32),
        ],
        compiler_params=pltpu.CompilerParams(vmem_limit_bytes=VMEM),
        cost_estimate=LIGHT,
        name="attend_group_back",
    )(mixed, grad, cosine, sine, bias, q_gain, k_gain)


def spread_back(grads, weights, groups, block, dtype, parts, by_rows=False):
    tokens = grads[0].shape[0]
    width = sum(w.shape[0] for w in weights[0])
    places = jnp.stack([jnp.asarray(g, jnp.int32) for group in groups for g in group])
    if block % 128:
        total = 0.0
        for grad, pieces, group in zip(grads, weights, groups):
            part = jnp.concatenate([against(grad, w) for w in pieces], axis=1)
            total = total + put_columns([part], block, [group])
        return jnp.split(total.astype(dtype), parts, axis=0 if by_rows else 1)
    flat = [w for pieces in weights for w in pieces]
    shape = (tokens // parts, width) if by_rows else (tokens, width // parts)

    def kernel(places_ref, *refs):
        grad_refs, refs = refs[: len(grads)], refs[len(grads) :]
        out_ref, at, k = refs[-1], 0, 0
        out_refs = refs[-1 - parts : -1]
        for gi, grad_ref in enumerate(grad_refs):
            for _ in weights[gi]:
                part = against(grad_ref[...], refs[k][...])
                for b in range(part.shape[1] // block):
                    start = pl.multiple_of(places_ref[at] * block, 128)
                    cols = pl.ds(start, block)
                    new = part[:, b * block : (b + 1) * block]
                    out_ref[:, cols] = new if gi == 0 else out_ref[:, cols] + new
                    at += 1
                k += 1
        for i, ref in enumerate(out_refs):
            size = ref.shape[0] if by_rows else ref.shape[1]
            part = slice(i * size, (i + 1) * size)
            ref[...] = (out_ref[part, :] if by_rows else out_ref[:, part]).astype(dtype)

    whole = lambda v: pl.BlockSpec(v.shape, lambda i, s: (0, 0))
    return pl.pallas_call(
        kernel,
        grid_spec=pltpu.PrefetchScalarGridSpec(
            num_scalar_prefetch=1,
            grid=(1,),
            in_specs=[whole(v) for v in grads] + [whole(w) for w in flat],
            out_specs=[pl.BlockSpec(shape, lambda i, s: (0, 0))] * parts,
            scratch_shapes=[pltpu.VMEM((tokens, width), F32)],
        ),
        out_shape=[jax.ShapeDtypeStruct(shape, dtype)] * parts,
        compiler_params=pltpu.CompilerParams(vmem_limit_bytes=VMEM),
        cost_estimate=LIGHT,
        name="spread_back",
    )(places, *grads, *flat)


def feed_forward(second, own, other, grad_low, down_own, down_other, core):
    rows, d = second[0].shape
    n = len(second)
    tokens = n * rows
    units = down_own.shape[0]
    tile, half = 384, d // 2

    def kernel(core_ref, *refs):
        x_refs, go_refs, gx_refs = refs[:n], refs[n : 2 * n], refs[2 * n : 3 * n]
        own_ref, other_ref, do_ref, dx_ref, hidden_ref, out_own_ref, out_other_ref = refs[3 * n :]
        first = core_ref[0] == 0
        for r in range(n):
            at = slice(r * rows, (r + 1) * rows)
            x = x_refs[r][...]
            a = jnp.dot(x, own_ref[...], preferred_element_type=F32)
            b = jnp.dot(x, other_ref[...], preferred_element_type=F32)
            gate, upward = jnp.where(first, a, b), jnp.where(first, b, a)
            sigma = jax.nn.sigmoid(gate)
            silu = gate * sigma
            hidden_ref[at, :] = (silu * upward).astype(BF16)
            grad = against(go_refs[r][...], do_ref[...]) + against(gx_refs[r][...], dx_ref[...])
            grad_gate = grad * upward * sigma * (1.0 + gate * (1.0 - sigma))
            grad_up = grad * silu
            out_own_ref[at, :] = jnp.where(first, grad_gate, grad_up).astype(BF16)
            out_other_ref[at, :] = jnp.where(first, grad_up, grad_gate).astype(BF16)

    once = pl.Buffered(1)
    in_specs = [pl.BlockSpec((rows, d), lambda j, s: (0, 0), pipeline_mode=once)] * n
    in_specs += [pl.BlockSpec((rows, half), lambda j, s: (0, s[0]), pipeline_mode=once)] * n
    in_specs += [pl.BlockSpec((rows, half), lambda j, s: (0, 1 - s[0]), pipeline_mode=once)] * n
    in_specs += [pl.BlockSpec((d, tile), lambda j, s: (0, j))] * 2
    in_specs += [pl.BlockSpec((tile, half), lambda j, s: (j, 0))] * 2
    return pl.pallas_call(
        kernel,
        grid_spec=pltpu.PrefetchScalarGridSpec(
            num_scalar_prefetch=1,
            grid=(units // tile,),
            in_specs=in_specs,
            out_specs=[pl.BlockSpec((tokens, tile), lambda j, s: (0, j))] * 3,
        ),
        out_shape=[jax.ShapeDtypeStruct((tokens, units), BF16)] * 3,
        compiler_params=pltpu.CompilerParams(vmem_limit_bytes=VMEM),
        cost_estimate=LIGHT,
        name="feed_forward",
    )(core.reshape(1), *second, *grad_low, *grad_low, own, other, down_own, down_other)


def feed_forward_back(grad_own, grad_other, own, other, places, block, n):
    tokens, units = grad_own.shape
    d = own.shape[0]
    rows = tokens // n
    if block % 128:
        part = against(grad_own, own) + against(grad_other, other)
        part = put_columns([part], block, [places]).astype(BF16)
        return [part[i * rows : (i + 1) * rows] for i in range(n)]
    width = 512

    def kernel(go_ref, gx_ref, own_ref, other_ref, *out_refs):
        for at in range(0, d, width):
            part = against(go_ref[...], own_ref[at : at + width, :])
            part += against(gx_ref[...], other_ref[at : at + width, :])
            part = part.astype(BF16)
            for b in range(width // block):
                to = places[at // block + b] * block
                for i in range(n):

                    @pl.when(pl.program_id(0) == (n - 1 - i) // 2)
                    def _(i=i, b=b, to=to):
                        row = (i % 2) * rows
                        out_refs[i][:, to : to + block] = part[
                            row : row + rows, b * block : (b + 1) * block
                        ]

    return pl.pallas_call(
        kernel,
        grid=(n // 2,),
        in_specs=[pl.BlockSpec((2 * rows, units), lambda i: (n // 2 - 1 - i, 0))] * 2
        + [pl.BlockSpec(own.shape, lambda i: (0, 0), pipeline_mode=pl.Buffered(1))] * 2,
        out_specs=[pl.BlockSpec((rows, d), lambda i: (0, 0))] * n,
        out_shape=[jax.ShapeDtypeStruct((rows, d), BF16)] * n,
        compiler_params=pltpu.CompilerParams(vmem_limit_bytes=VMEM),
        cost_estimate=LIGHT,
        name="feed_forward_back",
    )(grad_own, grad_other, own, other)


def weight_grad(lefts, tile, rights, column, width, added=None, split=False):
    units = lefts[0].shape[1]
    n, m = len(lefts), len(rights)
    steps = units // tile
    row_of = lambda vs, at: next(
        (i, at - sum(v.shape[0] for v in vs[:i]))
        for i in range(len(vs))
        if at < sum(v.shape[0] for v in vs[: i + 1])
    )
    tokens = sum(v.shape[0] for v in lefts)
    piece = min(v.shape[0] for v in [*lefts, *rights])

    def kernel(column_ref, *refs):
        left_refs, right_refs = refs[:n], refs[n : n + m]
        total = None
        for at in range(0, tokens, piece):
            (i, a), (j, b) = row_of(lefts, at), row_of(rights, at)
            part = through(left_refs[i][a : a + piece, :], right_refs[j][b : b + piece, :])
            total = part if total is None else total + part
        if added is not None:
            total += refs[n + m][...].astype(F32)
        if not split:
            refs[-1][...] = total.astype(BF16)
        else:

            @pl.when(pl.program_id(0) < steps // 2)
            def _():
                refs[-2][...] = total.astype(BF16)

            @pl.when(pl.program_id(0) >= steps // 2)
            def _():
                refs[-1][...] = total.astype(BF16)

    extra = [] if added is None else [added]
    once = pl.Buffered(1)
    half = steps // 2
    if split:
        out_specs = [
            pl.BlockSpec((tile, width), lambda i, s: (jnp.minimum(i, half - 1), 0)),
            pl.BlockSpec((tile, width), lambda i, s: (jnp.maximum(i - half, 0), 0)),
        ]
        out_shape = [jax.ShapeDtypeStruct((units // 2, width), BF16)] * 2
    else:
        out_specs = pl.BlockSpec((tile, width), lambda i, s: (i, 0))
        out_shape = jax.ShapeDtypeStruct((units, width), BF16)
    return pl.pallas_call(
        kernel,
        grid_spec=pltpu.PrefetchScalarGridSpec(
            num_scalar_prefetch=1,
            grid=(steps,),
            in_specs=[pl.BlockSpec((v.shape[0], tile), lambda i, s: (0, i)) for v in lefts]
            + [
                pl.BlockSpec((v.shape[0], width), lambda i, s: (0, s[0]), pipeline_mode=once)
                for v in rights
            ]
            + [pl.BlockSpec((tile, width), lambda i, s: (i, 0))] * len(extra),
            out_specs=out_specs,
        ),
        out_shape=out_shape,
        compiler_params=pltpu.CompilerParams(vmem_limit_bytes=VMEM),
        cost_estimate=LIGHT,
        name="weight_grad",
    )(jnp.asarray(column, jnp.int32).reshape(1), *lefts, *rights, *extra)


def down_project(hidden, own, other):
    tokens, units = hidden.shape
    half = own.shape[1]
    n = 4
    rows = tokens // n

    def kernel(hidden_ref, own_ref, other_ref, *out_refs):
        for r, out_ref in enumerate(out_refs):

            @pl.when(pl.program_id(0) == r)
            def _(out_ref=out_ref):
                for i, ref in enumerate((own_ref, other_ref)):
                    part = jnp.dot(hidden_ref[...], ref[...], preferred_element_type=F32)
                    out_ref[:, i * half : (i + 1) * half] = part.astype(BF16)

    once = pl.Buffered(1)
    return pl.pallas_call(
        kernel,
        grid=(n,),
        in_specs=[pl.BlockSpec((rows, units), lambda i: (i, 0))]
        + [pl.BlockSpec((units, half), lambda i: (0, 0), pipeline_mode=once)] * 2,
        out_specs=[pl.BlockSpec((rows, 2 * half), lambda i: (0, 0))] * n,
        out_shape=[jax.ShapeDtypeStruct((rows, 2 * half), BF16)] * n,
        compiler_params=pltpu.CompilerParams(vmem_limit_bytes=VMEM),
        cost_estimate=LIGHT,
        name="down_project",
    )(hidden, own, other)


def light(fn, *args, flags=()):
    flat, tree = jax.tree.flatten(args)
    n = len(flags)
    shapes = jax.eval_shape(lambda *v: fn(*[jnp.bool_(True)] * n, *v), *args)
    out_flat, out_tree = jax.tree.flatten(shapes)

    def kernel(*refs):
        flag_ref, refs = refs[0], refs[1:]
        values = jax.tree.unflatten(tree, [r[...] for r in refs[: len(flat)]])
        out = fn(*[flag_ref[i] != 0 for i in range(n)], *values)
        for ref, value in zip(refs[len(flat) :], jax.tree.leaves(out)):
            ref[...] = value

    bits = jnp.stack([jnp.asarray(f, jnp.int32) for f in (*flags, True)])
    whole = lambda v: pl.BlockSpec(v.shape, lambda i, s, r=len(v.shape): (0,) * r)
    out = pl.pallas_call(
        kernel,
        grid_spec=pltpu.PrefetchScalarGridSpec(
            num_scalar_prefetch=1,
            grid=(1,),
            in_specs=[whole(v) for v in flat],
            out_specs=[whole(v) for v in out_flat],
        ),
        out_shape=[jax.ShapeDtypeStruct(v.shape, v.dtype) for v in out_flat],
        compiler_params=pltpu.CompilerParams(vmem_limit_bytes=VMEM),
        cost_estimate=LIGHT,
        name="light",
    )(bits, *flat)
    return jax.tree.unflatten(out_tree, out)


def tables(lengths):
    segids, cosine, sine, live = pack_layout(lengths)
    slots = jnp.arange(PACK_CAPACITY, dtype=jnp.int32)
    allowed = (segids[:, None] == segids[None, :]) & (slots[:, None] >= slots[None, :])
    half = HEAD_SIZE // 2
    sine = jnp.concatenate([-sine[:, :half], sine[:, half:]], axis=1)
    return cosine, sine, jnp.where(allowed, 0.0, MASKED).astype(F32), live


def on_device(
    shards,
    copies,
    tokens,
    seq_lengths,
    in_gain,
    q_gain,
    key_norm_gain,
    post_gain,
    w_qkv,
    w_out,
    w_gate_up,
    w_down,
    cotangent,
):
    wires = Wires(shards, copies)
    me, core, top = wires.me, wires.core, wires.top
    first_core = core == 0
    rows = w_qkv.shape[0]
    d = in_gain.shape[0]
    half = d // 2
    by_core = lambda own, other: (jnp.where(first_core, own, other), jnp.where(first_core, other, own))
    ordered = lambda own, other: jnp.concatenate(by_core(own, other), axis=-1)
    dot = lambda a, b: jnp.dot(a, b, preferred_element_type=F32)
    through_low = lambda a, b: through(a, b).astype(BF16)
    both_packs = lambda v: jnp.concatenate([v, wires.swap_core(v)], axis=0)

    per_core = KEY_VALUE_HEADS // 2
    one, two = wires.team
    x, y, z = 1, 2, 4
    line = Line()
    stack = lambda *parts: jnp.concatenate(parts, axis=0)
    swap, swap_core = wires.swap, wires.swap_core
    low = lambda v: v.astype(BF16)
    wide = lambda v: v.astype(F32)

    def halves(v):
        n = v.shape[0] // 2
        return v[:n], v[n:]

    def head_blocks(core):
        return [
            [GROUPS * (per_core * core + g) + j for j in range(GROUPS)]
            + [QUERY_HEADS + per_core * core + g, QUERY_HEADS + KEY_VALUE_HEADS + per_core * core + g]
            for g in range(per_core)
        ]

    def parcels(core):
        by = head_blocks(core)
        return [by[0] + by[3][:GROUPS], by[1] + by[3][GROUPS:], by[2]]

    qkv_orders = [wires.far + o for o in ([z, x, y], [y, z, x], [x, y, z])]
    widths = [len(p) * HEAD_SIZE for p in parcels(core)]
    starts = [sum(widths[:i]) for i in range(len(widths))]

    lengths_got = swap_core(seq_lengths.astype(F32))
    gu_parts = line.run(
        lambda w: pick_columns(w, FF // shards, team_blocks(wires, core)), w_gate_up
    )
    gu_got = [swap(p, t) for p, t in zip(gu_parts[1:], (one, two, one | two))]
    (qkv_rows,) = line.run(
        lambda w: pick_columns(w, HEAD_SIZE, [sum(parcels(core), [])]), w_qkv
    )
    qkv_got = swap(qkv_rows, wires.far[0])
    lengths_got = line.take(lengths_got)
    row = lambda v: v.reshape(1, -1)
    first_own = line.light(
        lambda v, g: low(normalized_rows(wide(v), g)[0]), tokens, row(in_gain)
    )
    first_other = swap_core(first_own)
    at_home = wires.has(top) == (core == 1)
    away_to = lambda s, c: (s ^ top, c) if (s & top != 0) == (c == 1) else None
    cosine, sine, bias, live = tables(seq_lengths[0])
    lengths_other = lengths_got[0].astype(jnp.int32)
    packs = [
        jnp.concatenate(pair, axis=0)
        for pair in zip((cosine, sine, bias), tables(lengths_other)[:3])
    ]
    gains = [q_gain.reshape(1, -1), key_norm_gain.reshape(1, -1)]
    live = live[:, None].astype(F32)
    packs, live = line.run(lambda *v: v, packs, live)
    grad_low = line.light(lambda v, k: low(wide(v) * k), cotangent, live)
    (down_half,) = line.run(lambda w: pick_columns(w, half, [[core]]), w_down)
    gu_got, qkv_got, first_other = line.take((gu_got, qkv_got, first_other))

    def team_rows(has_one, has_two, own, by_one, by_two, by_both):
        near = ordered_pair(has_one, own, by_one)
        return ordered_pair(has_two, near, ordered_pair(has_one, by_two, by_both))

    team_flags = (wires.has(one), wires.has(two))
    for mask in wires.far:
        got = qkv_got if mask == wires.far[0] else line.take(swap(qkv_rows, mask))
        qkv_rows = line.light(stack, qkv_rows, got)
    legs = line.light(lambda v: [v[:, at : at + w] for at, w in zip(starts, widths)], qkv_rows)
    leg = len(wires.far)
    got = [swap(v, o[leg]) for v, o in zip(legs, qkv_orders)]
    away = wires.send(w_out, away_to)
    down_y = swap(line.take(down_half), y)
    gu_rows = line.light(
        lambda *v: halves(team_rows(*v)), gu_parts[0], *gu_got, flags=team_flags
    )
    gu_a, gu_b = gu_rows

    def spread_far(v):
        out = [v]
        for mask in wires.far:
            out = out + [swap(p, mask) for p in out]
        return out

    block_places = [[me ^ m for m in masks_of(order[::-1])] for order in qkv_orders]
    first_low = line.light(stack, first_own, first_other)
    first_moved = line.run(lambda v: pick_columns(v, rows, block_places), first_low)
    join = lambda a, b: [stack(v, g) for v, g in zip(a, b)]
    legs = line.light(join, legs, line.take(got))
    got = [swap(v, o[leg + 1]) for v, o in zip(legs, qkv_orders)]
    gu_a = spread_far(gu_a)
    got, away, down_y = line.take((got, away, down_y))
    legs = line.light(join, legs, got)
    got = [swap(v, o[leg + 2]) for v, o in zip(legs, qkv_orders)]
    out_legs = line.light(
        lambda home, v, w: jnp.where(home, w, v), away, w_out, flags=(at_home,)
    )
    got, gu_a = line.take((got, gu_a))
    qkv = [[v, g] for v, g in zip(legs, got)]

    out_masks = [m for m in wires.far if m != top]
    out_orders = [out_masks + o for o in ([z, x, y], [z, y, x])]
    for mask in out_masks:
        out_legs = line.light(stack, out_legs, line.take(swap(out_legs, mask)))
    out_legs, grad_low = line.take((out_legs, grad_low))
    got = swap(out_legs, z)
    grad_low_one = swap(grad_low, one)
    grad_low_two = swap(grad_low, two)
    gu_a_y = [swap(gu_a[0], y)]
    gu_b = spread_far(line.take(gu_b))
    attn, mixed = [], []

    def attend(g):
        if g < 3:
            sources = [(first_moved[g], qkv[g], (0, (GROUPS + 2) * HEAD_SIZE))]
        else:
            at = (GROUPS + 2) * HEAD_SIZE
            sources = [
                (first_moved[i], qkv[i], (at, at + GROUPS * HEAD_SIZE)) for i in range(2)
            ]
        out = line.run(
            lambda cosine: attend_group(sources, cosine, *packs[1:], *gains), packs[0]
        )
        attn.append(out[0])
        mixed.append(out[1])

    attend(0)
    attend(1)
    got, grad_low_one, gu_a_y[0] = line.take((got, grad_low_one, gu_a_y[0]))
    out_legs = line.light(
        lambda v, g: [stack(v, g)[:, i * half : (i + 1) * half] for i in range(2)], out_legs, got
    )
    got = [swap(v, o[-2]) for v, o in zip(out_legs, out_orders)]
    gu_b_y = [swap(line.take(gu_b[0]), y)]
    attend(2)
    attend(3)
    gu_b = line.take(gu_b)
    down_far = spread_far(line.take(down_half))
    got, grad_low_two, gu_b_y[0] = line.take((got, grad_low_two, gu_b_y[0]))
    out_legs = line.light(join, out_legs, got)
    got = [swap(v, o[-1]) for v, o in zip(out_legs, out_orders)]
    gu_a_y = gu_a_y + [swap(v, y) for v in line.take(gu_a[1:])]
    grad_low_both = swap(line.take(grad_low_one), two)
    below = top - 1
    out_places = [[(me & below) ^ m for m in masks_of(o[::-1])] for o in out_orders]
    attn = line.light(lambda *v: jnp.concatenate(v, axis=1), *attn)
    attn_moved = line.run(lambda v: pick_columns(v, rows, out_places), attn)
    got, grad_low_both, down_far = line.take((got, grad_low_both, down_far))
    out_w = [[v, g] for v, g in zip(out_legs, got)]

    def project_out(moved, weights):
        parts = []
        for v, w in zip(moved, weights):
            depth = w[0].shape[0]
            parts.append(sum(dot(v[:, i * depth : (i + 1) * depth], p) for i, p in enumerate(w)))
        part = jnp.concatenate(parts, axis=1)
        return part[:PACK_CAPACITY], low(part[PACK_CAPACITY:])

    out_part, out_send = line.light(project_out, attn_moved, out_w)
    out_got = line.take(swap_core(out_send))
    columns = [f | t for f in wires.sharers()[0] for t in (0, one, two, one | two)]

    def to_second(v, part, got, gain):
        middle = wide(v) + (part + wide(got))
        second = low(normalized_rows(middle, gain)[0])
        return middle, jnp.concatenate([second[:, c * rows : (c + 1) * rows] for c in columns], axis=1)

    middle, second_low = line.light(to_second, tokens, out_part, out_got, row(post_gain))

    second_two = swap(second_low, two)
    second_one = swap(second_low, one)
    gu_b_y = gu_b_y + [swap(v, y) for v in gu_b[1:]]
    down_far_y = [down_y] + [swap(v, y) for v in down_far[1:]]
    gu_a_y, gu_b_y, second_two = line.take((gu_a_y, gu_b_y, second_two))
    second_both = swap(second_two, one)
    second_one, second_both, down_far_y = line.take((second_one, second_both, down_far_y))
    order_flags = [wires.has(y)] + [wires.has(mask) for mask in wires.far]

    def in_order(*v):
        flags, (near, by_y) = v[: len(order_flags)], v[len(order_flags) :]
        rows_of = [ordered_pair(flags[0], a, b) for a, b in zip(near, by_y)]
        for flag in flags[1:]:
            rows_of = [ordered_pair(flag, a, b) for a, b in zip(rows_of[::2], rows_of[1::2])]
        return rows_of[0]

    gu_own = line.light(
        lambda *v: in_order(
            *v[: len(order_flags)],
            *[
                [jnp.concatenate(pair, axis=0) for pair in zip(a, b)]
                for a, b in (v[-4:-2], v[-2:])
            ],
        ),
        gu_a, gu_b, gu_a_y, gu_b_y, flags=order_flags,
    )
    gu_other = swap_core(gu_own)
    down_own = line.light(in_order, down_far, down_far_y, flags=order_flags)
    down_other = swap_core(down_own)
    gu_other, down_other = line.take((gu_other, down_other))

    second_team = [second_low, second_two, second_one, second_both]
    grad_low_team = [grad_low, grad_low_two, grad_low_one, grad_low_both]
    hidden_low, grad_own, grad_other = line.run(
        lambda v, g: feed_forward(v, gu_own, gu_other, g, down_own, down_other, core),
        second_team, grad_low_team,
    )
    def down_blocks(has_y, v):
        n = v.shape[0] // (shards // 4)
        by = [v[i * n : (i + 1) * n] for i in range(shards // 4)]
        low_y, high_y = jnp.concatenate(by[::2], axis=0), jnp.concatenate(by[1::2], axis=0)
        return jnp.where(has_y, high_y, low_y), jnp.where(has_y, low_y, high_y)

    def far_blocks(has_far, mine, got):
        one_half, other_half = halves(wide(mine) + wide(got))
        return (
            jnp.where(has_far, other_half, one_half),
            low(jnp.where(has_far, one_half, other_half)),
        )

    units = hidden_low.shape[1]
    gu_sent = swap_core(
        line.run(lambda g: weight_grad(second_team, 512, [g], 0, units), grad_other)
    )
    down_sent = swap_core(
        line.run(lambda h: weight_grad([h], 384, grad_low_team, 1 - core, half), hidden_low)
    )
    share_own, share_two, share_one, share_both = line.run(
        lambda a, b: feed_forward_back(a, b, gu_own, gu_other, columns, rows, 4),
        grad_own, grad_other,
    )
    got_two = swap(share_both, one)

    gu_sent, down_sent = line.take((gu_sent, down_sent))
    gu_keep = line.run(
        lambda g, sent: weight_grad(second_team, 512, [g], 0, units, sent), grad_own, gu_sent
    )
    gu_keep = line.light(
        lambda has_y, v: down_blocks(has_y, v), gu_keep, flags=(wires.has(y),)
    )
    gu_got = swap(gu_keep[1], y)
    got_two = line.take(got_two)
    got_last = swap(line.light(lambda a, b: low(wide(a) + wide(b)), share_two, got_two), two)
    got_own = swap(line.take(share_one), one)
    down_keep = line.run(
        lambda h, sent: weight_grad([h], 384, grad_low_team, core, half, sent), hidden_low, down_sent
    )
    down_keep = line.light(
        lambda has_y, v: down_blocks(has_y, v), down_keep, flags=(wires.has(y),)
    )
    down_got = swap(down_keep[1], y)
    part_own, part_two, part_one, part_both = line.run(
        lambda h: down_project(h, down_own, down_other), hidden_low
    )
    got_own, got_last = line.take((got_own, got_last))

    def norm_gradient(parts, v, gain):
        _, normed, scale = normalized_rows(v, gain)
        grad = sum(wide(p) for p in parts)
        scaled = grad * gain
        mean = jnp.mean(scaled * normed, axis=-1, keepdims=True)
        return scale * (scaled - normed * mean), jnp.sum(grad * normed, axis=0, keepdims=True)

    def to_middle(parts, v, gain, cotangent, live):
        norm_part, gain_part = norm_gradient(parts, v, gain)
        grad = wide(cotangent) * live + norm_part
        return grad, low(grad), gain_part

    grad_middle, grad_middle_own, post_gain_grad = line.light(
        to_middle, (share_own, got_own, got_last), middle, row(post_gain), cotangent, live
    )
    grad_middle_other = swap_core(grad_middle_own)
    part_got_two = swap(line.take(part_both), one)
    grad_middle_low, *out_cols = line.light(
        lambda a, b: (stack(a, b), stack(a, b)[:, :half], stack(a, b)[:, half:]),
        grad_middle_own, line.take(grad_middle_other),
    )
    grad_attn = line.run(
        lambda *cols: spread_back(cols, out_w, out_places, rows, BF16, per_core), *out_cols
    )
    n_out = attn_moved[0].shape[1]
    out_back = [x, z, y] + out_masks[::-1]
    attn_back = line.run(
        lambda v: pick_columns(v, rows, [[(me & below) ^ m for m in masks_of(out_back)]])[0], attn
    )
    grad_mixed, gain_grads = {}, []

    def attend_back(g):
        got = line.run(
            lambda v: attend_group_back(
                mixed[g],
                v[g],
                *packs,
                *gains,
            ),
            grad_attn,
        )
        grad_mixed[g] = got[0]
        gain_grads.append(got[1])

    q_width = GROUPS * HEAD_SIZE
    qkv_back = [o[::-1] for o in qkv_orders]

    def next_step(keep, got):
        mine, away = halves(wide(keep) + wide(got))
        return mine, low(away)

    def far_step(keep, got):
        for mask in wires.far[::-1]:
            keep, away = line.light(far_blocks, keep, got, flags=(wires.has(mask),))
            got = swap(away, mask)
            if mask != wires.far[0]:
                got = line.take(got)
        return keep, got

    def parcel_back(g, *extra):
        parcel = grad_mixed[g]
        if extra:
            parcel = line.light(lambda *v: jnp.concatenate(v, axis=1), parcel, *extra)
        keep = line.run(
            lambda v, p: weight_grad([v], 512, [p], 0, p.shape[1], split=True),
            first_moved[g], parcel,
        )
        return parcel, keep, swap(keep[1], qkv_back[g][0])

    def add_step(keep, got, mask):
        keep = line.light(next_step, keep[0], line.take(got))
        return keep, swap(keep[1], mask)

    attend_back(3)
    last_q, last_kv = line.light(lambda v: (v[:, :q_width], v[:, q_width:]), grad_mixed[3])
    attend_back(1)
    part_got_two = line.take(part_got_two)
    part_got_last = swap(line.light(lambda a, b: low(wide(a) + wide(b)), part_two, part_got_two), two)
    part_got_own = swap(line.take(part_one), one)
    parcels_back = {1: parcel_back(1, last_kv)}
    attend_back(2)
    parcels_back[2] = parcel_back(2)
    out_keep = line.run(
        lambda v: weight_grad([v], n_out // 4, [grad_middle_low], 0, d, split=True), attn_back
    )
    out_got = swap(out_keep[1], out_back[0])
    attend_back(0)
    part_got_own, part_got_last = line.take((part_got_own, part_got_last))

    def to_result(own_first, m, parts):
        total = sum(wide(v) for v in parts)
        a, b = total[:, :half], total[:, half:]
        columns = [jnp.where(own_first, a, b), jnp.where(own_first, b, a)]
        return low(m + jnp.concatenate(columns, axis=1))

    result = line.light(
        to_result, middle, (part_own, part_got_own, part_got_last), flags=(first_core,)
    )
    gu_got, down_got = line.take((gu_got, down_got))
    gu_mine, gu_far_got = far_step(gu_keep[0], gu_got)
    parcels_back[0] = parcel_back(0, last_q)
    grad_parcels = [parcels_back[g][0] for g in range(3)]
    keeps = [parcels_back[g][1] for g in range(3)]
    gots = [parcels_back[g][2] for g in range(3)]
    keeps[1], gots[1] = add_step(keeps[1], gots[1], qkv_back[1][1])
    keeps[2], gots[2] = add_step(keeps[2], gots[2], qkv_back[2][1])
    grad_first_part = line.run(
        lambda *g: spread_back(g, qkv, block_places, rows, BF16, 2, True), *grad_parcels
    )
    keeps[0], gots[0] = add_step(keeps[0], gots[0], qkv_back[0][1])
    keeps[1], gots[1] = add_step(keeps[1], gots[1], qkv_back[1][2])
    keeps[2], gots[2] = add_step(keeps[2], gots[2], qkv_back[2][2])
    out_keep, out_got = add_step(out_keep, out_got, out_back[1])
    gu_far_got = line.take(gu_far_got)
    gu_half = line.light(lambda a, b: low(a + wide(b)), gu_mine, gu_far_got)
    down_mine, down_got = far_step(down_keep[0], down_got)
    first_got = line.take(swap_core(grad_first_part[1]))

    def to_tokens(parts, v, gain, grad):
        norm_part, gain_part = norm_gradient(parts, wide(v), gain)
        return low(grad + norm_part), gain_part

    grad_tokens, in_gain_grad = line.light(
        to_tokens, (grad_first_part[0], first_got), tokens, row(in_gain), grad_middle
    )
    sums = jnp.concatenate(
        [
            in_gain_grad.reshape(-1, HEAD_SIZE),
            post_gain_grad.reshape(-1, HEAD_SIZE),
            sum(gain_grads),
        ]
    )
    keeps[0], gots[0] = add_step(keeps[0], gots[0], qkv_back[0][2])
    sums = sums + line.take(swap_core(sums))
    out_keep, out_got = add_step(out_keep, out_got, out_back[2])
    keeps = line.light(
        lambda a, b: [wide(k[0]) + wide(g) for k, g in zip(a, b)], keeps, line.take(gots)
    )
    cut = lambda v: (halves(v)[0], low(halves(v)[1]))
    mine, away = line.light(lambda *v: cut(jnp.concatenate(v, axis=1)), *keeps)
    for mask in wires.far[::-1]:
        last_got = swap(away, mask)
        if mask != wires.far[0]:
            mine, away = line.light(lambda a, b: cut(a + wide(b)), mine, line.take(last_got))
    def return_rows(has_one, has_two, v):
        by = [v[i * rows : (i + 1) * rows] for i in range(4)]
        near = [jnp.where(has_two, by[i + 2], by[i]) for i in range(2)]
        away = [jnp.where(has_two, by[i], by[i + 2]) for i in range(2)]
        pick = lambda pair: [
            jnp.where(has_one, pair[1], pair[0]), jnp.where(has_one, pair[0], pair[1])
        ]
        return pick(near) + pick(away)

    gu_back = line.light(return_rows, gu_half, flags=team_flags)
    gu_back[1:] = [swap(b, t) for b, t in zip(gu_back[1:], (one, two, one | two))]
    sums_got = swap(line.take(sums), wires.masks[0])
    down_got = line.take(down_got)
    down_done = line.light(lambda a, b: low(a + wide(b)), down_mine, down_got)
    down_sibling = swap_core(down_done)
    gu_back[1:] = line.take(gu_back[1:])
    gu_sibling = swap_core(line.light(lambda *v: jnp.concatenate(v, axis=1), *gu_back))
    out_got = line.take(out_got)
    out_done = line.light(lambda a, b: wide(a) + wide(b), out_keep[0], out_got)
    out_done = scatter_sum(wires, out_done, out_back[3:])
    out_away = line.light(low, out_done)
    back_to = lambda s, c: (s ^ top, c) if (s & top != 0) != (c == 1) else None
    out_got = wires.send(out_away, back_to)
    sums = sums + line.take(sums_got)
    sums_got = swap(sums, wires.masks[1])
    last_got, down_sibling, gu_sibling = line.take((last_got, down_sibling, gu_sibling))
    qkv_done = line.light(lambda a, b: low(a + wide(b)), mine, last_got)
    qkv_sibling = swap_core(qkv_done)
    sums = sums + line.take(sums_got)
    sums_got = swap(sums, wires.masks[2])
    gu_out = line.run(
        lambda *v: put_columns(
            list(v),
            FF // shards,
            team_blocks(wires, core) + [sum(team_blocks(wires, 1 - core), [])],
        ),
        *gu_back, gu_sibling,
    )
    out_low = line.light(lambda a, b: low(a + wide(b)), out_done, line.take(out_got))
    out_sibling = wires.send(
        out_low, lambda s, c: (s, 1 - c) if (s & top != 0) == (c == 1) else None
    )
    sums = sums + line.take(sums_got)
    sums_got = swap(sums, wires.masks[3])
    down_out = line.run(
        lambda a, b: put_columns([a, b], half, [[core], [1 - core]]), down_done, down_sibling
    )
    qkv_out = line.run(
        lambda a, b: put_columns(
            [a, b], HEAD_SIZE, [sum(parcels(core), []), sum(parcels(1 - core), [])]
        ),
        qkv_done, line.take(qkv_sibling),
    )
    out_done = line.light(
        lambda home, a, b: wide(jnp.where(home, a, b)),
        out_low, line.take(out_sibling), flags=(at_home,),
    )
    sums = sums + line.take(sums_got)
    for mask in wires.masks[4:]:
        sums = sums + line.take(swap(sums, mask))
    lanes = d // HEAD_SIZE

    return (
        result,
        grad_tokens,
        sums[:lanes].reshape(-1),
        sums[2 * lanes],
        sums[2 * lanes + 1],
        sums[lanes : 2 * lanes].reshape(-1),
        qkv_out,
        out_done,
        gu_out,
        down_out,
    )


def solution(mesh):
    shards, copies = mesh.shape["shard"], mesh.shape["replica"]
    body = lambda *args: on_device(shards, copies, *args)
    in_specs = (
        P(("shard", "replica"), None),
        P(("shard", "replica"), None),
        P(),
        P(),
        P(),
        P(),
        P("shard", None),
        P("shard", None),
        P("shard", None),
        P("shard", None),
        P(("shard", "replica"), None),
    )
    out_specs = (
        P(("shard", "replica"), None),
        P(("shard", "replica"), None),
        P(),
        P(),
        P(),
        P(),
        P("shard", None),
        P("shard", None),
        P("shard", None),
        P("shard", None),
    )
    return jax.shard_map(
        body, mesh=mesh, in_specs=in_specs, out_specs=out_specs, check_vma=False
    )
```

time: 1030 us -> 826 us (0.80)
  waiting for transfers between devices: 543 us -> 287 us
  Pallas kernels: 182 us -> 410 us
  other arithmetic: 91.6 us -> 11.5 us
  matrix products: 56.4 us -> 0 us
  local copies, waits for them, and re-layouts: 52.2 us -> 24.6 us
  starting transfers between devices: 99.3 us -> 84.6 us
    ppermute x97 -> x79, waiting for transfers between devices: 543 us -> 287 us  [send(): return lax.ppermute(value, AXES, pairs)]
    pallas_call x1 -> x58, Pallas kernels: 21.7 us -> 265 us  [the longest x48 166 us: light(): pl.pallas_call(kernel, grid_spec=pltpu.PrefetchScalarGridSpec(num_scalar_...]
    dot_general x15 -> x0, matrix products: 56.4 us -> none  [the longest x9 35.4 us: through(): lax.dot_general(left, grad, (((0,), (0,)), ((), ())), preferred_element_t...]
    add x25 -> x6, other arithmetic: 31.4 us -> 0.03 us  [the longest x4 0.02 us: on_device(): sums = sums + line.take(sums_got)]
    concatenate x11 -> x0, other arithmetic: 19.7 us -> none  [the longest x1 3.73 us: on_device(): jnp.concatenate(gather_team(wires, grad_out.astype(BF16)), axis=0)]
    pallas_call x9 -> x6, Pallas kernels: 39.1 us -> 22 us  [pick_columns(): pl.pallas_call(kernel, grid_spec=pltpu.PrefetchScalarGridSpec(num_scalar_...]
    convert_element_type x16 -> x2, other arithmetic: 18.2 us -> 1.33 us  [the longest x1 1.32 us: on_device(): live = live[:, None].astype(F32)]
    slice x27 -> x0, local copies, waits for them, and re-layouts: 15 us -> none  [the longest x23 10 us: scatter_sum(): got = wires.swap(keep[half:].astype(BF16), mask)]
  transfers between devices with their start and end apart: 97 -> 79, of which waited for: 44 -> 28; matrix products, arithmetic and copies ran while one was open for 18% -> 2% of each run, Pallas kernels for 11% -> 40%
where the time goes in v2:
time: 826 us; the launch traced here: 819 us
  Pallas kernels  410 us (50%)
  waiting for transfers between devices  287 us (35%)
  starting transfers between devices  84.6 us (10%)
  local copies, waits for them, and re-layouts  24.6 us (3%)
  other arithmetic  11.5 us (1%)
    ppermute x79, waiting for transfers between devices, send(): return lax.ppermute(value, AXES, pairs)  287 us
    pallas_call x48, Pallas kernels, light(): pl.pallas_call(kernel, grid_spec=pltpu.PrefetchScalarGridSpec(num_scalar_...  166 us
    ppermute x79, starting transfers between devices, send(): return lax.ppermute(value, AXES, pairs)  84.6 us
    pallas_call x8, Pallas kernels, weight_grad(): pl.pallas_call(kernel, grid_spec=pltpu.PrefetchScalarGridSpec(num_scalar_...  62.8 us
    pallas_call x1, Pallas kernels, feed_forward(): pl.pallas_call(kernel, grid_spec=pltpu.PrefetchScalarGridSpec(num_scalar_...  35.5 us
    pallas_call x4, Pallas kernels, attend_group(): pl.pallas_call(kernel, out_shape=[jax.ShapeDtypeStruct((tokens, GROUPS *...  28.2 us
    pallas_call x4, Pallas kernels, attend_group_back(): pl.pallas_call(kernel, out_shape=[jax.ShapeDtypeStruct((tokens, width), B...  25.5 us
    pallas_call x1, Pallas kernels, feed_forward_back(): pl.pallas_call(kernel, grid=(n // 2,), in_specs=[pl.BlockSpec((2 * rows,...  23.2 us
  transfers between devices with their start and end apart: 79, of which 28 were waited for; matrix products, arithmetic and copies ran while one was open for 2% of the time, Pallas kernels for 40%

profile of v2, /device:TPU:0, one launch (start us, length us, event | category | flops | bytes accessed | tf_op | source)
XLA Modules:
  0.0 819.3 jit_solution(15522974802884087022)
XLA Ops:
  33.2 7.5 collective-permute-done.3.refs_4_
  59.3 5.6 pick_columns.9
  75.8 15.3 %collective-permute-done.12.refs_1_ = bf16[128,2048]{1,0:T(8,128)(2,1)S(1)} collective-permute-done((bf16[128,2048]{1,0:T(8,128)(2,1)S(1)}, bf16[128,2048]{1,0:T(8,128)(2,1)S(1)}, u32[]{:S(2)}, u32[]{:S(2)}) %collective-permute-start.12) | collective-permute-done | bytes 524320 | tf_op jit(solution)/shard_map/ppermute | solution.py:87
  106.0 32.2 %collective-permute-done.17.refs_2_ = bf16[256,1536]{1,0:T(8,128)(2,1)} collective-permute-done((bf16[256,1536]{1,0:T(8,128)(2,1)}, bf16[256,1536]{1,0:T(8,128)(2,1)}, u32[]{:S(2)}, u32[]{:S(2)}) %collective-permute-start.17) | collective-permute-done | bytes 786464 | tf_op jit(solution)/shard_map/ppermute | solution.py:87
  147.9 6.7 attend_group.4
  154.7 6.8 attend_group.5
  161.4 15.8 %collective-permute-done.18.refs_2_ = bf16[128,2048]{1,0:T(8,128)(2,1)S(1)} collective-permute-done((bf16[128,2048]{1,0:T(8,128)(2,1)}, bf16[128,2048]{1,0:T(8,128)(2,1)S(1)}, u32[]{:S(2)}, u32[]{:S(2)}) %collective-permute-start.18) | collective-permute-done | bytes 524320 | tf_op jit(solution)/shard_map/ppermute | solution.py:87
  183.4 6.5 attend_group.6
  189.9 8.3 %attend_group.7 = (bf16[512,256]{1,0:T(8,128)(2,1)}, f32[512,512]{1,0:T(8,128)}) custom-call(bf16[512,2048]{1,0:T(8,128)(2,1)} %get-tuple-element.671.refs_0_, bf16[1024,768]{1,0:T(8,128)(2,1)} %get-tuple-element.465.refs_1_.refs_3_, bf16[1024,768]{1,0:T(8,128)(2,1)} %copy-done.4, bf16[512,2048]{1,0:T(8,128)(2,1)} %get-tuple-element.640.refs_0_.refs_3_, ...), custom_call_target="tpu_custom_call" | custom-call | flops 1 | bytes 1 | tf_op jit(solution)/shard_map/attend_group/pallas_call | solution.py:297
  198.2 9.1 %collective-permute-done.22.refs_4_ = bf16[256,1024]{1,0:T(8,128)(2,1)} collective-permute-done((bf16[256,1024]{1,0:T(8,128)(2,1)}, bf16[256,1024]{1,0:T(8,128)(2,1)}, u32[]{:S(2)}, u32[]{:S(2)}) %collective-permute-start.22) | collective-permute-done | bytes 524320 | tf_op jit(solution)/shard_map/ppermute | solution.py:87
  221.3 23.8 %collective-permute-done.29.refs_2_ = bf16[384,1024]{1,0:T(8,128)(2,1)} collective-permute-done((bf16[384,1024]{1,0:T(8,128)(2,1)}, bf16[384,1024]{1,0:T(8,128)(2,1)}, u32[]{:S(2)}, u32[]{:S(2)}) %collective-permute-start.29) | collective-permute-done | bytes 786464 | tf_op jit(solution)/shard_map/ppermute | solution.py:87
  247.2 7.1 light.60
  267.9 17.5 %collective-permute-done.32.refs_8_ = bf16[256,1536]{1,0:T(8,128)(2,1)S(1)} collective-permute-done((bf16[256,1536]{1,0:T(8,128)(2,1)}, bf16[256,1536]{1,0:T(8,128)(2,1)S(1)}, u32[]{:S(2)}, u32[]{:S(2)}) %collective-permute-start.32) | collective-permute-done | bytes 786464 | tf_op jit(solution)/shard_map/ppermute | solution.py:87
  285.4 16.0 %collective-permute-done.31.refs_6_ = bf16[256,1536]{1,0:T(8,128)(2,1)S(1)} collective-permute-done((bf16[256,1536]{1,0:T(8,128)(2,1)}, bf16[256,1536]{1,0:T(8,128)(2,1)S(1)}, u32[]{:S(2)}, u32[]{:S(2)}) %collective-permute-start.31) | collective-permute-done | bytes 786464 | tf_op jit(solution)/shard_map/ppermute | solution.py:87
  305.5 16.6 %collective-permute-done.36.refs_4_ = bf16[384,1024]{1,0:T(8,128)(2,1)} collective-permute-done((bf16[384,1024]{1,0:T(8,128)(2,1)}, bf16[384,1024]{1,0:T(8,128)(2,1)}, u32[]{:S(2)}, u32[]{:S(2)}) %collective-permute-start.36) | collective-permute-done | bytes 786464 | tf_op jit(solution)/shard_map/ppermute | solution.py:87
  326.5 7.2 light.62.refs_12_.own_ref
  339.1 9.6 %collective-permute-done.38.refs_15_.other_ref = bf16[1536,1024]{1,0:T(8,128)(2,1)S(1)} collective-permute-done((bf16[1536,1024]{1,0:T(8,128)(2,1)}, bf16[1536,1024]{1,0:T(8,128)(2,1)S(1)}, u32[]{:S(2)}, u32[]{:S(2)}) %collective-permute-start.38) | collective-permute-done | bytes 3145760 | tf_op jit(solution)/shard_map/ppermute | solution.py:87
  350.4 35.5 %feed_forward.1 = (bf16[1024,1536]{1,0:T(8,128)(2,1)}, bf16[1024,1536]{1,0:T(8,128)(2,1)}, bf16[1024,1536]{1,0:T(8,128)(2,1)}) custom-call(s32[1]{0:T(128)} %bitcast.58.places_ref.core_ref.column_ref, bf16[256,2048]{1,0:T(8,128)(2,1)} %get-tuple-element.563.refs_0_, bf16[256,2048]{1,0:T(8,128)(2,1)} %copy-done.6, bf16[256,2048]{1,0:T(8,128)(2,1)} %copy-done.7, ...), custom_call_target="tpu_custom_call" | custom-call | flops 1 | bytes 1 | tf_op jit(solution)/shard_map/feed_forward/pallas_call | solution.py:443
  385.8 11.1 %weight_grad.8 = bf16[2048,1536]{1,0:T(8,128)(2,1)} custom-call(s32[1]{0:T(128)} %constant.85.clone.1.column_ref, bf16[256,2048]{1,0:T(8,128)(2,1)} %get-tuple-element.563.refs_0_, bf16[256,2048]{1,0:T(8,128)(2,1)} %copy-done.6, bf16[256,2048]{1,0:T(8,128)(2,1)} %copy-done.7, bf16[256,2048]{1,0:T(8,128)(2,1)} %copy-done.8, ...), custom_call_target="tpu_custom_call" | custom-call | flops 1 | bytes 1 | tf_op jit(solution)/shard_map/weight_grad/pallas_call | solution.py:542
  397.0 7.2 weight_grad.9
  404.6 23.2 %feed_forward_back.1 = (bf16[256,2048]{1,0:T(8,128)(2,1)}, bf16[256,2048]{1,0:T(8,128)(2,1)}, bf16[256,2048]{1,0:T(8,128)(2,1)}, bf16[256,2048]{1,0:T(8,128)(2,1)}) custom-call(bf16[1024,1536]{1,0:T(8,128)(2,1)} %get-tuple-element.584.go_ref.refs_4_, bf16[1024,1536]{1,0:T(8,128)(2,1)} %get-tuple-element.577.refs_4_.gx_ref, ...), custom_call_target="tpu_custom_call" | custom-call | flops 1 | bytes 1 | tf_op jit(solution)/shard_map/feed_forward_back/pallas_call | solution.py:484
  429.7 13.1 %weight_grad.10.refs_1_ = bf16[2048,1536]{1,0:T(8,128)(2,1)} custom-call(s32[1]{0:T(128)} %constant.85.clone.1.column_ref, bf16[256,2048]{1,0:T(8,128)(2,1)} %get-tuple-element.563.refs_0_, bf16[256,2048]{1,0:T(8,128)(2,1)} %copy-done.6, bf16[256,2048]{1,0:T(8,128)(2,1)} %copy-done.7, bf16[256,2048]{1,0:T(8,128)(2,1)} %copy-done.8, ...), custom_call_target="tpu_custom_call" | custom-call | flops 1 | bytes 1 | tf_op jit(solution)/shard_map/weight_grad/pallas_call | solution.py:542
  442.8 6.7 light.64
  460.2 7.7 weight_grad.11.refs_1_
  472.5 12.8 %down_project.1 = (bf16[256,2048]{1,0:T(8,128)(2,1)}, bf16[256,2048]{1,0:T(8,128)(2,1)}, bf16[256,2048]{1,0:T(8,128)(2,1)}, bf16[256,2048]{1,0:T(8,128)(2,1)}) custom-call(bf16[1024,1536]{1,0:T(8,128)(2,1)} %get-tuple-element.596.refs_0_.hidden_ref, bf16[1536,1024]{1,0:T(8,128)(2,1)} %light.63.refs_14_.own_ref, bf16[1536,1024]{1,0:T(8,128)(2,1)} %copy-done.5), custom_call_target="tpu_custom_call" | custom-call | flops 1 | bytes 1 | tf_op jit(solution)/shard_map/down_project/pallas_call | solution.py:578
  485.3 6.3 light.67
  498.3 7.5 spread_back.2
  508.8 6.4 attend_group_back.4
  517.0 6.4 attend_group_back.5
  529.6 5.9 weight_grad.12
  536.8 6.4 attend_group_back.6
  543.2 5.1 weight_grad.13
  548.2 6.7 weight_grad.14
  556.3 6.4 attend_group_back.7
  569.0 6.4 light.73
  577.4 6.1 weight_grad.15
  591.3 40.8 %collective-permute-done.50.refs_2_ = bf16[1024,512]{1,0:T(8,128)(2,1)} collective-permute-done((bf16[1024,512]{1,0:T(8,128)(2,1)}, bf16[1024,512]{1,0:T(8,128)(2,1)}, u32[]{:S(2)}, u32[]{:S(2)}) %collective-permute-start.50) | collective-permute-done | bytes 1048608 | tf_op jit(solution)/shard_map/ppermute | solution.py:87
  636.3 12.5 %spread_back.3 = (bf16[256,2048]{1,0:T(8,128)(2,1)}, bf16[256,2048]{1,0:T(8,128)(2,1)}) custom-call(s32[48]{0:T(128)} %stack.262.places_ref, bf16[512,768]{1,0:T(8,128)(2,1)} %light.74.refs_1_.refs_0_, bf16[512,768]{1,0:T(8,128)(2,1)} %light.71.refs_1_, bf16[512,512]{1,0:T(8,128)(2,1)} %get-tuple-element.687.refs_1_.refs_2_, ...), custom_call_target="tpu_custom_call" | custom-call | flops 1 | bytes 1 | tf_op jit(solution)/shard_map/spread_back/pallas_call | solution.py:395
  653.5 5.4 collective-permute-done.56.refs_2_
  683.7 5.3 light.83
  695.6 11.8 %collective-permute-done.63.refs_2_ = bf16[256,2048]{1,0:T(8,128)(2,1)S(1)} collective-permute-done((bf16[256,2048]{1,0:T(8,128)(2,1)}, bf16[256,2048]{1,0:T(8,128)(2,1)S(1)}, u32[]{:S(2)}, u32[]{:S(2)}) %collective-permute-start.63) | collective-permute-done | bytes 1048608 | tf_op jit(solution)/shard_map/ppermute | solution.py:87
  711.5 6.8 collective-permute-done.60.refs_7_
  732.0 8.7 %collective-permute-done.64.refs_2_.refs_1_ = bf16[128,1536]{1,0:T(8,128)(2,1)S(1)} collective-permute-done((bf16[128,1536]{1,0:T(8,128)(2,1)}, bf16[128,1536]{1,0:T(8,128)(2,1)S(1)}, u32[]{:S(2)}, u32[]{:S(2)}) %collective-permute-start.64) | collective-permute-done | bytes 393248 | tf_op jit(solution)/shard_map/ppermute | solution.py:87
  740.8 4.9 collective-permute-done.66.refs_4_.refs_3_
  756.7 9.8 %collective-permute-done.68.refs_2_ = bf16[128,2048]{1,0:T(8,128)(2,1)S(1)} collective-permute-done((bf16[128,2048]{1,0:T(8,128)(2,1)}, bf16[128,2048]{1,0:T(8,128)(2,1)S(1)}, u32[]{:S(2)}, u32[]{:S(2)}) %collective-permute-start.68) | collective-permute-done | bytes 524320 | tf_op jit(solution)/shard_map/ppermute | solution.py:87
  779.1 7.1 collective-permute-done.71.refs_2_
  789.4 5.1 put_columns.3
  805.3 5.6 put_columns.4
  (333 shorter events, 295.5 us)
Async XLA Ops:
  7.1 26.0 %collective-permute-start.1 = (bf16[128,1536]{1,0:T(8,128)(2,1)}, bf16[128,1536]{1,0:T(8,128)(2,1)S(1)}, u32[]{:S(2)}, u32[]{:S(2)}) collective-permute-start(bf16[128,1536]{1,0:T(8,128)(2,1)} %get-tuple-element.406), channel_id=1, source_target_pairs={{0,2},{1,3},{2,0},{3,1},{4,6},{5,7},{6,4},{7,5},{8,10},{9,11},{10,... | collective-permute-start | bytes 1179656 | tf_op jit(solution)/shard_map/ppermute | solution.py:87
  11.2 29.5 %collective-permute-start.3 = (bf16[128,1536]{1,0:T(8,128)(2,1)}, bf16[128,1536]{1,0:T(8,128)(2,1)}, u32[]{:S(2)}, u32[]{:S(2)}) collective-permute-start(bf16[128,1536]{1,0:T(8,128)(2,1)} %get-tuple-element.408), channel_id=1, source_target_pairs={{0,10},{1,11},{2,8},{3,9},{4,14},{5,15},{6,12},{7,13},{8,2},{9,3},... | collective-permute-start | bytes 1179656 | tf_op jit(solution)/shard_map/ppermute | solution.py:87
  14.6 26.0 %collective-permute-start.4 = (bf16[128,2048]{1,0:T(8,128)(2,1)}, bf16[128,2048]{1,0:T(8,128)(2,1)S(1)}, u32[]{:S(2)}, u32[]{:S(2)}) collective-permute-start(bf16[128,2048]{1,0:T(8,128)(2,1)} %pick_columns.7.refs_1_), channel_id=1, source_target_pairs={{0,16},{1,17},{2,18},{3,19},{4,20},{5,21},{6,22},{7,23},{8,24},{9,... | collective-permute-start | bytes 1572872 | tf_op jit(solution)/shard_map/ppermute | solution.py:87
  52.4 38.8 %collective-permute-start.13 = (bf16[384,1024]{1,0:T(8,128)(2,1)S(1)}, bf16[384,1024]{1,0:T(8,128)(2,1)}, u32[]{:S(2)}, u32[]{:S(2)}) collective-permute-start(bf16[384,1024]{1,0:T(8,128)(2,1)S(1)} %copy-done.9), channel_id=1, source_target_pairs={{0,4},{1,5},{2,6},{3,7},{4,0},{5,1},{6,2},{7,3},{8,12},{9,13},{10,... | collective-permute-start | bytes 2359304 | tf_op jit(solution)/shard_map/ppermute | solution.py:87
  97.7 44.9 %collective-permute-start.14 = (bf16[1024,768]{1,0:T(8,128)(2,1)}, bf16[1024,768]{1,0:T(8,128)(2,1)S(1)}, u32[]{:S(2)}, u32[]{:S(2)}) collective-permute-start(bf16[1024,768]{1,0:T(8,128)(2,1)} %get-tuple-element.465.refs_1_.refs_3_), channel_id=1, source_target_pairs={{0,4},{1,5},{2,6},{3,7},{4,0},{5,1},{6,2},{7,3},{8,12},{9,13},{10,... | collective-permute-start | bytes 4718600 | tf_op jit(solution)/shard_map/ppermute | solution.py:87
  99.2 44.5 %collective-permute-start.15 = (bf16[1024,768]{1,0:T(8,128)(2,1)}, bf16[1024,768]{1,0:T(8,128)(2,1)}, u32[]{:S(2)}, u32[]{:S(2)}) collective-permute-start(bf16[1024,768]{1,0:T(8,128)(2,1)} %get-tuple-element.466.refs_1_.refs_4_.refs_5_), channel_id=1, source_target_pairs={{0,2},{1,3},{2,0},{3,1},{4,6},{5,7},{6,4},{7,5},{8,10},{9,11},{10,... | collective-permute-start | bytes 4718600 | tf_op jit(solution)/shard_map/ppermute | solution.py:87
  99.7 42.9 %collective-permute-start.16 = (bf16[1024,512]{1,0:T(8,128)(2,1)}, bf16[1024,512]{1,0:T(8,128)(2,1)}, u32[]{:S(2)}, u32[]{:S(2)}) collective-permute-start(bf16[1024,512]{1,0:T(8,128)(2,1)} %get-tuple-element.467.refs_1_.refs_7_), channel_id=1, source_target_pairs={{0,8},{1,9},{2,10},{3,11},{4,12},{5,13},{6,14},{7,15},{8,0},{9,1},... | collective-permute-start | bytes 3145736 | tf_op jit(solution)/shard_map/ppermute | solution.py:87
  99.7 38.5 %collective-permute-start.17 = (bf16[256,1536]{1,0:T(8,128)(2,1)}, bf16[256,1536]{1,0:T(8,128)(2,1)}, u32[]{:S(2)}, u32[]{:S(2)}) collective-permute-start(bf16[256,1536]{1,0:T(8,128)(2,1)} %get-tuple-element.549.refs_1_), channel_id=1, source_target_pairs={{0,16},{1,17},{2,18},{3,19},{4,20},{5,21},{6,22},{7,23},{8,24},{9,... | collective-permute-start | bytes 2359304 | tf_op jit(solution)/shard_map/ppermute | solution.py:87
  143.7 33.6 %collective-permute-start.19 = (bf16[256,2048]{1,0:T(8,128)(2,1)S(1)}, bf16[256,2048]{1,0:T(8,128)(2,1)S(1)}, u32[]{:S(2)}, u32[]{:S(2)}) collective-permute-start(bf16[256,2048]{1,0:T(8,128)(2,1)S(1)} %copy-done), channel_id=1, source_target_pairs={{0,2},{1,3},{2,0},{3,1},{4,6},{5,7},{6,4},{7,5},{8,10},{9,11},{10,... | collective-permute-start | bytes 3145736 | tf_op jit(solution)/shard_map/ppermute | solution.py:87
  144.8 32.5 %collective-permute-start.20 = (bf16[256,1536]{1,0:T(8,128)(2,1)}, bf16[256,1536]{1,0:T(8,128)(2,1)}, u32[]{:S(2)}, u32[]{:S(2)}) collective-permute-start(bf16[256,1536]{1,0:T(8,128)(2,1)} %get-tuple-element.549.refs_1_), channel_id=1, source_target_pairs={{0,4},{1,5},{2,6},{3,7},{4,0},{5,1},{6,2},{7,3},{8,12},{9,13},{10,... | collective-permute-start | bytes 2359304 | tf_op jit(solution)/shard_map/ppermute | solution.py:87
  145.4 31.9 %collective-permute-start.18 = (bf16[128,2048]{1,0:T(8,128)(2,1)}, bf16[128,2048]{1,0:T(8,128)(2,1)S(1)}, u32[]{:S(2)}, u32[]{:S(2)}) collective-permute-start(bf16[128,2048]{1,0:T(8,128)(2,1)} %light.56.refs_1_), channel_id=1, source_target_pairs={{0,8},{1,9},{2,10},{3,11},{4,12},{5,13},{6,14},{7,15},{8,0},{9,1},... | collective-permute-start | bytes 1572872 | tf_op jit(solution)/shard_map/ppermute | solution.py:87
  145.4 52.8 %collective-permute-start.23 = (bf16[256,2048]{1,0:T(8,128)(2,1)S(1)}, bf16[256,2048]{1,0:T(8,128)(2,1)S(1)}, u32[]{:S(2)}, u32[]{:S(2)}) collective-permute-start(bf16[256,2048]{1,0:T(8,128)(2,1)S(1)} %copy-done), channel_id=1, source_target_pairs={{0,8},{1,9},{2,10},{3,11},{4,12},{5,13},{6,14},{7,15},{8,0},{9,1},... | collective-permute-start | bytes 3145736 | tf_op jit(solution)/shard_map/ppermute | solution.py:87
  147.4 50.8 %collective-permute-start.25 = (bf16[256,1536]{1,0:T(8,128)(2,1)}, bf16[256,1536]{1,0:T(8,128)(2,1)}, u32[]{:S(2)}, u32[]{:S(2)}) collective-permute-start(bf16[256,1536]{1,0:T(8,128)(2,1)} %get-tuple-element.551.refs_3_), channel_id=1, source_target_pairs={{0,16},{1,17},{2,18},{3,19},{4,20},{5,21},{6,22},{7,23},{8,24},{9,... | collective-permute-start | bytes 2359304 | tf_op jit(solution)/shard_map/ppermute | solution.py:87
  180.3 27.0 %collective-permute-start.24 = (bf16[256,1536]{1,0:T(8,128)(2,1)}, bf16[256,1536]{1,0:T(8,128)(2,1)}, u32[]{:S(2)}, u32[]{:S(2)}) collective-permute-start(bf16[256,1536]{1,0:T(8,128)(2,1)} %get-tuple-element.551.refs_3_), channel_id=1, source_target_pairs={{0,4},{1,5},{2,6},{3,7},{4,0},{5,1},{6,2},{7,3},{8,12},{9,13},{10,... | collective-permute-start | bytes 2359304 | tf_op jit(solution)/shard_map/ppermute | solution.py:87
  182.7 24.6 %collective-permute-start.22 = (bf16[256,1024]{1,0:T(8,128)(2,1)}, bf16[256,1024]{1,0:T(8,128)(2,1)}, u32[]{:S(2)}, u32[]{:S(2)}) collective-permute-start(bf16[256,1024]{1,0:T(8,128)(2,1)} %get-tuple-element.506.refs_2_), channel_id=1, source_target_pairs={{0,4},{1,5},{2,6},{3,7},{4,0},{5,1},{6,2},{7,3},{8,12},{9,13},{10,... | collective-permute-start | bytes 1572872 | tf_op jit(solution)/shard_map/ppermute | solution.py:87
  210.2 37.0 %collective-permute-start.28 = (bf16[256,2048]{1,0:T(8,128)(2,1)S(1)}, bf16[256,2048]{1,0:T(8,128)(2,1)S(1)}, u32[]{:S(2)}, u32[]{:S(2)}) collective-permute-start(bf16[256,2048]{1,0:T(8,128)(2,1)S(1)} %collective-permute-done.19.refs_6_.refs_10_.refs_3_), channel_id=1, source_target_pairs={{0,8},{1,9},{2,10},{3,11},{4,12},{5,13},{6,14},{7,15},{8,0},{9,1},... | collective-permute-start | bytes 3145736 | tf_op jit(solution)/shard_map/ppermute | solution.py:87
  210.2 37.0 %collective-permute-start.26 = (bf16[512,1024]{1,0:T(8,128)(2,1)}, bf16[512,1024]{1,0:T(8,128)(2,1)}, u32[]{:S(2)}, u32[]{:S(2)}) collective-permute-start(bf16[512,1024]{1,0:T(8,128)(2,1)} %get-tuple-element.527.refs_3_.refs_2_), channel_id=1, source_target_pairs={{0,4},{1,5},{2,6},{3,7},{4,0},{5,1},{6,2},{7,3},{8,12},{9,13},{10,... | collective-permute-start | bytes 3145736 | tf_op jit(solution)/shard_map/ppermute | solution.py:87
  211.5 35.6 %collective-permute-start.27 = (bf16[512,1024]{1,0:T(8,128)(2,1)}, bf16[512,1024]{1,0:T(8,128)(2,1)}, u32[]{:S(2)}, u32[]{:S(2)}) collective-permute-start(bf16[512,1024]{1,0:T(8,128)(2,1)} %get-tuple-element.529.refs_5_.refs_4_), channel_id=1, source_target_pairs={{0,2},{1,3},{2,0},{3,1},{4,6},{5,7},{6,4},{7,5},{8,10},{9,11},{10,... | collective-permute-start | bytes 3145736 | tf_op jit(solution)/shard_map/ppermute | solution.py:87
  213.9 31.1 %collective-permute-start.29 = (bf16[384,1024]{1,0:T(8,128)(2,1)}, bf16[384,1024]{1,0:T(8,128)(2,1)}, u32[]{:S(2)}, u32[]{:S(2)}) collective-permute-start(bf16[384,1024]{1,0:T(8,128)(2,1)} %pick_columns.8.refs_1_), channel_id=1, source_target_pairs={{0,16},{1,17},{2,18},{3,19},{4,20},{5,21},{6,22},{7,23},{8,24},{9,... | collective-permute-start | bytes 2359304 | tf_op jit(solution)/shard_map/ppermute | solution.py:87
  262.4 39.0 %collective-permute-start.33 = (bf16[256,2048]{1,0:T(8,128)(2,1)}, bf16[256,2048]{1,0:T(8,128)(2,1)S(1)}, u32[]{:S(2)}, u32[]{:S(2)}) collective-permute-start(bf16[256,2048]{1,0:T(8,128)(2,1)} %get-tuple-element.563.refs_0_), channel_id=1, source_target_pairs={{0,8},{1,9},{2,10},{3,11},{4,12},{5,13},{6,14},{7,15},{8,0},{9,1},... | collective-permute-start | bytes 3145736 | tf_op jit(solution)/shard_map/ppermute | solution.py:87
  266.7 34.6 %collective-permute-start.31 = (bf16[256,1536]{1,0:T(8,128)(2,1)}, bf16[256,1536]{1,0:T(8,128)(2,1)S(1)}, u32[]{:S(2)}, u32[]{:S(2)}) collective-permute-start(bf16[256,1536]{1,0:T(8,128)(2,1)} %collective-permute-done.17.refs_2_), channel_id=1, source_target_pairs={{0,4},{1,5},{2,6},{3,7},{4,0},{5,1},{6,2},{7,3},{8,12},{9,13},{10,... | collective-permute-start | bytes 2359304 | tf_op jit(solution)/shard_map/ppermute | solution.py:87
  266.8 55.4 %collective-permute-start.34 = (bf16[256,2048]{1,0:T(8,128)(2,1)}, bf16[256,2048]{1,0:T(8,128)(2,1)S(1)}, u32[]{:S(2)}, u32[]{:S(2)}) collective-permute-start(bf16[256,2048]{1,0:T(8,128)(2,1)} %get-tuple-element.563.refs_0_), channel_id=1, source_target_pairs={{0,2},{1,3},{2,0},{3,1},{4,6},{5,7},{6,4},{7,5},{8,10},{9,11},{10,... | collective-permute-start | bytes 3145736 | tf_op jit(solution)/shard_map/ppermute | solution.py:87
  396.9 32.8 %collective-permute-start.39 = (bf16[2048,1536]{1,0:T(8,128)(2,1)}, bf16[2048,1536]{1,0:T(8,128)(2,1)}, u32[]{:S(2)}, u32[]{:S(2)}) collective-permute-start(bf16[2048,1536]{1,0:T(8,128)(2,1)} %weight_grad.8), channel_id=1, source_target_pairs={{0,1},{1,0},{2,3},{3,2},{4,5},{5,4},{6,7},{7,6},{8,9},{9,8},{10,11... | collective-permute-start | bytes 18874376 | tf_op jit(solution)/shard_map/ppermute | solution.py:87
  404.2 25.5 %collective-permute-start.40 = (bf16[1536,1024]{1,0:T(8,128)(2,1)}, bf16[1536,1024]{1,0:T(8,128)(2,1)S(1)}, u32[]{:S(2)}, u32[]{:S(2)}) collective-permute-start(bf16[1536,1024]{1,0:T(8,128)(2,1)} %weight_grad.9), channel_id=1, source_target_pairs={{0,1},{1,0},{2,3},{3,2},{4,5},{5,4},{6,7},{7,6},{8,9},{9,8},{10,11... | collective-permute-start | bytes 9437192 | tf_op jit(solution)/shard_map/ppermute | solution.py:87
  427.8 25.5 %collective-permute-start.41 = (bf16[256,2048]{1,0:T(8,128)(2,1)}, bf16[256,2048]{1,0:T(8,128)(2,1)}, u32[]{:S(2)}, u32[]{:S(2)}) collective-permute-start(bf16[256,2048]{1,0:T(8,128)(2,1)} %get-tuple-element.581), channel_id=1, source_target_pairs={{0,2},{1,3},{2,0},{3,1},{4,6},{5,7},{6,4},{7,5},{8,10},{9,11},{10,... | collective-permute-start | bytes 3145736 | tf_op jit(solution)/shard_map/ppermute | solution.py:87
  456.1 29.2 %collective-permute-start.42 = (bf16[256,2048]{1,0:T(8,128)(2,1)}, bf16[256,2048]{1,0:T(8,128)(2,1)}, u32[]{:S(2)}, u32[]{:S(2)}) collective-permute-start(bf16[256,2048]{1,0:T(8,128)(2,1)} %get-tuple-element.591), channel_id=1, source_target_pairs={{0,2},{1,3},{2,0},{3,1},{4,6},{5,7},{6,4},{7,5},{8,10},{9,11},{10,... | collective-permute-start | bytes 3145736 | tf_op jit(solution)/shard_map/ppermute | solution.py:87
  457.3 28.0 %collective-permute-start.43 = (bf16[256,2048]{1,0:T(8,128)(2,1)}, bf16[256,2048]{1,0:T(8,128)(2,1)}, u32[]{:S(2)}, u32[]{:S(2)}) collective-permute-start(bf16[256,2048]{1,0:T(8,128)(2,1)} %light.65), channel_id=1, source_target_pairs={{0,8},{1,9},{2,10},{3,11},{4,12},{5,13},{6,14},{7,15},{8,0},{9,1},... | collective-permute-start | bytes 3145736 | tf_op jit(solution)/shard_map/ppermute | solution.py:87
  458.7 108.6 %collective-permute-start.48 = (bf16[1024,1536]{1,0:T(8,128)(2,1)}, bf16[1024,1536]{1,0:T(8,128)(2,1)S(1)}, u32[]{:S(2)}, u32[]{:S(2)}) collective-permute-start(bf16[1024,1536]{1,0:T(8,128)(2,1)} %get-tuple-element.587), channel_id=1, source_target_pairs={{0,4},{1,5},{2,6},{3,7},{4,0},{5,1},{6,2},{7,3},{8,12},{9,13},{10,... | collective-permute-start | bytes 9437192 | tf_op jit(solution)/shard_map/ppermute | solution.py:87
  491.6 31.8 %collective-permute-start.44 = (bf16[256,2048]{1,0:T(8,128)(2,1)}, bf16[256,2048]{1,0:T(8,128)(2,1)}, u32[]{:S(2)}, u32[]{:S(2)}) collective-permute-start(bf16[256,2048]{1,0:T(8,128)(2,1)} %get-tuple-element.613), channel_id=1, source_target_pairs={{0,2},{1,3},{2,0},{3,1},{4,6},{5,7},{6,4},{7,5},{8,10},{9,11},{10,... | collective-permute-start | bytes 3145736 | tf_op jit(solution)/shard_map/ppermute | solution.py:87
  491.9 75.4 %collective-permute-start.49 = (bf16[768,1024]{1,0:T(8,128)(2,1)}, bf16[768,1024]{1,0:T(8,128)(2,1)}, u32[]{:S(2)}, u32[]{:S(2)}) collective-permute-start(bf16[768,1024]{1,0:T(8,128)(2,1)} %get-tuple-element.595), channel_id=1, source_target_pairs={{0,4},{1,5},{2,6},{3,7},{4,0},{5,1},{6,2},{7,3},{8,12},{9,13},{10,... | collective-permute-start | bytes 4718600 | tf_op jit(solution)/shard_map/ppermute | solution.py:87
  526.2 28.8 %collective-permute-start.46 = (bf16[256,2048]{1,0:T(8,128)(2,1)}, bf16[256,2048]{1,0:T(8,128)(2,1)}, u32[]{:S(2)}, u32[]{:S(2)}) collective-permute-start(bf16[256,2048]{1,0:T(8,128)(2,1)} %get-tuple-element.637), channel_id=1, source_target_pairs={{0,2},{1,3},{2,0},{3,1},{4,6},{5,7},{6,4},{7,5},{8,10},{9,11},{10,... | collective-permute-start | bytes 3145736 | tf_op jit(solution)/shard_map/ppermute | solution.py:87
  526.4 36.2 %collective-permute-start.47 = (bf16[256,2048]{1,0:T(8,128)(2,1)}, bf16[256,2048]{1,0:T(8,128)(2,1)}, u32[]{:S(2)}, u32[]{:S(2)}) collective-permute-start(bf16[256,2048]{1,0:T(8,128)(2,1)} %light.70), channel_id=1, source_target_pairs={{0,8},{1,9},{2,10},{3,11},{4,12},{5,13},{6,14},{7,15},{8,0},{9,1},... | collective-permute-start | bytes 3145736 | tf_op jit(solution)/shard_map/ppermute | solution.py:87
  535.5 51.6 %collective-permute-start.51 = (bf16[1024,768]{1,0:T(8,128)(2,1)}, bf16[1024,768]{1,0:T(8,128)(2,1)}, u32[]{:S(2)}, u32[]{:S(2)}) collective-permute-start(bf16[1024,768]{1,0:T(8,128)(2,1)} %get-tuple-element.643), channel_id=1, source_target_pairs={{0,2},{1,3},{2,0},{3,1},{4,6},{5,7},{6,4},{7,5},{8,10},{9,11},{10,... | collective-permute-start | bytes 4718600 | tf_op jit(solution)/shard_map/ppermute | solution.py:87
  554.9 110.9 %collective-permute-start.54 = (bf16[512,2048]{1,0:T(8,128)(2,1)}, bf16[512,2048]{1,0:T(8,128)(2,1)}, u32[]{:S(2)}, u32[]{:S(2)}) collective-permute-start(bf16[512,2048]{1,0:T(8,128)(2,1)} %get-tuple-element.653), channel_id=1, source_target_pairs={{0,2},{1,3},{2,0},{3,1},{4,6},{5,7},{6,4},{7,5},{8,10},{9,11},{10,... | collective-permute-start | bytes 6291464 | tf_op jit(solution)/shard_map/ppermute | solution.py:87
  583.5 65.3 %collective-permute-start.57 = (bf16[1024,768]{1,0:T(8,128)(2,1)}, bf16[1024,768]{1,0:T(8,128)(2,1)S(1)}, u32[]{:S(2)}, u32[]{:S(2)}) collective-permute-start(bf16[1024,768]{1,0:T(8,128)(2,1)} %get-tuple-element.674), channel_id=1, source_target_pairs={{0,4},{1,5},{2,6},{3,7},{4,0},{5,1},{6,2},{7,3},{8,12},{9,13},{10,... | collective-permute-start | bytes 4718600 | tf_op jit(solution)/shard_map/ppermute | solution.py:87
  584.5 47.5 %collective-permute-start.50 = (bf16[1024,512]{1,0:T(8,128)(2,1)}, bf16[1024,512]{1,0:T(8,128)(2,1)}, u32[]{:S(2)}, u32[]{:S(2)}) collective-permute-start(bf16[1024,512]{1,0:T(8,128)(2,1)} %get-tuple-element.650), channel_id=1, source_target_pairs={{0,8},{1,9},{2,10},{3,11},{4,12},{5,13},{6,14},{7,15},{8,0},{9,1},... | collective-permute-start | bytes 3145736 | tf_op jit(solution)/shard_map/ppermute | solution.py:87
  585.9 87.3 %collective-permute-start.53 = (bf16[512,1536]{1,0:T(8,128)(2,1)}, bf16[512,1536]{1,0:T(8,128)(2,1)S(1)}, u32[]{:S(2)}, u32[]{:S(2)}) collective-permute-start(bf16[512,1536]{1,0:T(8,128)(2,1)} %get-tuple-element.668), channel_id=1, source_target_pairs={{0,16},{1,17},{2,18},{3,19},{4,20},{5,21},{6,22},{7,23},{8,24},{9,... | collective-permute-start | bytes 4718600 | tf_op jit(solution)/shard_map/ppermute | solution.py:87
  590.6 68.2 %collective-permute-start.56 = (bf16[512,768]{1,0:T(8,128)(2,1)}, bf16[512,768]{1,0:T(8,128)(2,1)S(1)}, u32[]{:S(2)}, u32[]{:S(2)}) collective-permute-start(bf16[512,768]{1,0:T(8,128)(2,1)} %get-tuple-element.679), channel_id=1, source_target_pairs={{0,8},{1,9},{2,10},{3,11},{4,12},{5,13},{6,14},{7,15},{8,0},{9,1},... | collective-permute-start | bytes 2359304 | tf_op jit(solution)/shard_map/ppermute | solution.py:87
  634.8 28.7 %collective-permute-start.55 = (bf16[512,512]{1,0:T(8,128)(2,1)}, bf16[512,512]{1,0:T(8,128)(2,1)}, u32[]{:S(2)}, u32[]{:S(2)}) collective-permute-start(bf16[512,512]{1,0:T(8,128)(2,1)} %get-tuple-element.684), channel_id=1, source_target_pairs={{0,4},{1,5},{2,6},{3,7},{4,0},{5,1},{6,2},{7,3},{8,12},{9,13},{10,... | collective-permute-start | bytes 1572872 | tf_op jit(solution)/shard_map/ppermute | solution.py:87
  648.8 34.8 %collective-permute-start.52 = (bf16[256,2048]{1,0:T(8,128)(2,1)}, bf16[256,2048]{1,0:T(8,128)(2,1)}, u32[]{:S(2)}, u32[]{:S(2)}) collective-permute-start(bf16[256,2048]{1,0:T(8,128)(2,1)} %get-tuple-element.689), channel_id=1, source_target_pairs={{0,1},{1,0},{2,3},{3,2},{4,5},{5,4},{6,7},{7,6},{8,9},{9,8},{10,11... | collective-permute-start | bytes 3145736 | tf_op jit(solution)/shard_map/ppermute | solution.py:87
  659.7 29.3 %collective-permute-start.59 = (bf16[512,768]{1,0:T(8,128)(2,1)}, bf16[512,768]{1,0:T(8,128)(2,1)S(1)}, u32[]{:S(2)}, u32[]{:S(2)}) collective-permute-start(bf16[512,768]{1,0:T(8,128)(2,1)} %get-tuple-element.694), channel_id=1, source_target_pairs={{0,2},{1,3},{2,0},{3,1},{4,6},{5,7},{6,4},{7,5},{8,10},{9,11},{10,... | collective-permute-start | bytes 2359304 | tf_op jit(solution)/shard_map/ppermute | solution.py:87
  670.0 37.4 %collective-permute-start.63 = (bf16[256,2048]{1,0:T(8,128)(2,1)}, bf16[256,2048]{1,0:T(8,128)(2,1)S(1)}, u32[]{:S(2)}, u32[]{:S(2)}) collective-permute-start(bf16[256,2048]{1,0:T(8,128)(2,1)} %get-tuple-element.709), channel_id=1, source_target_pairs={{0,8},{1,9},{2,10},{3,11},{4,12},{5,13},{6,14},{7,15},{8,0},{9,1},... | collective-permute-start | bytes 3145736 | tf_op jit(solution)/shard_map/ppermute | solution.py:87
  671.5 39.9 %collective-permute-start.61 = (bf16[256,768]{1,0:T(8,128)(2,1)S(1)}, bf16[256,768]{1,0:T(8,128)(2,1)}, u32[]{:S(2)}, u32[]{:S(2)}) collective-permute-start(bf16[256,768]{1,0:T(8,128)(2,1)S(1)} %copy-done.37), channel_id=1, source_target_pairs={{0,4},{1,5},{2,6},{3,7},{4,0},{5,1},{6,2},{7,3},{8,12},{9,13},{10,... | collective-permute-start | bytes 1179656 | tf_op jit(solution)/shard_map/ppermute | solution.py:87
  682.4 63.3 %collective-permute-start.69 = (bf16[384,1024]{1,0:T(8,128)(2,1)}, bf16[384,1024]{1,0:T(8,128)(2,1)S(1)}, u32[]{:S(2)}, u32[]{:S(2)}) collective-permute-start(bf16[384,1024]{1,0:T(8,128)(2,1)} %get-tuple-element.716), channel_id=1, source_target_pairs={{0,16},{1,17},{2,18},{3,19},{4,20},{5,21},{6,22},{7,23},{8,24},{9,... | collective-permute-start | bytes 2359304 | tf_op jit(solution)/shard_map/ppermute | solution.py:87
  692.6 25.6 %collective-permute-start.60 = (bf16[256,768]{1,0:T(8,128)(2,1)}, bf16[256,768]{1,0:T(8,128)(2,1)S(1)}, u32[]{:S(2)}, u32[]{:S(2)}) collective-permute-start(bf16[256,768]{1,0:T(8,128)(2,1)} %get-tuple-element.741.refs_2_), channel_id=1, source_target_pairs={{0,8},{1,9},{2,10},{3,11},{4,12},{5,13},{6,14},{7,15},{8,0},{9,1},... | collective-permute-start | bytes 1179656 | tf_op jit(solution)/shard_map/ppermute | solution.py:87
  751.9 34.3 %collective-permute-start.73 = (bf16[128,6144]{1,0:T(8,128)(2,1)}, bf16[128,6144]{1,0:T(8,128)(2,1)S(1)}, u32[]{:S(2)}, u32[]{:S(2)}) collective-permute-start(bf16[128,6144]{1,0:T(8,128)(2,1)} %light.90), channel_id=1, source_target_pairs={{0,1},{1,0},{2,3},{3,2},{4,5},{5,4},{6,7},{7,6},{8,9},{9,8},{10,11... | collective-permute-start | bytes 4718600 | tf_op jit(solution)/shard_map/ppermute | solution.py:87
  753.5 32.8 %collective-permute-start.72 = (bf16[384,1024]{1,0:T(8,128)(2,1)S(1)}, bf16[384,1024]{1,0:T(8,128)(2,1)S(1)}, u32[]{:S(2)}, u32[]{:S(2)}) collective-permute-start(bf16[384,1024]{1,0:T(8,128)(2,1)S(1)} %copy-done.12), channel_id=1, source_target_pairs={{0,1},{1,0},{2,3},{3,2},{4,5},{5,4},{6,7},{7,6},{8,9},{9,8},{10,11... | collective-permute-start | bytes 2359304 | tf_op jit(solution)/shard_map/ppermute | solution.py:87
  753.7 32.5 %collective-permute-start.71 = (bf16[128,2048]{1,0:T(8,128)(2,1)}, bf16[128,2048]{1,0:T(8,128)(2,1)}, u32[]{:S(2)}, u32[]{:S(2)}) collective-permute-start(bf16[128,2048]{1,0:T(8,128)(2,1)} %get-tuple-element.753), channel_id=1, source_target_pairs={{0,16},{1,17},{2,18},{3,19},{4,20},{5,21},{6,22},{7,23},{8,24},{9,... | collective-permute-start | bytes 1572872 | tf_op jit(solution)/shard_map/ppermute | solution.py:87
  (82 other events, 882.9 us)

commit v3 on v2

--- a/solution.py
+++ b/solution.py
@@ -1006,6 +1006,8 @@
     result = line.light(
         to_result, middle, (part_own, part_got_own, part_got_last), flags=(first_core,)
     )
+    keep_2, got_2 = add_step(parcels_back[2][1], parcels_back[2][2], qkv_back[2][1])
+    parcels_back[2] = (parcels_back[2][0], keep_2, got_2)
     gu_got, down_got = line.take((gu_got, down_got))
     gu_mine, gu_far_got = far_step(gu_keep[0], gu_got)
     parcels_back[0] = parcel_back(0, last_q)
@@ -1013,7 +1015,6 @@
     keeps = [parcels_back[g][1] for g in range(3)]
     gots = [parcels_back[g][2] for g in range(3)]
     keeps[1], gots[1] = add_step(keeps[1], gots[1], qkv_back[1][1])
-    keeps[2], gots[2] = add_step(keeps[2], gots[2], qkv_back[2][1])
     grad_first_part = line.run(
         lambda *g: spread_back(g, qkv, block_places, rows, BF16, 2, True), *grad_parcels
     )
@@ -1041,17 +1042,6 @@
         ]
     )
     keeps[0], gots[0] = add_step(keeps[0], gots[0], qkv_back[0][2])
-    sums = sums + line.take(swap_core(sums))
-    out_keep, out_got = add_step(out_keep, out_got, out_back[2])
-    keeps = line.light(
-        lambda a, b: [wide(k[0]) + wide(g) for k, g in zip(a, b)], keeps, line.take(gots)
-    )
-    cut = lambda v: (halves(v)[0], low(halves(v)[1]))
-    mine, away = line.light(lambda *v: cut(jnp.concatenate(v, axis=1)), *keeps)
-    for mask in wires.far[::-1]:
-        last_got = swap(away, mask)
-        if mask != wires.far[0]:
-            mine, away = line.light(lambda a, b: cut(a + wide(b)), mine, line.take(last_got))
     def return_rows(has_one, has_two, v):
         by = [v[i * rows : (i + 1) * rows] for i in range(4)]
         near = [jnp.where(has_two, by[i + 2], by[i]) for i in range(2)]
@@ -1061,27 +1051,46 @@
         ]
         return pick(near) + pick(away)
 
-    gu_back = line.light(return_rows, gu_half, flags=team_flags)
-    gu_back[1:] = [swap(b, t) for b, t in zip(gu_back[1:], (one, two, one | two))]
-    sums_got = swap(line.take(sums), wires.masks[0])
-    down_got = line.take(down_got)
-    down_done = line.light(lambda a, b: low(a + wide(b)), down_mine, down_got)
-    down_sibling = swap_core(down_done)
-    gu_back[1:] = line.take(gu_back[1:])
-    gu_sibling = swap_core(line.light(lambda *v: jnp.concatenate(v, axis=1), *gu_back))
-    out_got = line.take(out_got)
+    back_to = lambda s, c: (s ^ top, c) if (s & top != 0) != (c == 1) else None
+    sums = sums + line.take(swap_core(sums))
+    sums_got = swap(sums, wires.masks[0])
+    out_keep, out_got = add_step(out_keep, out_got, out_back[2])
+    sums = sums + line.take(sums_got)
+    sums_got = swap(sums, wires.masks[1])
+    gots, out_got, sums_got = line.take((gots, out_got, sums_got))
+    sums = sums + sums_got
+    cut = lambda v: (halves(v)[0], low(halves(v)[1]))
+    mine, away = line.light(
+        lambda a, b: cut(jnp.concatenate([wide(k[0]) + wide(g) for k, g in zip(a, b)], axis=1)),
+        keeps, gots,
+    )
+    for mask in wires.far[::-1]:
+        last_got = swap(away, mask)
+        if mask != wires.far[0]:
+            mine, away = line.light(lambda a, b: cut(a + wide(b)), mine, line.take(last_got))
     out_done = line.light(lambda a, b: wide(a) + wide(b), out_keep[0], out_got)
     out_done = scatter_sum(wires, out_done, out_back[3:])
     out_away = line.light(low, out_done)
-    back_to = lambda s, c: (s ^ top, c) if (s & top != 0) != (c == 1) else None
     out_got = wires.send(out_away, back_to)
-    sums = sums + line.take(sums_got)
-    sums_got = swap(sums, wires.masks[1])
-    last_got, down_sibling, gu_sibling = line.take((last_got, down_sibling, gu_sibling))
+    gu_back = line.light(return_rows, gu_half, flags=team_flags)
+    gu_back[1:] = [swap(b, t) for b, t in zip(gu_back[1:], (one, two, one | two))]
+    down_got = line.take(down_got)
+    down_done = line.light(lambda a, b: low(a + wide(b)), down_mine, down_got)
+    gu_back[1:], last_got, out_got, sums = line.take((gu_back[1:], last_got, out_got, sums))
+    gu_sibling = swap_core(line.light(lambda *v: jnp.concatenate(v, axis=1), *gu_back))
     qkv_done = line.light(lambda a, b: low(a + wide(b)), mine, last_got)
     qkv_sibling = swap_core(qkv_done)
-    sums = sums + line.take(sums_got)
+    out_low = line.light(lambda a, b: low(a + wide(b)), out_done, out_got)
+    out_sibling = wires.send(
+        out_low, lambda s, c: (s, 1 - c) if (s & top != 0) == (c == 1) else None
+    )
+    down_sibling = swap_core(down_done)
     sums_got = swap(sums, wires.masks[2])
+    gu_sibling, qkv_sibling, out_sibling, down_sibling, sums_got = line.take(
+        (gu_sibling, qkv_sibling, out_sibling, down_sibling, sums_got)
+    )
+    sums = sums + sums_got
+    sums_got = swap(sums, wires.masks[3])
     gu_out = line.run(
         lambda *v: put_columns(
             list(v),
@@ -1090,12 +1099,6 @@
         ),
         *gu_back, gu_sibling,
     )
-    out_low = line.light(lambda a, b: low(a + wide(b)), out_done, line.take(out_got))
-    out_sibling = wires.send(
-        out_low, lambda s, c: (s, 1 - c) if (s & top != 0) == (c == 1) else None
-    )
-    sums = sums + line.take(sums_got)
-    sums_got = swap(sums, wires.masks[3])
     down_out = line.run(
         lambda a, b: put_columns([a, b], half, [[core], [1 - core]]), down_done, down_sibling
     )
@@ -1103,11 +1106,11 @@
         lambda a, b: put_columns(
             [a, b], HEAD_SIZE, [sum(parcels(core), []), sum(parcels(1 - core), [])]
         ),
-        qkv_done, line.take(qkv_sibling),
+        qkv_done, qkv_sibling,
     )
     out_done = line.light(
         lambda home, a, b: wide(jnp.where(home, a, b)),
-        out_low, line.take(out_sibling), flags=(at_home,),
+        out_low, out_sibling, flags=(at_home,),
     )
     sums = sums + line.take(sums_got)
     for mask in wires.masks[4:]:

time: 826 us -> 817 us (0.989)
    pallas_call x48 -> x47, Pallas kernels: 166 us -> 163 us  [light(): pl.pallas_call(kernel, grid_spec=pltpu.PrefetchScalarGridSpec(num_scalar_...]
    unnamed x102 -> x108, local copies, waits for them, and re-layouts: 17.8 us -> 16.2 us
  transfers between devices with their start and end apart: 79 -> 79, of which waited for: 28 -> 30; matrix products, arithmetic and copies ran while one was open for 2% -> 2% of each run, Pallas kernels for 40% -> 40%
where the time goes in v3:
time: 817 us; the launch traced here: 809 us
  Pallas kernels  408 us (50%)
  waiting for transfers between devices  280 us (34%)
  starting transfers between devices  85.5 us (10%)
  local copies, waits for them, and re-layouts  22.9 us (3%)
  other arithmetic  12.2 us (1%)
    ppermute x79, waiting for transfers between devices, send(): return lax.ppermute(value, AXES, pairs)  280 us
    pallas_call x47, Pallas kernels, light(): pl.pallas_call(kernel, grid_spec=pltpu.PrefetchScalarGridSpec(num_scalar_...  163 us
    ppermute x79, starting transfers between devices, send(): return lax.ppermute(value, AXES, pairs)  85.5 us
    pallas_call x8, Pallas kernels, weight_grad(): pl.pallas_call(kernel, grid_spec=pltpu.PrefetchScalarGridSpec(num_scalar_...  63 us
    pallas_call x1, Pallas kernels, feed_forward(): pl.pallas_call(kernel, grid_spec=pltpu.PrefetchScalarGridSpec(num_scalar_...  35.6 us
    pallas_call x4, Pallas kernels, attend_group(): pl.pallas_call(kernel, out_shape=[jax.ShapeDtypeStruct((tokens, GROUPS *...  28.3 us
    pallas_call x4, Pallas kernels, attend_group_back(): pl.pallas_call(kernel, out_shape=[jax.ShapeDtypeStruct((tokens, width), B...  25.6 us
    pallas_call x1, Pallas kernels, feed_forward_back(): pl.pallas_call(kernel, grid=(n // 2,), in_specs=[pl.BlockSpec((2 * rows,...  23.2 us
  transfers between devices with their start and end apart: 79, of which 30 were waited for; matrix products, arithmetic and copies ran while one was open for 2% of the time, Pallas kernels for 40%

profile of v3, /device:TPU:0, one launch (start us, length us, event | category | flops | bytes accessed | tf_op | source)
XLA Modules:
  0.0 809.5 jit_solution(2131369175577231364)
XLA Ops:
  33.2 7.5 collective-permute-done.3.refs_4_
  59.2 5.6 pick_columns.9
  75.7 15.3 %collective-permute-done.12.refs_1_ = bf16[128,2048]{1,0:T(8,128)(2,1)S(1)} collective-permute-done((bf16[128,2048]{1,0:T(8,128)(2,1)S(1)}, bf16[128,2048]{1,0:T(8,128)(2,1)S(1)}, u32[]{:S(2)}, u32[]{:S(2)}) %collective-permute-start.12) | collective-permute-done | bytes 524320 | tf_op jit(solution)/shard_map/ppermute | solution.py:87
  105.9 32.2 %collective-permute-done.17.refs_2_ = bf16[256,1536]{1,0:T(8,128)(2,1)} collective-permute-done((bf16[256,1536]{1,0:T(8,128)(2,1)}, bf16[256,1536]{1,0:T(8,128)(2,1)}, u32[]{:S(2)}, u32[]{:S(2)}) %collective-permute-start.17) | collective-permute-done | bytes 786464 | tf_op jit(solution)/shard_map/ppermute | solution.py:87
  147.8 6.7 attend_group.4
  154.6 6.8 attend_group.5
  161.3 15.8 %collective-permute-done.18.refs_2_ = bf16[128,2048]{1,0:T(8,128)(2,1)S(1)} collective-permute-done((bf16[128,2048]{1,0:T(8,128)(2,1)}, bf16[128,2048]{1,0:T(8,128)(2,1)S(1)}, u32[]{:S(2)}, u32[]{:S(2)}) %collective-permute-start.18) | collective-permute-done | bytes 524320 | tf_op jit(solution)/shard_map/ppermute | solution.py:87
  183.4 6.5 attend_group.6
  189.8 8.3 %attend_group.7 = (bf16[512,256]{1,0:T(8,128)(2,1)}, f32[512,512]{1,0:T(8,128)}) custom-call(bf16[512,2048]{1,0:T(8,128)(2,1)} %get-tuple-element.673.refs_0_, bf16[1024,768]{1,0:T(8,128)(2,1)} %get-tuple-element.462.refs_1_.refs_3_, bf16[1024,768]{1,0:T(8,128)(2,1)} %copy-done.4, bf16[512,2048]{1,0:T(8,128)(2,1)} %get-tuple-element.637.refs_0_.refs_3_, ...), custom_call_target="tpu_custom_call" | custom-call | flops 1 | bytes 1 | tf_op jit(solution)/shard_map/attend_group/pallas_call | solution.py:297
  198.2 9.1 %collective-permute-done.22.refs_4_ = bf16[256,1024]{1,0:T(8,128)(2,1)} collective-permute-done((bf16[256,1024]{1,0:T(8,128)(2,1)}, bf16[256,1024]{1,0:T(8,128)(2,1)}, u32[]{:S(2)}, u32[]{:S(2)}) %collective-permute-start.22) | collective-permute-done | bytes 524320 | tf_op jit(solution)/shard_map/ppermute | solution.py:87
  221.1 23.9 %collective-permute-done.29.refs_2_ = bf16[384,1024]{1,0:T(8,128)(2,1)} collective-permute-done((bf16[384,1024]{1,0:T(8,128)(2,1)}, bf16[384,1024]{1,0:T(8,128)(2,1)}, u32[]{:S(2)}, u32[]{:S(2)}) %collective-permute-start.29) | collective-permute-done | bytes 786464 | tf_op jit(solution)/shard_map/ppermute | solution.py:87
  247.2 7.1 light.59
  267.8 17.4 %collective-permute-done.32.refs_8_ = bf16[256,1536]{1,0:T(8,128)(2,1)S(1)} collective-permute-done((bf16[256,1536]{1,0:T(8,128)(2,1)}, bf16[256,1536]{1,0:T(8,128)(2,1)S(1)}, u32[]{:S(2)}, u32[]{:S(2)}) %collective-permute-start.32) | collective-permute-done | bytes 786464 | tf_op jit(solution)/shard_map/ppermute | solution.py:87
  285.2 16.0 %collective-permute-done.31.refs_6_ = bf16[256,1536]{1,0:T(8,128)(2,1)S(1)} collective-permute-done((bf16[256,1536]{1,0:T(8,128)(2,1)}, bf16[256,1536]{1,0:T(8,128)(2,1)S(1)}, u32[]{:S(2)}, u32[]{:S(2)}) %collective-permute-start.31) | collective-permute-done | bytes 786464 | tf_op jit(solution)/shard_map/ppermute | solution.py:87
  305.4 16.7 %collective-permute-done.36.refs_4_ = bf16[384,1024]{1,0:T(8,128)(2,1)} collective-permute-done((bf16[384,1024]{1,0:T(8,128)(2,1)}, bf16[384,1024]{1,0:T(8,128)(2,1)}, u32[]{:S(2)}, u32[]{:S(2)}) %collective-permute-start.36) | collective-permute-done | bytes 786464 | tf_op jit(solution)/shard_map/ppermute | solution.py:87
  326.5 7.2 light.61.refs_12_.own_ref
  333.8 4.8 light.62.refs_14_.own_ref
  339.1 9.6 %collective-permute-done.38.refs_15_.other_ref = bf16[1536,1024]{1,0:T(8,128)(2,1)S(1)} collective-permute-done((bf16[1536,1024]{1,0:T(8,128)(2,1)}, bf16[1536,1024]{1,0:T(8,128)(2,1)S(1)}, u32[]{:S(2)}, u32[]{:S(2)}) %collective-permute-start.38) | collective-permute-done | bytes 3145760 | tf_op jit(solution)/shard_map/ppermute | solution.py:87
  350.3 35.6 %feed_forward.1 = (bf16[1024,1536]{1,0:T(8,128)(2,1)}, bf16[1024,1536]{1,0:T(8,128)(2,1)}, bf16[1024,1536]{1,0:T(8,128)(2,1)}) custom-call(s32[1]{0:T(128)} %bitcast.58.places_ref.core_ref.column_ref, bf16[256,2048]{1,0:T(8,128)(2,1)} %get-tuple-element.560.refs_0_, bf16[256,2048]{1,0:T(8,128)(2,1)} %copy-done.6, bf16[256,2048]{1,0:T(8,128)(2,1)} %copy-done.7, ...), custom_call_target="tpu_custom_call" | custom-call | flops 1 | bytes 1 | tf_op jit(solution)/shard_map/feed_forward/pallas_call | solution.py:443
  385.9 11.1 %weight_grad.8 = bf16[2048,1536]{1,0:T(8,128)(2,1)} custom-call(s32[1]{0:T(128)} %constant.85.clone.1.column_ref, bf16[256,2048]{1,0:T(8,128)(2,1)} %get-tuple-element.560.refs_0_, bf16[256,2048]{1,0:T(8,128)(2,1)} %copy-done.6, bf16[256,2048]{1,0:T(8,128)(2,1)} %copy-done.7, bf16[256,2048]{1,0:T(8,128)(2,1)} %copy-done.8, ...), custom_call_target="tpu_custom_call" | custom-call | flops 1 | bytes 1 | tf_op jit(solution)/shard_map/weight_grad/pallas_call | solution.py:542
  397.1 7.2 weight_grad.9
  404.7 23.2 %feed_forward_back.1 = (bf16[256,2048]{1,0:T(8,128)(2,1)}, bf16[256,2048]{1,0:T(8,128)(2,1)}, bf16[256,2048]{1,0:T(8,128)(2,1)}, bf16[256,2048]{1,0:T(8,128)(2,1)}) custom-call(bf16[1024,1536]{1,0:T(8,128)(2,1)} %get-tuple-element.581.go_ref.refs_4_, bf16[1024,1536]{1,0:T(8,128)(2,1)} %get-tuple-element.574.refs_4_.gx_ref, ...), custom_call_target="tpu_custom_call" | custom-call | flops 1 | bytes 1 | tf_op jit(solution)/shard_map/feed_forward_back/pallas_call | solution.py:484
  429.7 13.1 %weight_grad.10.refs_1_ = bf16[2048,1536]{1,0:T(8,128)(2,1)} custom-call(s32[1]{0:T(128)} %constant.85.clone.1.column_ref, bf16[256,2048]{1,0:T(8,128)(2,1)} %get-tuple-element.560.refs_0_, bf16[256,2048]{1,0:T(8,128)(2,1)} %copy-done.6, bf16[256,2048]{1,0:T(8,128)(2,1)} %copy-done.7, bf16[256,2048]{1,0:T(8,128)(2,1)} %copy-done.8, ...), custom_call_target="tpu_custom_call" | custom-call | flops 1 | bytes 1 | tf_op jit(solution)/shard_map/weight_grad/pallas_call | solution.py:542
  442.8 6.7 light.63
  460.2 7.9 weight_grad.11.refs_1_
  472.7 12.6 %down_project.1 = (bf16[256,2048]{1,0:T(8,128)(2,1)}, bf16[256,2048]{1,0:T(8,128)(2,1)}, bf16[256,2048]{1,0:T(8,128)(2,1)}, bf16[256,2048]{1,0:T(8,128)(2,1)}) custom-call(bf16[1024,1536]{1,0:T(8,128)(2,1)} %get-tuple-element.593.refs_0_.hidden_ref, bf16[1536,1024]{1,0:T(8,128)(2,1)} %light.62.refs_14_.own_ref, bf16[1536,1024]{1,0:T(8,128)(2,1)} %copy-done.5), custom_call_target="tpu_custom_call" | custom-call | flops 1 | bytes 1 | tf_op jit(solution)/shard_map/down_project/pallas_call | solution.py:578
  485.3 6.3 light.66
  498.3 7.5 spread_back.2
  509.0 6.4 attend_group_back.4
  517.3 6.4 attend_group_back.5
  530.6 6.0 weight_grad.12
  536.5 6.4 attend_group_back.6
  542.9 5.1 weight_grad.13
  552.3 6.9 weight_grad.14
  561.6 6.4 attend_group_back.7
  579.2 6.4 light.73
  587.7 5.9 weight_grad.15
  602.0 12.5 %spread_back.3 = (bf16[256,2048]{1,0:T(8,128)(2,1)}, bf16[256,2048]{1,0:T(8,128)(2,1)}) custom-call(s32[48]{0:T(128)} %stack.262.places_ref, bf16[512,768]{1,0:T(8,128)(2,1)} %light.74.refs_1_.refs_0_, bf16[512,768]{1,0:T(8,128)(2,1)} %light.70.refs_1_, bf16[512,512]{1,0:T(8,128)(2,1)} %get-tuple-element.684.refs_1_.refs_2_, ...), custom_call_target="tpu_custom_call" | custom-call | flops 1 | bytes 1 | tf_op jit(solution)/shard_map/spread_back/pallas_call | solution.py:395
  614.5 16.7 %collective-permute-done.57.refs_2_ = bf16[1024,768]{1,0:T(8,128)(2,1)S(1)} collective-permute-done((bf16[1024,768]{1,0:T(8,128)(2,1)}, bf16[1024,768]{1,0:T(8,128)(2,1)S(1)}, u32[]{:S(2)}, u32[]{:S(2)}) %collective-permute-start.57) | collective-permute-done | bytes 1572896 | tf_op jit(solution)/shard_map/ppermute | solution.py:87
  648.9 20.2 %collective-permute-done.53.refs_2_ = bf16[512,1536]{1,0:T(8,128)(2,1)S(1)} collective-permute-done((bf16[512,1536]{1,0:T(8,128)(2,1)}, bf16[512,1536]{1,0:T(8,128)(2,1)S(1)}, u32[]{:S(2)}, u32[]{:S(2)}) %collective-permute-start.53) | collective-permute-done | bytes 1572896 | tf_op jit(solution)/shard_map/ppermute | solution.py:87
  678.4 5.4 light.82
  702.0 5.3 collective-permute-done.63.refs_9_
  711.0 6.3 collective-permute-done.61.refs_7_
  738.2 6.6 collective-permute-done.67.refs_2_.refs_1_
  744.8 7.7 collective-permute-done.68.refs_3_.refs_2_
  752.4 16.9 %collective-permute-done.69.refs_4_.refs_3_ = bf16[128,1536]{1,0:T(8,128)(2,1)S(1)} collective-permute-done((bf16[128,1536]{1,0:T(8,128)(2,1)}, bf16[128,1536]{1,0:T(8,128)(2,1)S(1)}, u32[]{:S(2)}, u32[]{:S(2)}) %collective-permute-start.69) | collective-permute-done | bytes 393248 | tf_op jit(solution)/shard_map/ppermute | solution.py:87
  791.4 5.1 put_columns.3
  796.5 5.6 put_columns.4
  (338 shorter events, 296.4 us)
Async XLA Ops:
  7.1 26.0 %collective-permute-start.1 = (bf16[128,1536]{1,0:T(8,128)(2,1)}, bf16[128,1536]{1,0:T(8,128)(2,1)S(1)}, u32[]{:S(2)}, u32[]{:S(2)}) collective-permute-start(bf16[128,1536]{1,0:T(8,128)(2,1)} %get-tuple-element.403), channel_id=1, source_target_pairs={{0,2},{1,3},{2,0},{3,1},{4,6},{5,7},{6,4},{7,5},{8,10},{9,11},{10,... | collective-permute-start | bytes 1179656 | tf_op jit(solution)/shard_map/ppermute | solution.py:87
  11.2 29.5 %collective-permute-start.3 = (bf16[128,1536]{1,0:T(8,128)(2,1)}, bf16[128,1536]{1,0:T(8,128)(2,1)}, u32[]{:S(2)}, u32[]{:S(2)}) collective-permute-start(bf16[128,1536]{1,0:T(8,128)(2,1)} %get-tuple-element.405), channel_id=1, source_target_pairs={{0,10},{1,11},{2,8},{3,9},{4,14},{5,15},{6,12},{7,13},{8,2},{9,3},... | collective-permute-start | bytes 1179656 | tf_op jit(solution)/shard_map/ppermute | solution.py:87
  14.6 26.0 %collective-permute-start.4 = (bf16[128,2048]{1,0:T(8,128)(2,1)}, bf16[128,2048]{1,0:T(8,128)(2,1)S(1)}, u32[]{:S(2)}, u32[]{:S(2)}) collective-permute-start(bf16[128,2048]{1,0:T(8,128)(2,1)} %pick_columns.7.refs_1_), channel_id=1, source_target_pairs={{0,16},{1,17},{2,18},{3,19},{4,20},{5,21},{6,22},{7,23},{8,24},{9,... | collective-permute-start | bytes 1572872 | tf_op jit(solution)/shard_map/ppermute | solution.py:87
  52.3 38.7 %collective-permute-start.13 = (bf16[384,1024]{1,0:T(8,128)(2,1)S(1)}, bf16[384,1024]{1,0:T(8,128)(2,1)}, u32[]{:S(2)}, u32[]{:S(2)}) collective-permute-start(bf16[384,1024]{1,0:T(8,128)(2,1)S(1)} %copy-done.9), channel_id=1, source_target_pairs={{0,4},{1,5},{2,6},{3,7},{4,0},{5,1},{6,2},{7,3},{8,12},{9,13},{10,... | collective-permute-start | bytes 2359304 | tf_op jit(solution)/shard_map/ppermute | solution.py:87
  97.6 44.9 %collective-permute-start.14 = (bf16[1024,768]{1,0:T(8,128)(2,1)}, bf16[1024,768]{1,0:T(8,128)(2,1)S(1)}, u32[]{:S(2)}, u32[]{:S(2)}) collective-permute-start(bf16[1024,768]{1,0:T(8,128)(2,1)} %get-tuple-element.462.refs_1_.refs_3_), channel_id=1, source_target_pairs={{0,4},{1,5},{2,6},{3,7},{4,0},{5,1},{6,2},{7,3},{8,12},{9,13},{10,... | collective-permute-start | bytes 4718600 | tf_op jit(solution)/shard_map/ppermute | solution.py:87
  99.1 44.5 %collective-permute-start.15 = (bf16[1024,768]{1,0:T(8,128)(2,1)}, bf16[1024,768]{1,0:T(8,128)(2,1)}, u32[]{:S(2)}, u32[]{:S(2)}) collective-permute-start(bf16[1024,768]{1,0:T(8,128)(2,1)} %get-tuple-element.463.refs_1_.refs_4_.refs_5_), channel_id=1, source_target_pairs={{0,2},{1,3},{2,0},{3,1},{4,6},{5,7},{6,4},{7,5},{8,10},{9,11},{10,... | collective-permute-start | bytes 4718600 | tf_op jit(solution)/shard_map/ppermute | solution.py:87
  99.6 42.9 %collective-permute-start.16 = (bf16[1024,512]{1,0:T(8,128)(2,1)}, bf16[1024,512]{1,0:T(8,128)(2,1)}, u32[]{:S(2)}, u32[]{:S(2)}) collective-permute-start(bf16[1024,512]{1,0:T(8,128)(2,1)} %get-tuple-element.464.refs_1_.refs_7_), channel_id=1, source_target_pairs={{0,8},{1,9},{2,10},{3,11},{4,12},{5,13},{6,14},{7,15},{8,0},{9,1},... | collective-permute-start | bytes 3145736 | tf_op jit(solution)/shard_map/ppermute | solution.py:87
  99.6 38.5 %collective-permute-start.17 = (bf16[256,1536]{1,0:T(8,128)(2,1)}, bf16[256,1536]{1,0:T(8,128)(2,1)}, u32[]{:S(2)}, u32[]{:S(2)}) collective-permute-start(bf16[256,1536]{1,0:T(8,128)(2,1)} %get-tuple-element.546.refs_1_), channel_id=1, source_target_pairs={{0,16},{1,17},{2,18},{3,19},{4,20},{5,21},{6,22},{7,23},{8,24},{9,... | collective-permute-start | bytes 2359304 | tf_op jit(solution)/shard_map/ppermute | solution.py:87
  143.6 33.6 %collective-permute-start.19 = (bf16[256,2048]{1,0:T(8,128)(2,1)S(1)}, bf16[256,2048]{1,0:T(8,128)(2,1)S(1)}, u32[]{:S(2)}, u32[]{:S(2)}) collective-permute-start(bf16[256,2048]{1,0:T(8,128)(2,1)S(1)} %copy-done), channel_id=1, source_target_pairs={{0,2},{1,3},{2,0},{3,1},{4,6},{5,7},{6,4},{7,5},{8,10},{9,11},{10,... | collective-permute-start | bytes 3145736 | tf_op jit(solution)/shard_map/ppermute | solution.py:87
  144.7 32.5 %collective-permute-start.20 = (bf16[256,1536]{1,0:T(8,128)(2,1)}, bf16[256,1536]{1,0:T(8,128)(2,1)}, u32[]{:S(2)}, u32[]{:S(2)}) collective-permute-start(bf16[256,1536]{1,0:T(8,128)(2,1)} %get-tuple-element.546.refs_1_), channel_id=1, source_target_pairs={{0,4},{1,5},{2,6},{3,7},{4,0},{5,1},{6,2},{7,3},{8,12},{9,13},{10,... | collective-permute-start | bytes 2359304 | tf_op jit(solution)/shard_map/ppermute | solution.py:87
  145.3 31.9 %collective-permute-start.18 = (bf16[128,2048]{1,0:T(8,128)(2,1)}, bf16[128,2048]{1,0:T(8,128)(2,1)S(1)}, u32[]{:S(2)}, u32[]{:S(2)}) collective-permute-start(bf16[128,2048]{1,0:T(8,128)(2,1)} %light.55.refs_1_), channel_id=1, source_target_pairs={{0,8},{1,9},{2,10},{3,11},{4,12},{5,13},{6,14},{7,15},{8,0},{9,1},... | collective-permute-start | bytes 1572872 | tf_op jit(solution)/shard_map/ppermute | solution.py:87
  145.3 52.8 %collective-permute-start.23 = (bf16[256,2048]{1,0:T(8,128)(2,1)S(1)}, bf16[256,2048]{1,0:T(8,128)(2,1)S(1)}, u32[]{:S(2)}, u32[]{:S(2)}) collective-permute-start(bf16[256,2048]{1,0:T(8,128)(2,1)S(1)} %copy-done), channel_id=1, source_target_pairs={{0,8},{1,9},{2,10},{3,11},{4,12},{5,13},{6,14},{7,15},{8,0},{9,1},... | collective-permute-start | bytes 3145736 | tf_op jit(solution)/shard_map/ppermute | solution.py:87
  147.3 50.8 %collective-permute-start.25 = (bf16[256,1536]{1,0:T(8,128)(2,1)}, bf16[256,1536]{1,0:T(8,128)(2,1)}, u32[]{:S(2)}, u32[]{:S(2)}) collective-permute-start(bf16[256,1536]{1,0:T(8,128)(2,1)} %get-tuple-element.548.refs_3_), channel_id=1, source_target_pairs={{0,16},{1,17},{2,18},{3,19},{4,20},{5,21},{6,22},{7,23},{8,24},{9,... | collective-permute-start | bytes 2359304 | tf_op jit(solution)/shard_map/ppermute | solution.py:87
  180.2 27.0 %collective-permute-start.24 = (bf16[256,1536]{1,0:T(8,128)(2,1)}, bf16[256,1536]{1,0:T(8,128)(2,1)}, u32[]{:S(2)}, u32[]{:S(2)}) collective-permute-start(bf16[256,1536]{1,0:T(8,128)(2,1)} %get-tuple-element.548.refs_3_), channel_id=1, source_target_pairs={{0,4},{1,5},{2,6},{3,7},{4,0},{5,1},{6,2},{7,3},{8,12},{9,13},{10,... | collective-permute-start | bytes 2359304 | tf_op jit(solution)/shard_map/ppermute | solution.py:87
  182.6 24.6 %collective-permute-start.22 = (bf16[256,1024]{1,0:T(8,128)(2,1)}, bf16[256,1024]{1,0:T(8,128)(2,1)}, u32[]{:S(2)}, u32[]{:S(2)}) collective-permute-start(bf16[256,1024]{1,0:T(8,128)(2,1)} %get-tuple-element.503.refs_2_), channel_id=1, source_target_pairs={{0,4},{1,5},{2,6},{3,7},{4,0},{5,1},{6,2},{7,3},{8,12},{9,13},{10,... | collective-permute-start | bytes 1572872 | tf_op jit(solution)/shard_map/ppermute | solution.py:87
  210.1 37.0 %collective-permute-start.28 = (bf16[256,2048]{1,0:T(8,128)(2,1)S(1)}, bf16[256,2048]{1,0:T(8,128)(2,1)S(1)}, u32[]{:S(2)}, u32[]{:S(2)}) collective-permute-start(bf16[256,2048]{1,0:T(8,128)(2,1)S(1)} %collective-permute-done.19.refs_6_.refs_10_.refs_3_), channel_id=1, source_target_pairs={{0,8},{1,9},{2,10},{3,11},{4,12},{5,13},{6,14},{7,15},{8,0},{9,1},... | collective-permute-start | bytes 3145736 | tf_op jit(solution)/shard_map/ppermute | solution.py:87
  210.1 37.0 %collective-permute-start.26 = (bf16[512,1024]{1,0:T(8,128)(2,1)}, bf16[512,1024]{1,0:T(8,128)(2,1)}, u32[]{:S(2)}, u32[]{:S(2)}) collective-permute-start(bf16[512,1024]{1,0:T(8,128)(2,1)} %get-tuple-element.524.refs_3_.refs_2_), channel_id=1, source_target_pairs={{0,4},{1,5},{2,6},{3,7},{4,0},{5,1},{6,2},{7,3},{8,12},{9,13},{10,... | collective-permute-start | bytes 3145736 | tf_op jit(solution)/shard_map/ppermute | solution.py:87
  211.4 35.7 %collective-permute-start.27 = (bf16[512,1024]{1,0:T(8,128)(2,1)}, bf16[512,1024]{1,0:T(8,128)(2,1)}, u32[]{:S(2)}, u32[]{:S(2)}) collective-permute-start(bf16[512,1024]{1,0:T(8,128)(2,1)} %get-tuple-element.526.refs_5_.refs_4_), channel_id=1, source_target_pairs={{0,2},{1,3},{2,0},{3,1},{4,6},{5,7},{6,4},{7,5},{8,10},{9,11},{10,... | collective-permute-start | bytes 3145736 | tf_op jit(solution)/shard_map/ppermute | solution.py:87
  213.8 31.2 %collective-permute-start.29 = (bf16[384,1024]{1,0:T(8,128)(2,1)}, bf16[384,1024]{1,0:T(8,128)(2,1)}, u32[]{:S(2)}, u32[]{:S(2)}) collective-permute-start(bf16[384,1024]{1,0:T(8,128)(2,1)} %pick_columns.8.refs_1_), channel_id=1, source_target_pairs={{0,16},{1,17},{2,18},{3,19},{4,20},{5,21},{6,22},{7,23},{8,24},{9,... | collective-permute-start | bytes 2359304 | tf_op jit(solution)/shard_map/ppermute | solution.py:87
  262.4 38.9 %collective-permute-start.33 = (bf16[256,2048]{1,0:T(8,128)(2,1)}, bf16[256,2048]{1,0:T(8,128)(2,1)S(1)}, u32[]{:S(2)}, u32[]{:S(2)}) collective-permute-start(bf16[256,2048]{1,0:T(8,128)(2,1)} %get-tuple-element.560.refs_0_), channel_id=1, source_target_pairs={{0,8},{1,9},{2,10},{3,11},{4,12},{5,13},{6,14},{7,15},{8,0},{9,1},... | collective-permute-start | bytes 3145736 | tf_op jit(solution)/shard_map/ppermute | solution.py:87
  266.6 34.6 %collective-permute-start.31 = (bf16[256,1536]{1,0:T(8,128)(2,1)}, bf16[256,1536]{1,0:T(8,128)(2,1)S(1)}, u32[]{:S(2)}, u32[]{:S(2)}) collective-permute-start(bf16[256,1536]{1,0:T(8,128)(2,1)} %collective-permute-done.17.refs_2_), channel_id=1, source_target_pairs={{0,4},{1,5},{2,6},{3,7},{4,0},{5,1},{6,2},{7,3},{8,12},{9,13},{10,... | collective-permute-start | bytes 2359304 | tf_op jit(solution)/shard_map/ppermute | solution.py:87
  266.7 55.4 %collective-permute-start.34 = (bf16[256,2048]{1,0:T(8,128)(2,1)}, bf16[256,2048]{1,0:T(8,128)(2,1)S(1)}, u32[]{:S(2)}, u32[]{:S(2)}) collective-permute-start(bf16[256,2048]{1,0:T(8,128)(2,1)} %get-tuple-element.560.refs_0_), channel_id=1, source_target_pairs={{0,2},{1,3},{2,0},{3,1},{4,6},{5,7},{6,4},{7,5},{8,10},{9,11},{10,... | collective-permute-start | bytes 3145736 | tf_op jit(solution)/shard_map/ppermute | solution.py:87
  302.1 24.4 %collective-permute-start.35 = (bf16[256,2048]{1,0:T(8,128)(2,1)S(1)}, bf16[256,2048]{1,0:T(8,128)(2,1)S(1)}, u32[]{:S(2)}, u32[]{:S(2)}) collective-permute-start(bf16[256,2048]{1,0:T(8,128)(2,1)S(1)} %collective-permute-done.33.refs_1_), channel_id=1, source_target_pairs={{0,2},{1,3},{2,0},{3,1},{4,6},{5,7},{6,4},{7,5},{8,10},{9,11},{10,... | collective-permute-start | bytes 3145736 | tf_op jit(solution)/shard_map/ppermute | solution.py:87
  397.0 32.7 %collective-permute-start.39 = (bf16[2048,1536]{1,0:T(8,128)(2,1)}, bf16[2048,1536]{1,0:T(8,128)(2,1)}, u32[]{:S(2)}, u32[]{:S(2)}) collective-permute-start(bf16[2048,1536]{1,0:T(8,128)(2,1)} %weight_grad.8), channel_id=1, source_target_pairs={{0,1},{1,0},{2,3},{3,2},{4,5},{5,4},{6,7},{7,6},{8,9},{9,8},{10,11... | collective-permute-start | bytes 18874376 | tf_op jit(solution)/shard_map/ppermute | solution.py:87
  404.3 25.4 %collective-permute-start.40 = (bf16[1536,1024]{1,0:T(8,128)(2,1)}, bf16[1536,1024]{1,0:T(8,128)(2,1)S(1)}, u32[]{:S(2)}, u32[]{:S(2)}) collective-permute-start(bf16[1536,1024]{1,0:T(8,128)(2,1)} %weight_grad.9), channel_id=1, source_target_pairs={{0,1},{1,0},{2,3},{3,2},{4,5},{5,4},{6,7},{7,6},{8,9},{9,8},{10,11... | collective-permute-start | bytes 9437192 | tf_op jit(solution)/shard_map/ppermute | solution.py:87
  427.9 25.5 %collective-permute-start.41 = (bf16[256,2048]{1,0:T(8,128)(2,1)}, bf16[256,2048]{1,0:T(8,128)(2,1)}, u32[]{:S(2)}, u32[]{:S(2)}) collective-permute-start(bf16[256,2048]{1,0:T(8,128)(2,1)} %get-tuple-element.578), channel_id=1, source_target_pairs={{0,2},{1,3},{2,0},{3,1},{4,6},{5,7},{6,4},{7,5},{8,10},{9,11},{10,... | collective-permute-start | bytes 3145736 | tf_op jit(solution)/shard_map/ppermute | solution.py:87
  456.1 29.2 %collective-permute-start.42 = (bf16[256,2048]{1,0:T(8,128)(2,1)}, bf16[256,2048]{1,0:T(8,128)(2,1)}, u32[]{:S(2)}, u32[]{:S(2)}) collective-permute-start(bf16[256,2048]{1,0:T(8,128)(2,1)} %get-tuple-element.588), channel_id=1, source_target_pairs={{0,2},{1,3},{2,0},{3,1},{4,6},{5,7},{6,4},{7,5},{8,10},{9,11},{10,... | collective-permute-start | bytes 3145736 | tf_op jit(solution)/shard_map/ppermute | solution.py:87
  457.3 28.0 %collective-permute-start.43 = (bf16[256,2048]{1,0:T(8,128)(2,1)}, bf16[256,2048]{1,0:T(8,128)(2,1)}, u32[]{:S(2)}, u32[]{:S(2)}) collective-permute-start(bf16[256,2048]{1,0:T(8,128)(2,1)} %light.64), channel_id=1, source_target_pairs={{0,8},{1,9},{2,10},{3,11},{4,12},{5,13},{6,14},{7,15},{8,0},{9,1},... | collective-permute-start | bytes 3145736 | tf_op jit(solution)/shard_map/ppermute | solution.py:87
  458.7 118.8 %collective-permute-start.48 = (bf16[1024,1536]{1,0:T(8,128)(2,1)}, bf16[1024,1536]{1,0:T(8,128)(2,1)S(1)}, u32[]{:S(2)}, u32[]{:S(2)}) collective-permute-start(bf16[1024,1536]{1,0:T(8,128)(2,1)} %get-tuple-element.584), channel_id=1, source_target_pairs={{0,4},{1,5},{2,6},{3,7},{4,0},{5,1},{6,2},{7,3},{8,12},{9,13},{10,... | collective-permute-start | bytes 9437192 | tf_op jit(solution)/shard_map/ppermute | solution.py:87
  491.6 32.1 %collective-permute-start.44 = (bf16[256,2048]{1,0:T(8,128)(2,1)}, bf16[256,2048]{1,0:T(8,128)(2,1)}, u32[]{:S(2)}, u32[]{:S(2)}) collective-permute-start(bf16[256,2048]{1,0:T(8,128)(2,1)} %get-tuple-element.610), channel_id=1, source_target_pairs={{0,2},{1,3},{2,0},{3,1},{4,6},{5,7},{6,4},{7,5},{8,10},{9,11},{10,... | collective-permute-start | bytes 3145736 | tf_op jit(solution)/shard_map/ppermute | solution.py:87
  526.5 25.5 %collective-permute-start.46 = (bf16[256,2048]{1,0:T(8,128)(2,1)}, bf16[256,2048]{1,0:T(8,128)(2,1)}, u32[]{:S(2)}, u32[]{:S(2)}) collective-permute-start(bf16[256,2048]{1,0:T(8,128)(2,1)} %get-tuple-element.634), channel_id=1, source_target_pairs={{0,2},{1,3},{2,0},{3,1},{4,6},{5,7},{6,4},{7,5},{8,10},{9,11},{10,... | collective-permute-start | bytes 3145736 | tf_op jit(solution)/shard_map/ppermute | solution.py:87
  526.8 50.8 %collective-permute-start.49 = (bf16[768,1024]{1,0:T(8,128)(2,1)}, bf16[768,1024]{1,0:T(8,128)(2,1)}, u32[]{:S(2)}, u32[]{:S(2)}) collective-permute-start(bf16[768,1024]{1,0:T(8,128)(2,1)} %get-tuple-element.592), channel_id=1, source_target_pairs={{0,4},{1,5},{2,6},{3,7},{4,0},{5,1},{6,2},{7,3},{8,12},{9,13},{10,... | collective-permute-start | bytes 4718600 | tf_op jit(solution)/shard_map/ppermute | solution.py:87
  527.3 31.9 %collective-permute-start.47 = (bf16[256,2048]{1,0:T(8,128)(2,1)}, bf16[256,2048]{1,0:T(8,128)(2,1)}, u32[]{:S(2)}, u32[]{:S(2)}) collective-permute-start(bf16[256,2048]{1,0:T(8,128)(2,1)} %light.69), channel_id=1, source_target_pairs={{0,8},{1,9},{2,10},{3,11},{4,12},{5,13},{6,14},{7,15},{8,0},{9,1},... | collective-permute-start | bytes 3145736 | tf_op jit(solution)/shard_map/ppermute | solution.py:87
  548.0 26.8 %collective-permute-start.50 = (bf16[1024,512]{1,0:T(8,128)(2,1)}, bf16[1024,512]{1,0:T(8,128)(2,1)}, u32[]{:S(2)}, u32[]{:S(2)}) collective-permute-start(bf16[1024,512]{1,0:T(8,128)(2,1)} %get-tuple-element.647), channel_id=1, source_target_pairs={{0,8},{1,9},{2,10},{3,11},{4,12},{5,13},{6,14},{7,15},{8,0},{9,1},... | collective-permute-start | bytes 3145736 | tf_op jit(solution)/shard_map/ppermute | solution.py:87
  552.0 43.1 %collective-permute-start.51 = (bf16[1024,768]{1,0:T(8,128)(2,1)}, bf16[1024,768]{1,0:T(8,128)(2,1)}, u32[]{:S(2)}, u32[]{:S(2)}) collective-permute-start(bf16[1024,768]{1,0:T(8,128)(2,1)} %get-tuple-element.640), channel_id=1, source_target_pairs={{0,2},{1,3},{2,0},{3,1},{4,6},{5,7},{6,4},{7,5},{8,10},{9,11},{10,... | collective-permute-start | bytes 4718600 | tf_op jit(solution)/shard_map/ppermute | solution.py:87
  559.2 83.2 %collective-permute-start.54 = (bf16[512,2048]{1,0:T(8,128)(2,1)}, bf16[512,2048]{1,0:T(8,128)(2,1)}, u32[]{:S(2)}, u32[]{:S(2)}) collective-permute-start(bf16[512,2048]{1,0:T(8,128)(2,1)} %get-tuple-element.650), channel_id=1, source_target_pairs={{0,2},{1,3},{2,0},{3,1},{4,6},{5,7},{6,4},{7,5},{8,10},{9,11},{10,... | collective-permute-start | bytes 6291464 | tf_op jit(solution)/shard_map/ppermute | solution.py:87
  593.6 37.5 %collective-permute-start.57 = (bf16[1024,768]{1,0:T(8,128)(2,1)}, bf16[1024,768]{1,0:T(8,128)(2,1)S(1)}, u32[]{:S(2)}, u32[]{:S(2)}) collective-permute-start(bf16[1024,768]{1,0:T(8,128)(2,1)} %get-tuple-element.676), channel_id=1, source_target_pairs={{0,4},{1,5},{2,6},{3,7},{4,0},{5,1},{6,2},{7,3},{8,12},{9,13},{10,... | collective-permute-start | bytes 4718600 | tf_op jit(solution)/shard_map/ppermute | solution.py:87
  598.6 37.1 %collective-permute-start.56 = (bf16[512,768]{1,0:T(8,128)(2,1)}, bf16[512,768]{1,0:T(8,128)(2,1)S(1)}, u32[]{:S(2)}, u32[]{:S(2)}) collective-permute-start(bf16[512,768]{1,0:T(8,128)(2,1)} %get-tuple-element.681), channel_id=1, source_target_pairs={{0,8},{1,9},{2,10},{3,11},{4,12},{5,13},{6,14},{7,15},{8,0},{9,1},... | collective-permute-start | bytes 2359304 | tf_op jit(solution)/shard_map/ppermute | solution.py:87
  599.7 69.4 %collective-permute-start.53 = (bf16[512,1536]{1,0:T(8,128)(2,1)}, bf16[512,1536]{1,0:T(8,128)(2,1)S(1)}, u32[]{:S(2)}, u32[]{:S(2)}) collective-permute-start(bf16[512,1536]{1,0:T(8,128)(2,1)} %get-tuple-element.670), channel_id=1, source_target_pairs={{0,16},{1,17},{2,18},{3,19},{4,20},{5,21},{6,22},{7,23},{8,24},{9,... | collective-permute-start | bytes 4718600 | tf_op jit(solution)/shard_map/ppermute | solution.py:87
  601.4 38.8 %collective-permute-start.55 = (bf16[512,512]{1,0:T(8,128)(2,1)}, bf16[512,512]{1,0:T(8,128)(2,1)}, u32[]{:S(2)}, u32[]{:S(2)}) collective-permute-start(bf16[512,512]{1,0:T(8,128)(2,1)} %get-tuple-element.664), channel_id=1, source_target_pairs={{0,4},{1,5},{2,6},{3,7},{4,0},{5,1},{6,2},{7,3},{8,12},{9,13},{10,... | collective-permute-start | bytes 1572872 | tf_op jit(solution)/shard_map/ppermute | solution.py:87
  631.1 47.2 %collective-permute-start.52 = (bf16[256,2048]{1,0:T(8,128)(2,1)}, bf16[256,2048]{1,0:T(8,128)(2,1)}, u32[]{:S(2)}, u32[]{:S(2)}) collective-permute-start(bf16[256,2048]{1,0:T(8,128)(2,1)} %get-tuple-element.686), channel_id=1, source_target_pairs={{0,1},{1,0},{2,3},{3,2},{4,5},{5,4},{6,7},{7,6},{8,9},{9,8},{10,11... | collective-permute-start | bytes 3145736 | tf_op jit(solution)/shard_map/ppermute | solution.py:87
  646.6 44.3 %collective-permute-start.58 = (bf16[256,2048]{1,0:T(8,128)(2,1)}, bf16[256,2048]{1,0:T(8,128)(2,1)S(1)}, u32[]{:S(2)}, u32[]{:S(2)}) collective-permute-start(bf16[256,2048]{1,0:T(8,128)(2,1)} %get-tuple-element.706), channel_id=1, source_target_pairs={{0,8},{1,9},{2,10},{3,11},{4,12},{5,13},{6,14},{7,15},{8,0},{9,1},... | collective-permute-start | bytes 3145736 | tf_op jit(solution)/shard_map/ppermute | solution.py:87
  647.7 37.3 %collective-permute-start.60 = (bf16[512,768]{1,0:T(8,128)(2,1)}, bf16[512,768]{1,0:T(8,128)(2,1)S(1)}, u32[]{:S(2)}, u32[]{:S(2)}) collective-permute-start(bf16[512,768]{1,0:T(8,128)(2,1)} %get-tuple-element.691), channel_id=1, source_target_pairs={{0,2},{1,3},{2,0},{3,1},{4,6},{5,7},{6,4},{7,5},{8,10},{9,11},{10,... | collective-permute-start | bytes 2359304 | tf_op jit(solution)/shard_map/ppermute | solution.py:87
  678.4 58.0 %collective-permute-start.72 = (bf16[384,1024]{1,0:T(8,128)(2,1)}, bf16[384,1024]{1,0:T(8,128)(2,1)S(1)}, u32[]{:S(2)}, u32[]{:S(2)}) collective-permute-start(bf16[384,1024]{1,0:T(8,128)(2,1)} %get-tuple-element.713), channel_id=1, source_target_pairs={{0,16},{1,17},{2,18},{3,19},{4,20},{5,21},{6,22},{7,23},{8,24},{9,... | collective-permute-start | bytes 2359304 | tf_op jit(solution)/shard_map/ppermute | solution.py:87
  688.7 28.7 %collective-permute-start.61 = (bf16[256,768]{1,0:T(8,128)(2,1)}, bf16[256,768]{1,0:T(8,128)(2,1)S(1)}, u32[]{:S(2)}, u32[]{:S(2)}) collective-permute-start(bf16[256,768]{1,0:T(8,128)(2,1)} %get-tuple-element.741.refs_2_), channel_id=1, source_target_pairs={{0,8},{1,9},{2,10},{3,11},{4,12},{5,13},{6,14},{7,15},{8,0},{9,1},... | collective-permute-start | bytes 1179656 | tf_op jit(solution)/shard_map/ppermute | solution.py:87
  726.2 46.0 %collective-permute-start.71 = (bf16[128,2048]{1,0:T(8,128)(2,1)}, bf16[128,2048]{1,0:T(8,128)(2,1)S(1)}, u32[]{:S(2)}, u32[]{:S(2)}) collective-permute-start(bf16[128,2048]{1,0:T(8,128)(2,1)} %light.87), channel_id=1, source_target_pairs={{1,17},{3,19},{5,21},{7,23},{9,25},{11,27},{13,29},{15,31},{16,0},... | collective-permute-start | bytes 1572872 | tf_op jit(solution)/shard_map/ppermute | solution.py:87
  727.7 44.5 %collective-permute-start.70 = (bf16[128,2048]{1,0:T(8,128)(2,1)}, bf16[128,2048]{1,0:T(8,128)(2,1)S(1)}, u32[]{:S(2)}, u32[]{:S(2)}) collective-permute-start(bf16[128,2048]{1,0:T(8,128)(2,1)} %get-tuple-element.750), channel_id=1, source_target_pairs={{0,16},{1,17},{2,18},{3,19},{4,20},{5,21},{6,22},{7,23},{8,24},{9,... | collective-permute-start | bytes 1572872 | tf_op jit(solution)/shard_map/ppermute | solution.py:87
  736.3 33.0 %collective-permute-start.69 = (bf16[128,1536]{1,0:T(8,128)(2,1)}, bf16[128,1536]{1,0:T(8,128)(2,1)S(1)}, u32[]{:S(2)}, u32[]{:S(2)}) collective-permute-start(bf16[128,1536]{1,0:T(8,128)(2,1)} %get-tuple-element.757), channel_id=1, source_target_pairs={{0,10},{1,11},{2,8},{3,9},{4,14},{5,15},{6,12},{7,13},{8,2},{9,3},... | collective-permute-start | bytes 1179656 | tf_op jit(solution)/shard_map/ppermute | solution.py:87
  (85 other events, 942.1 us)
